TPU v7x, 512 devices: a whole 4x4x16 slice. The times are simulated.
512 devices in a mesh: tx: 8 (over x, core), rx: 16 (over z), freq: 4 (over y).
Axes of the slice: x: 4, y: 4, z: 16, core: 2. Of those that a mesh axis runs over, the one named last changes fastest.
Arguments:
- spectrum: float32 [2, 8, 2048, 2048], P(None, 'freq', 'tx', 'rx'), may hold values from -6 to 6
- measured: float32 [2, 8, 2048, 2048], P(None, 'freq', 'tx', 'rx'), may hold values from -12 to 12
- wavenumber: float32 [8], replicated, may hold values from 1.5 to 3
- send_weight: float32 [2048], P('tx'), may hold values from 0.25 to 2
- hear_weight: float32 [2048], P('rx'), may hold values from 0.25 to 2
- aperture: int32 [128, 128], P('tx', 'rx'), may hold values 0 or 1
Outputs:
- updated: float32 [2, 8, 2048, 2048], P(None, 'freq', 'tx', 'rx')
- residual: float32 [2, 8, 2048, 2048], P(None, 'freq', 'tx', 'rx')
Inputs may be any that keep to these rules, and one draw needn't show every extreme that they name: `aperture`: 1 marks a live tile of 16 x 16 antenna pairs, 0 a silent one.
All inputs are finite; a program needn't handle non-finite values. No bound on the sum of `aperture` on one device may be relied on, other than what follows from the above.
Results may differ from a plain program's by a relative error of at most 0.00016.
Values sent between devices are 32-bit elements; how exact they have to be, the bound alone decides.
No kernel may reach another device: no remote copies, remote signals or barrier semaphores. Data moves between devices by JAX's collectives and lax.ppermute only.
A program may use at most 128 MiB of HBM per device.

v0:
```python
import math

import jax
import jax.numpy as jnp
from jax import lax
from jax.sharding import PartitionSpec as P

depth_step = 2.0
step_size = 0.125
root_floor = 0.25
highest = lax.Precision.HIGHEST


def split_up(value, dim, peers):
    dims = value.shape
    pieces = value.reshape(*dims[:dim], peers, dims[dim] // peers, *dims[dim + 1 :])
    return jnp.moveaxis(pieces, dim, 0)


def sent_and_summed(value, axis, dim):
    pieces = split_up(value, dim, lax.axis_size(axis))
    arrived = lax.all_to_all(pieces, axis, split_axis=0, concat_axis=0, tiled=True)
    return arrived.sum(axis=0)


def sent_together(arrays, axis, dim, along):
    widths = [a.shape[along] for a in arrays]
    both = jnp.concatenate(arrays, axis=along)
    out = sent_and_summed(both, axis, dim)
    return tuple(jnp.split(out, [sum(widths[:k]) for k in range(1, len(widths))], axis=along))


def in_one_piece(arrays, axis, dim, along):
    ends, at = ([], 0)
    for a in arrays[:-1]:
        at += a.shape[along]
        ends.append(at)
    both = jnp.concatenate(arrays, axis=along)
    return tuple(jnp.split(lax.all_gather(both, axis, axis=dim, tiled=True), ends, axis=along))


def wave_numbers(offset, length, total):
    indices = offset + jnp.arange(length, dtype=jnp.int32)
    signed = jnp.where(indices < total // 2, indices, indices - total)
    return 2.0 * jnp.pi / total * signed.astype(jnp.float32)


def vertical(wavenumber, waves_sent, waves_heard):
    squared = (wavenumber * wavenumber)[:, None, None]
    first_root = jnp.sqrt(
        jnp.maximum(squared - (waves_sent * waves_sent)[None, :, None], 0.0) + root_floor
    )
    second_root = jnp.sqrt(
        jnp.maximum(squared - (waves_heard * waves_heard)[None, None, :], 0.0) + root_floor
    )
    return first_root + second_root


def unit_table(total, sign):
    indices = jnp.arange(total, dtype=jnp.int32)
    product = indices[:, None] * indices[None, :] % total
    phases = sign * 2.0 * math.pi / total * product.astype(jnp.float32)
    return (jnp.cos(phases), jnp.sin(phases))


def twiddle_table(outer, inner, sign):
    total = outer * inner
    product = (
        jnp.arange(outer, dtype=jnp.int32)[:, None]
        * jnp.arange(inner, dtype=jnp.int32)[None, :]
        % total
    )
    phases = sign * 2.0 * math.pi / total * product.astype(jnp.float32)
    return (jnp.cos(phases), jnp.sin(phases))


def complex_product(left_real, left_imag, table_real, table_imag, form):

    def einsum_of(operand, table):
        return jnp.einsum(form, operand, table, precision=highest)

    return (
        einsum_of(left_real, table_real) - einsum_of(left_imag, table_imag),
        einsum_of(left_real, table_imag) + einsum_of(left_imag, table_real),
    )


def split_length(total):
    inner = math.gcd(total, 128)
    return (total // inner, inner)


def transform_last(real_part, imag_part, sign):
    total = real_part.shape[-1]
    outer, inner = split_length(total)
    leading = real_part.shape[:-1]
    real_part = real_part.reshape(leading + (outer, inner))
    imag_part = imag_part.reshape(leading + (outer, inner))
    first_real, first_imag = unit_table(outer, sign)
    mixed_real, mixed_imag = complex_product(
        real_part, imag_part, first_real, first_imag, "...ab,ca->...cb"
    )
    twist_real, twist_imag = twiddle_table(outer, inner, sign)
    mixed_real, mixed_imag = (
        mixed_real * twist_real - mixed_imag * twist_imag,
        mixed_real * twist_imag + mixed_imag * twist_real,
    )
    second_real, second_imag = unit_table(inner, sign)
    final_real, final_imag = complex_product(
        mixed_real, mixed_imag, second_real, second_imag, "...cb,db->...dc"
    )
    scale = 1.0 / math.sqrt(total)
    return (
        (final_real * scale).reshape(leading + (total,)),
        (final_imag * scale).reshape(leading + (total,)),
    )


def transform_rows(real_part, imag_part, sign):
    turned_real = jnp.swapaxes(real_part, -1, -2)
    turned_imag = jnp.swapaxes(imag_part, -1, -2)
    done_real, done_imag = transform_last(turned_real, turned_imag, sign)
    return (jnp.swapaxes(done_real, -1, -2), jnp.swapaxes(done_imag, -1, -2))


def natural_columns(values, senders, hearers):
    leading = values.shape[:-1]
    width = values.shape[-1] // (senders * hearers)
    values = values.reshape(leading + (senders, hearers, width))
    values = jnp.swapaxes(values, -3, -2)
    return values.reshape(leading + (senders * hearers * width,))


def plane_transform(real_part, imag_part, sign):
    senders = lax.axis_size("tx")
    hearers = lax.axis_size("rx")
    rows_real, rows_imag = transform_rows(
        lax.all_to_all(real_part, "tx", split_axis=2, concat_axis=1, tiled=True),
        lax.all_to_all(imag_part, "tx", split_axis=2, concat_axis=1, tiled=True),
        sign,
    )
    spread_real = lax.all_to_all(rows_real, ("tx", "rx"), split_axis=1, concat_axis=2, tiled=True)
    spread_imag = lax.all_to_all(rows_imag, ("tx", "rx"), split_axis=1, concat_axis=2, tiled=True)
    spread_real = natural_columns(spread_real, senders, hearers)
    spread_imag = natural_columns(spread_imag, senders, hearers)
    done_real, done_imag = transform_last(spread_real, spread_imag, sign)
    return (
        lax.all_to_all(done_real, "rx", split_axis=2, concat_axis=1, tiled=True),
        lax.all_to_all(done_imag, "rx", split_axis=2, concat_axis=1, tiled=True),
    )


def per_device(spectrum, measured, wavenumber, send_weight, hear_weight, aperture):
    depth_local = spectrum.shape[1]
    rows_sent = spectrum.shape[2]
    rows_heard = spectrum.shape[3]
    freq_total = wavenumber.shape[0]
    senders = lax.axis_size("tx")
    hearers = lax.axis_size("rx")
    waves_sent = wave_numbers(lax.axis_index("tx") * rows_sent, rows_sent, rows_sent * senders)
    waves_heard = wave_numbers(lax.axis_index("rx") * rows_heard, rows_heard, rows_heard * hearers)
    vertical_waves = vertical(wavenumber, waves_sent, waves_heard)
    first_depth = lax.axis_index("freq") * depth_local
    cosine_layers = []
    sine_layers = []
    pair_real = jnp.zeros((freq_total, rows_sent, rows_heard), jnp.float32)
    pair_imag = jnp.zeros((freq_total, rows_sent, rows_heard), jnp.float32)
    for depth_index in range(depth_local):
        height = (first_depth + depth_index + 1).astype(jnp.float32) * depth_step
        phases = vertical_waves * height
        cosine = jnp.cos(phases)
        sine_part = jnp.sin(phases)
        cosine_layers.append(cosine)
        sine_layers.append(sine_part)
        layer_real = spectrum[0, depth_index][None]
        layer_imag = spectrum[1, depth_index][None]
        pair_real = pair_real + (cosine * layer_real + sine_part * layer_imag)
        pair_imag = pair_imag + (cosine * layer_imag - sine_part * layer_real)
    pair_real, pair_imag = sent_together((pair_real, pair_imag), "freq", 0, 1)
    field_real, field_imag = plane_transform(pair_real, pair_imag, 1.0)
    tiles_sent, tiles_heard = aperture.shape
    gate = aperture.astype(jnp.float32)
    weights = (
        send_weight.reshape(tiles_sent, -1)[:, :, None, None]
        * gate[:, None, :, None]
        * hear_weight.reshape(tiles_heard, -1)[None, None, :, :]
    ).reshape(rows_sent, rows_heard)
    resid_real = weights[None] * (measured[0] - field_real)
    resid_imag = weights[None] * (measured[1] - field_imag)
    back_real, back_imag = plane_transform(resid_real, resid_imag, -1.0)
    piece_real, piece_imag = in_one_piece((back_real, back_imag), "freq", 0, 1)
    layers_real = []
    layers_imag = []
    for depth_index in range(depth_local):
        cosine = cosine_layers[depth_index]
        sine_part = sine_layers[depth_index]
        layers_real.append(jnp.sum(cosine * piece_real - sine_part * piece_imag, axis=0))
        layers_imag.append(jnp.sum(cosine * piece_imag + sine_part * piece_real, axis=0))
    grad_real = jnp.stack(layers_real)
    grad_imag = jnp.stack(layers_imag)
    updated = spectrum + step_size * jnp.stack([grad_real, grad_imag])
    return (updated, jnp.stack([resid_real, resid_imag]))


def solution(mesh):
    placed = (
        P(None, "freq", "tx", "rx"),
        P(None, "freq", "tx", "rx"),
        P(),
        P("tx"),
        P("rx"),
        P("tx", "rx"),
    )
    return jax.shard_map(
        per_device,
        mesh=mesh,
        in_specs=placed,
        out_specs=(P(None, "freq", "tx", "rx"), P(None, "freq", "tx", "rx")),
        check_vma=False,
    )
```

profile of v0, /device:TPU:1, one launch (start us, length us, event | category | flops | bytes accessed | tf_op | source)
XLA Modules:
  0.0 437.8 jit_solution(6166563022022994847)
XLA Ops:
  10.2 7.8 %fusion.49 = (f32[4,2,256,128]{3,2,1,0:T(8,128)S(1)}, f32[4,2,256,128]{3,2,1,0:T(8,128)S(1)}) fusion(f32[256,128]{1,0:T(8,128)S(1)} %get-tuple-element.19, f32[256,128]{1,0:T(8,128)S(1)} %get-tuple-element.17, f32[]{:T(128)S(6)} %mul.978, f32[256,128]{1,0:T(8,128)S(1)} %get-tuple-element.18, f32[256,128]{1,0:T(8,128)S(1)} %get-tuple-element.16, ...), kind=kLoop, calls=%fused_computation.70 | loop fusion | flops 4456448 | bytes 2633736 | tf_op jit(solution)/shard_map/add | solution.py:177
  18.2 26.6 %all_to_all.215 = f32[4,2,512,128]{3,2,1,0:T(8,128)S(1)} all-to-all(f32[4,2,512,128]{3,2,1,0:T(8,128)S(1)} %pad_maximum_fusion), channel_id=1, replica_groups=mesh['tx'=8,'rx'=16,'freq'=4] {'freq'}, dimensions={0} | all-to-all | bytes 4194304 | tf_op jit(solution)/shard_map/all_to_all | solution.py:22
  45.9 9.7 %all-to-all-start.1 = ((f32[2,256,128]{1,0,2:T(2,128)}), f32[2,256,128]{1,0,2:T(2,128)S(1)}, u32[]{:S(2)}, u32[]{:S(2)}) async-start(f32[2,256,128]{1,0,2:T(2,128)} %copy.111), calls=%async_computation.1 | async-start | bytes 524288 | tf_op jit(solution)/shard_map/all_to_all | solution.py:138
  56.5 5.6 %all-to-all-done.1 = f32[2,256,128]{1,0,2:T(2,128)S(1)} async-done(((f32[2,256,128]{1,0,2:T(2,128)}), f32[2,256,128]{1,0,2:T(2,128)S(1)}, u32[]{:S(2)}, u32[]{:S(2)}) %all-to-all-start.1) | async-done | bytes 262176 | tf_op jit(solution)/shard_map/all_to_all | solution.py:138
  67.3 5.9 %all-to-all-done.2 = f32[2,256,128]{1,0,2:T(2,128)S(1)} async-done(((f32[2,256,128]{1,0,2:T(2,128)}), f32[2,256,128]{1,0,2:T(2,128)S(1)}, u32[]{:S(2)}, u32[]{:S(2)}) %all-to-all-start.2) | async-done | bytes 262176 | tf_op jit(solution)/shard_map/all_to_all | solution.py:139
  82.6 18.6 %all-to-all-start.3 = ((f32[128,1,512]{2,1,0:T(1,128)}), f32[128,1,512]{2,1,0:T(1,128)S(1)}, u32[]{:S(2)}, u32[]{:S(2)}) async-start(f32[128,1,512]{2,1,0:T(1,128)} %reshape.287), calls=%async_computation.3 | async-start | bytes 524288 | tf_op jit(solution)/shard_map/all_to_all | solution.py:142
  109.3 14.9 %all-to-all-done.3 = f32[128,1,512]{2,1,0:T(1,128)S(1)} async-done(((f32[128,1,512]{2,1,0:T(1,128)}), f32[128,1,512]{2,1,0:T(1,128)S(1)}, u32[]{:S(2)}, u32[]{:S(2)}) %all-to-all-start.3) | async-done | bytes 262176 | tf_op jit(solution)/shard_map/all_to_all | solution.py:142
  124.2 6.0 %all-to-all-start.4 = ((f32[128,1,512]{2,1,0:T(1,128)}), f32[128,1,512]{2,1,0:T(1,128)S(1)}, u32[]{:S(2)}, u32[]{:S(2)}) async-start(f32[128,1,512]{2,1,0:T(1,128)} %reshape.289), calls=%async_computation.4 | async-start | bytes 524288 | tf_op jit(solution)/shard_map/all_to_all | solution.py:143
  141.3 11.9 %all-to-all-done.4 = f32[128,1,512]{2,1,0:T(1,128)S(1)} async-done(((f32[128,1,512]{2,1,0:T(1,128)}), f32[128,1,512]{2,1,0:T(1,128)S(1)}, u32[]{:S(2)}, u32[]{:S(2)}) %all-to-all-start.4) | async-done | bytes 262176 | tf_op jit(solution)/shard_map/all_to_all | solution.py:143
  181.7 7.2 %all-to-all-done.5 = f32[16,1,4096]{2,1,0:T(1,128)S(1)} async-done(((f32[16,1,4096]{2,1,0:T(1,128)}), f32[16,1,4096]{2,1,0:T(1,128)S(1)}, u32[]{:S(2)}, u32[]{:S(2)}) %all-to-all-start.5) | async-done | bytes 262176 | tf_op jit(solution)/shard_map/all_to_all | solution.py:148
  188.9 10.0 %all-to-all-start.7 = ((f32[16,1,4096]{2,1,0:T(1,128)}), f32[16,1,4096]{2,1,0:T(1,128)S(1)}, u32[]{:S(2)}, u32[]{:S(2)}) async-start(f32[16,1,4096]{2,1,0:T(1,128)} %reshape.293), calls=%async_computation.7 | async-start | bytes 524288 | tf_op jit(solution)/shard_map/all_to_all | solution.py:149
  204.7 7.9 %all-to-all-done.7 = f32[16,1,4096]{2,1,0:T(1,128)S(1)} async-done(((f32[16,1,4096]{2,1,0:T(1,128)}), f32[16,1,4096]{2,1,0:T(1,128)S(1)}, u32[]{:S(2)}, u32[]{:S(2)}) %all-to-all-start.7) | async-done | bytes 262176 | tf_op jit(solution)/shard_map/all_to_all | solution.py:149
  218.4 8.8 %all-to-all-start.6 = ((f32[2,256,128]{1,0,2:T(2,128)}), f32[2,256,128]{1,0,2:T(2,128)S(1)}, u32[]{:S(2)}, u32[]{:S(2)}) async-start(f32[2,256,128]{1,0,2:T(2,128)} %copy.131), calls=%async_computation.6 | async-start | bytes 524288 | tf_op jit(solution)/shard_map/all_to_all | solution.py:138
  228.1 5.6 %all-to-all-done.6 = f32[2,256,128]{1,0,2:T(2,128)S(1)} async-done(((f32[2,256,128]{1,0,2:T(2,128)}), f32[2,256,128]{1,0,2:T(2,128)S(1)}, u32[]{:S(2)}, u32[]{:S(2)}) %all-to-all-start.6) | async-done | bytes 262176 | tf_op jit(solution)/shard_map/all_to_all | solution.py:138
  239.0 5.9 %all-to-all-done.8 = f32[2,256,128]{1,0,2:T(2,128)S(1)} async-done(((f32[2,256,128]{1,0,2:T(2,128)}), f32[2,256,128]{1,0,2:T(2,128)S(1)}, u32[]{:S(2)}, u32[]{:S(2)}) %all-to-all-start.8) | async-done | bytes 262176 | tf_op jit(solution)/shard_map/all_to_all | solution.py:139
  254.4 9.1 %all-to-all-start.9 = ((f32[128,1,512]{2,1,0:T(1,128)}), f32[128,1,512]{2,1,0:T(1,128)S(1)}, u32[]{:S(2)}, u32[]{:S(2)}) async-start(f32[128,1,512]{2,1,0:T(1,128)} %reshape.295), calls=%async_computation.9 | async-start | bytes 524288 | tf_op jit(solution)/shard_map/all_to_all | solution.py:142
  273.2 13.3 %all-to-all-done.9 = f32[128,1,512]{2,1,0:T(1,128)S(1)} async-done(((f32[128,1,512]{2,1,0:T(1,128)}), f32[128,1,512]{2,1,0:T(1,128)S(1)}, u32[]{:S(2)}, u32[]{:S(2)}) %all-to-all-start.9) | async-done | bytes 262176 | tf_op jit(solution)/shard_map/all_to_all | solution.py:142
  286.5 6.6 %all-to-all-start.10 = ((f32[128,1,512]{2,1,0:T(1,128)}), f32[128,1,512]{2,1,0:T(1,128)}, u32[]{:S(2)}, u32[]{:S(2)}) async-start(f32[128,1,512]{2,1,0:T(1,128)} %reshape.297), calls=%async_computation.10 | async-start | bytes 524288 | tf_op jit(solution)/shard_map/all_to_all | solution.py:143
  303.7 11.9 %all-to-all-done.10 = f32[128,1,512]{2,1,0:T(1,128)} async-done(((f32[128,1,512]{2,1,0:T(1,128)}), f32[128,1,512]{2,1,0:T(1,128)}, u32[]{:S(2)}, u32[]{:S(2)}) %all-to-all-start.10) | async-done | bytes 262176 | tf_op jit(solution)/shard_map/all_to_all | solution.py:143
  346.7 5.6 %all-to-all-done.11 = f32[16,1,4096]{2,1,0:T(1,128)S(1)} async-done(((f32[16,1,4096]{2,1,0:T(1,128)}), f32[16,1,4096]{2,1,0:T(1,128)S(1)}, u32[]{:S(2)}, u32[]{:S(2)}) %all-to-all-start.11) | async-done | bytes 262176 | tf_op jit(solution)/shard_map/all_to_all | solution.py:148
  352.2 10.0 %all-to-all-start.12 = ((f32[16,1,4096]{2,1,0:T(1,128)}), f32[16,1,4096]{2,1,0:T(1,128)S(1)}, u32[]{:S(2)}, u32[]{:S(2)}) async-start(f32[16,1,4096]{2,1,0:T(1,128)} %reshape.299), calls=%async_computation.12 | async-start | bytes 524288 | tf_op jit(solution)/shard_map/all_to_all | solution.py:149
  367.5 8.5 %all-to-all-done.12 = f32[16,1,4096]{2,1,0:T(1,128)S(1)} async-done(((f32[16,1,4096]{2,1,0:T(1,128)}), f32[16,1,4096]{2,1,0:T(1,128)S(1)}, u32[]{:S(2)}, u32[]{:S(2)}) %all-to-all-start.12) | async-done | bytes 262176 | tf_op jit(solution)/shard_map/all_to_all | solution.py:149
  384.8 34.7 %all-gather.2.cloned.1.call-done = f32[8,512,128]{2,1,0:T(8,128)} async-done(((f32[2,512,128]{2,1,0:T(8,128)}), f32[8,512,128]{2,1,0:T(8,128)}) %all-gather.2.cloned.1.call-update) | async-done | bytes 2097168 | tf_op jit(solution)/shard_map/all_gather | solution.py:39
  419.5 10.1 %fusion.41 = (f32[256,128]{1,0:T(8,128)S(1)}, f32[256,128]{1,0:T(8,128)S(1)}, f32[256,128]{1,0:T(8,128)S(1)}, f32[256,128]{1,0:T(8,128)S(1)}) fusion(f32[8,512,128]{2,1,0:T(8,128)} %all-gather.2.cloned.1.call-done, f32[]{:T(128)S(6)} %mul.948, f32[8,128]{1,0:T(8,128)S(1)} %add_sqrt_fusion.3, f32[8,256]{1,0:T(8,128)S(1)} %add_sqrt_fusion.1, f32[]{:T(128)S(6)} %mul.978), kind=kLoop, calls=%fused_computation.62 | loop fusion | flops 4849664 | bytes 2633736 | tf_op jit(solution)/shard_map/reduce_sum | solution.py:197
  (167 shorter events, 160.0 us)
Async XLA Ops:
  7.2 1.3 copy-start.6
  8.5 0.5 copy-start.8
  45.9 16.3 %all-to-all-start.1 = ((f32[2,256,128]{1,0,2:T(2,128)}), f32[2,256,128]{1,0,2:T(2,128)S(1)}, u32[]{:S(2)}, u32[]{:S(2)}) async-start(f32[2,256,128]{1,0,2:T(2,128)} %copy.111), calls=%async_computation.1 | async-start | bytes 524288 | tf_op jit(solution)/shard_map/all_to_all | solution.py:138
  62.1 11.1 %all-to-all-start.2 = ((f32[2,256,128]{1,0,2:T(2,128)}), f32[2,256,128]{1,0,2:T(2,128)S(1)}, u32[]{:S(2)}, u32[]{:S(2)}) async-start(f32[2,256,128]{1,0,2:T(2,128)} %copy.114), calls=%async_computation.2 | async-start | bytes 524288 | tf_op jit(solution)/shard_map/all_to_all | solution.py:139
  82.6 41.6 %all-to-all-start.3 = ((f32[128,1,512]{2,1,0:T(1,128)}), f32[128,1,512]{2,1,0:T(1,128)S(1)}, u32[]{:S(2)}, u32[]{:S(2)}) async-start(f32[128,1,512]{2,1,0:T(1,128)} %reshape.287), calls=%async_computation.3 | async-start | bytes 524288 | tf_op jit(solution)/shard_map/all_to_all | solution.py:142
  124.2 29.0 %all-to-all-start.4 = ((f32[128,1,512]{2,1,0:T(1,128)}), f32[128,1,512]{2,1,0:T(1,128)S(1)}, u32[]{:S(2)}, u32[]{:S(2)}) async-start(f32[128,1,512]{2,1,0:T(1,128)} %reshape.289), calls=%async_computation.4 | async-start | bytes 524288 | tf_op jit(solution)/shard_map/all_to_all | solution.py:143
  171.1 17.8 %all-to-all-start.5 = ((f32[16,1,4096]{2,1,0:T(1,128)}), f32[16,1,4096]{2,1,0:T(1,128)S(1)}, u32[]{:S(2)}, u32[]{:S(2)}) async-start(f32[16,1,4096]{2,1,0:T(1,128)} %reshape.291), calls=%async_computation.5 | async-start | bytes 524288 | tf_op jit(solution)/shard_map/all_to_all | solution.py:148
  175.9 23.0 %copy-start.5 = (s32[16,8]{0,1:T(8,128)S(1)}, s32[16,8]{0,1:T(8,128)}, u32[]{:S(2)}) copy-start(s32[16,8]{0,1:T(8,128)} %param.11) | copy-start | bytes 1540
  175.9 23.1 %copy-start.10 = (f32[256]{0:T(256)S(1)}, f32[256]{0:T(256)}, u32[]{:S(2)}) copy-start(f32[256]{0:T(256)} %param.9) | copy-start | bytes 3076
  181.7 18.1 %copy-start.11 = (f32[128]{0:T(128)S(1)}, f32[128]{0:T(128)}, u32[]{:S(2)}) copy-start(f32[128]{0:T(128)} %param.10) | copy-start | bytes 1540
  188.9 23.7 %all-to-all-start.7 = ((f32[16,1,4096]{2,1,0:T(1,128)}), f32[16,1,4096]{2,1,0:T(1,128)S(1)}, u32[]{:S(2)}, u32[]{:S(2)}) async-start(f32[16,1,4096]{2,1,0:T(1,128)} %reshape.293), calls=%async_computation.7 | async-start | bytes 524288 | tf_op jit(solution)/shard_map/all_to_all | solution.py:149
  213.8 3.7 copy-start.1
  218.4 15.3 %all-to-all-start.6 = ((f32[2,256,128]{1,0,2:T(2,128)}), f32[2,256,128]{1,0,2:T(2,128)S(1)}, u32[]{:S(2)}, u32[]{:S(2)}) async-start(f32[2,256,128]{1,0,2:T(2,128)} %copy.131), calls=%async_computation.6 | async-start | bytes 524288 | tf_op jit(solution)/shard_map/all_to_all | solution.py:138
  233.7 11.3 %all-to-all-start.8 = ((f32[2,256,128]{1,0,2:T(2,128)}), f32[2,256,128]{1,0,2:T(2,128)S(1)}, u32[]{:S(2)}, u32[]{:S(2)}) async-start(f32[2,256,128]{1,0,2:T(2,128)} %copy.138), calls=%async_computation.8 | async-start | bytes 524288 | tf_op jit(solution)/shard_map/all_to_all | solution.py:139
  254.4 32.1 %all-to-all-start.9 = ((f32[128,1,512]{2,1,0:T(1,128)}), f32[128,1,512]{2,1,0:T(1,128)S(1)}, u32[]{:S(2)}, u32[]{:S(2)}) async-start(f32[128,1,512]{2,1,0:T(1,128)} %reshape.295), calls=%async_computation.9 | async-start | bytes 524288 | tf_op jit(solution)/shard_map/all_to_all | solution.py:142
  286.5 29.1 %all-to-all-start.10 = ((f32[128,1,512]{2,1,0:T(1,128)}), f32[128,1,512]{2,1,0:T(1,128)}, u32[]{:S(2)}, u32[]{:S(2)}) async-start(f32[128,1,512]{2,1,0:T(1,128)} %reshape.297), calls=%async_computation.10 | async-start | bytes 524288 | tf_op jit(solution)/shard_map/all_to_all | solution.py:143
  334.4 17.8 %all-to-all-start.11 = ((f32[16,1,4096]{2,1,0:T(1,128)}), f32[16,1,4096]{2,1,0:T(1,128)S(1)}, u32[]{:S(2)}, u32[]{:S(2)}) async-start(f32[16,1,4096]{2,1,0:T(1,128)} %reshape.301), calls=%async_computation.11 | async-start | bytes 524288 | tf_op jit(solution)/shard_map/all_to_all | solution.py:148
  352.2 23.7 %all-to-all-start.12 = ((f32[16,1,4096]{2,1,0:T(1,128)}), f32[16,1,4096]{2,1,0:T(1,128)S(1)}, u32[]{:S(2)}, u32[]{:S(2)}) async-start(f32[16,1,4096]{2,1,0:T(1,128)} %reshape.299), calls=%async_computation.12 | async-start | bytes 524288 | tf_op jit(solution)/shard_map/all_to_all | solution.py:149
  362.3 57.2 %all-gather.2.cloned.1.call-start = ((), (), s32[]{:S(2)}) async-start(), calls=%async_computation.13 | async-start | bytes 2621440 | tf_op jit(solution)/shard_map/all_gather | solution.py:39
  380.0 3.8 copy-start.4
  380.0 3.8 copy-start.9
  380.0 3.8 copy-start.7
  380.0 3.9 copy-start.2
  384.8 44.8 %copy-start = (f32[2,2,256,128]{3,2,1,0:T(8,128)S(1)}, f32[2,2,256,128]{3,2,1,0:T(8,128)}, u32[]{:S(2)}) copy-start(f32[2,2,256,128]{3,2,1,0:T(8,128)} %param.6) | copy-start | bytes 1572868
  (1 other events, 0.5 us)
Sparse Core Ops, SparseCore 0:
  383.9 35.5 all-gather.1
where the time goes:
time: 446 us; the launch traced here: 438 us
  waiting for transfers between devices  139 us (31%)
  local copies, waits for them, and re-layouts  109 us (24%)
  starting transfers between devices  95.3 us (21%)
  other arithmetic  33.8 us (8%)
  blocking collectives  26.6 us (6%)
  matrix products  18 us (4%)
  between operations  15.5 us (3%)
    unnamed x44, local copies, waits for them, and re-layouts  52.2 us
    all_gather x1, waiting for transfers between devices, in_one_piece(): lax.all_gather(both, axis, axis=dim, tiled=True)  34.7 us
    all_to_all x2, waiting for transfers between devices, plane_transform(): lax.all_to_all(rows_real, ('tx', 'rx'), split_axis=1, concat_axis=2, tile...  28.2 us
    all_to_all x2, starting transfers between devices, plane_transform(): lax.all_to_all(rows_real, ('tx', 'rx'), split_axis=1, concat_axis=2, tile...  27.7 us
    all_to_all x1, blocking collectives, sent_and_summed(): lax.all_to_all(pieces, axis, split_axis=0, concat_axis=0, tiled=True)  26.6 us
    all_to_all x2, waiting for transfers between devices, plane_transform(): lax.all_to_all(rows_imag, ('tx', 'rx'), split_axis=1, concat_axis=2, tile...  23.9 us
    all_to_all x2, starting transfers between devices, plane_transform(): lax.all_to_all(done_imag, 'rx', split_axis=2, concat_axis=1, tiled=True)  20 us
    all_to_all x2, starting transfers between devices, plane_transform(): lax.all_to_all(real_part, 'tx', split_axis=2, concat_axis=1, tiled=True)  18.6 us
  transfers between devices with their start and end apart: 13, of which 13 were waited for; matrix products, arithmetic and copies ran while one was open for 16% of the time, Pallas kernels for 0%

commit v1 on v0

v1 whole, which is shorter than its diff:
```python
import functools
import math

import jax
import jax.numpy as jnp
import ml_dtypes
import numpy as np
from jax import lax
from jax.experimental import pallas as pl
from jax.experimental.pallas import tpu as pltpu
from jax.sharding import PartitionSpec as P

depth_step = 2.0
step_size = 0.125
root_floor = 0.25
bf16 = jnp.bfloat16
f32 = jnp.float32
nt_form = (((1,), (1,)), ((), ()))
params = pltpu.CompilerParams(vmem_limit_bytes=56 * 1024 * 1024)


def halves(table):
    high = table.astype(np.float32).astype(ml_dtypes.bfloat16)
    low = (table - high.astype(np.float64)).astype(np.float32).astype(ml_dtypes.bfloat16)
    return high, low


def angles(left, right, total):
    return 2.0 * np.pi / total * ((left[:, None] * right[None, :]) % total)


@functools.cache
def tables():
    index = np.arange(128)
    theta = angles(index, index, 128)
    scale = 1.0 / math.sqrt(2048.0)
    cosine, sine = np.cos(theta) * scale, np.sin(theta) * scale
    lanes = np.block([[cosine, -sine], [sine, cosine]])
    theta = angles(np.arange(16), index, 2048)
    twist_heard = np.stack([np.cos(theta), np.sin(theta)])
    twist_heard = np.broadcast_to(twist_heard[:, :, None, :], (2, 16, 8, 128)).astype(np.float32)
    z, tx, y = np.meshgrid(np.arange(16), np.arange(8), np.arange(4), indexing="ij")
    high = (tx * 64 + z * 4 + y).reshape(-1)
    theta = angles(np.arange(512), high, 512)
    cosine, sine = np.cos(theta) * scale, np.sin(theta) * scale
    long = np.zeros((2, 512, 512, 2))
    long[0, :, :, 0], long[0, :, :, 1] = cosine, -sine
    long[1, :, :, 0], long[1, :, :, 1] = sine, cosine
    long = long.reshape(1024, 1024)
    low_of_lane = np.arange(128) % 4
    theta = angles(np.arange(512), low_of_lane, 2048)
    twist_sent = np.stack([np.cos(theta), np.sin(theta)]).astype(np.float32)
    mix = np.zeros((2, 16, 2, 4, 2, 4, 2, 16))
    quarter = ((1, 0), (0, 1), (-1, 0), (0, -1))
    for r0 in range(16):
        for f0 in range(2):
            for mi in range(4):
                for t1 in range(4):
                    c, s = quarter[mi * t1 % 4]
                    mix[0, r0, f0, mi, 0, t1, f0, r0] = c
                    mix[1, r0, f0, mi, 0, t1, f0, r0] = -s
                    mix[0, r0, f0, mi, 1, t1, f0, r0] = s
                    mix[1, r0, f0, mi, 1, t1, f0, r0] = c
    mix = mix.reshape(256, 256).astype(ml_dtypes.bfloat16)
    return dict(
        lanes=halves(lanes),
        twist_heard=twist_heard,
        long=halves(long),
        long_back=halves(long.T.copy()),
        twist_sent=twist_sent,
        mix=mix,
        mix_back=mix.T.copy(),
    )


def split(value):
    high = value.astype(bf16)
    return high, (value - high.astype(f32)).astype(bf16)


def dot(left, right):
    return jnp.dot(left, right, preferred_element_type=f32)


def swap_groups(arrays, width):
    arrays = list(arrays)
    group = lax.broadcasted_iota(jnp.int32, arrays[0].shape, 1) // width
    bit = 1
    while bit < len(arrays):
        high = (group & bit) != 0
        for i in range(len(arrays)):
            if i & bit:
                continue
            a, b = arrays[i], arrays[i | bit]
            arrays[i] = jnp.where(high, pltpu.roll(b, bit * width, 1), a)
            arrays[i | bit] = jnp.where(high, b, pltpu.roll(a, 128 - bit * width, 1))
        bit *= 2
    return arrays


def times(value, c, s):
    re, im = value
    if (c, s) == (1, 0):
        return value
    if (c, s) == (0, 1):
        return -im, re
    if (c, s) == (0, -1):
        return im, -re
    if (c, s) == (-1, 0):
        return -re, -im
    return re * c - im * s, re * s + im * c


def sixteen(values, sign):
    count = len(values)
    if count == 1:
        return values
    even = sixteen(values[0::2], sign)
    odd = sixteen(values[1::2], sign)
    first, second = [], []
    for k in range(count // 2):
        if 4 * k == 0:
            turn = (1, 0)
        elif 4 * k == count:
            turn = (0, sign)
        else:
            angle = 2.0 * math.pi * k / count
            turn = (math.cos(angle), sign * math.sin(angle))
        a, b = even[k], times(odd[k], *turn)
        first.append((a[0] + b[0], a[1] + b[1]))
        second.append((a[0] - b[0], a[1] - b[1]))
    return first + second


def send_kernel(spectrum, out):
    for c in range(2):
        a = spectrum[c, 0].reshape(32, 8, 128)
        b = spectrum[c, 1].reshape(32, 8, 128)
        low = lax.broadcasted_iota(jnp.int32, a.shape, 1) < 4
        out[:, 0, c] = jnp.where(low, a, pltpu.roll(b, 4, 1))
        out[:, 1, c] = jnp.where(low, pltpu.roll(a, 4, 1), b)


def update_kernel(arrived, spectrum, out):
    for c in range(2):
        a = arrived[:, 0, c]
        b = arrived[:, 1, c]
        low = lax.broadcasted_iota(jnp.int32, a.shape, 1) < 4
        first = jnp.where(low, a, pltpu.roll(b, 4, 1)).reshape(256, 128)
        second = jnp.where(low, pltpu.roll(a, 4, 1), b).reshape(256, 128)
        out[c, 0] = spectrum[c, 0] + step_size * first
        out[c, 1] = spectrum[c, 1] + step_size * second


def pack_kernel(measured, weights, out):
    for k in range(3):
        pieces = []
        for q in range(4):
            for f0 in range(2):
                rows = pl.ds(q * 64, 64)
                pieces.append(measured[k, f0, rows, :] if k < 2 else weights[rows, :])
        for d, piece in enumerate(swap_groups(pieces, 16)):
            out[d, k * 64 : (k + 1) * 64, :] = piece


def unpack_kernel(arrived, out):
    for k in range(2):
        pieces = [arrived[d, k * 64 : (k + 1) * 64, :] for d in range(8)]
        for g, piece in enumerate(swap_groups(pieces, 16)):
            out[k, g % 2, pl.ds(g // 2 * 64, 64), :] = piece


def pair_kernel(arrived, turn, twist, table_high, table_low, out):
    low = lax.broadcasted_iota(jnp.int32, (8, 128), 0) < 4
    for y in range(4):
        points = []
        for z in range(16):
            wr, wi = turn[0, z, y], turn[1, z, y]
            pr = pi = None
            for layer in range(7, -1, -1):
                re, im = arrived[z, layer // 2, 0], arrived[z, layer // 2, 1]
                if layer % 2:
                    re = jnp.where(low, pltpu.roll(re, 4, 0), re)
                    im = jnp.where(low, pltpu.roll(im, 4, 0), im)
                else:
                    re = jnp.where(low, re, pltpu.roll(re, 4, 0))
                    im = jnp.where(low, im, pltpu.roll(im, 4, 0))
                if pr is not None:
                    re, im = re + (pr * wr + pi * wi), im + (pi * wr - pr * wi)
                pr, pi = re, im
            points.append((pr * wr + pi * wi, pi * wr - pr * wi))
        points = sixteen(points, 1)
        res, ims = [], []
        for r0, (re, im) in enumerate(points):
            tr, ti = twist[0, r0], twist[1, r0]
            res.append(re * tr - im * ti)
            ims.append(re * ti + im * tr)
        both = jnp.concatenate([jnp.concatenate(res, 0), jnp.concatenate(ims, 0)], 1)
        high, rest = split(both)
        stacked = jnp.concatenate([high, rest], 0)
        first = lax.dot_general(table_high[...], stacked, nt_form, preferred_element_type=f32)
        second = lax.dot_general(table_low[...], high, nt_form, preferred_element_type=f32)
        done = first[:, :128] + first[:, 128:] + second
        for c in range(2):
            out[pl.ds(y * 2 + c, 128, stride=8), :] = done[c * 128 : (c + 1) * 128]


def gradient_kernel(arrived, turn, twist, table_high, table_low, out, points):
    for y in range(4):
        re = arrived[pl.ds(y * 2, 128, stride=8), :]
        im = arrived[pl.ds(y * 2 + 1, 128, stride=8), :]
        both = jnp.concatenate([re.T, im.T], 1)
        high, rest = split(both)
        first = dot(jnp.concatenate([high, rest], 0), table_high[...])
        done = first[:128] + first[128:] + dot(high, table_low[...])
        values = []
        for r0 in range(16):
            re = done[r0 * 8 : (r0 + 1) * 8, :128]
            im = done[r0 * 8 : (r0 + 1) * 8, 128:]
            tr, ti = twist[0, r0], twist[1, r0]
            values.append((re * tr + im * ti, im * tr - re * ti))
        for z, (re, im) in enumerate(sixteen(values, -1)):
            points[y, z, 0] = re
            points[y, z, 1] = im
    low = lax.broadcasted_iota(jnp.int32, (8, 128), 0) < 4
    for z in range(16):
        sums = [None] * 8
        for y in range(4):
            wr, wi = turn[0, z, y], turn[1, z, y]
            re, im = points[y, z, 0], points[y, z, 1]
            for layer in range(8):
                re, im = re * wr - im * wi, im * wr + re * wi
                if sums[layer] is None:
                    sums[layer] = (re, im)
                else:
                    sums[layer] = (sums[layer][0] + re, sums[layer][1] + im)
        for y in range(4):
            for c in range(2):
                a, b = sums[2 * y][c], sums[2 * y + 1][c]
                x = jnp.where(low, a, pltpu.roll(b, 4, 0))
                w = jnp.where(low, pltpu.roll(a, 4, 0), b)
                out[z, y, c] = x + w


def middle_kernel(
    arrived,
    echoes,
    twist,
    mix,
    mix_back,
    long_high,
    long_low,
    back_high,
    back_low,
    out,
    resid,
):
    high, rest = split(arrived[...])
    first = dot(long_high[...], jnp.concatenate([high, rest], 1))
    done = first[:, :128] + first[:, 128:] + dot(long_low[...], high)
    re, im = done[:512], done[512:]
    tr, ti = twist[0], twist[1]
    both = jnp.concatenate([re * tr - im * ti, re * ti + im * tr], 1)
    high, rest = split(both)
    field = dot(high, mix[...]) + dot(rest, mix[...])
    parts = []
    for k in range(3):
        rows = []
        for odd in range(2):
            pieces = [echoes[2 * t1 + odd, k * 64 : (k + 1) * 64, :] for t1 in range(4)]
            rows += swap_groups(pieces, 32)
        parts.append(jnp.concatenate(rows, 0))
    left = []
    for k in range(2):
        value = parts[2] * (parts[k] - field[:, k * 128 : (k + 1) * 128])
        left.append(value)
        for odd in range(2):
            pieces = [value[odd * 256 + q * 64 : odd * 256 + (q + 1) * 64] for q in range(4)]
            for t1, piece in enumerate(swap_groups(pieces, 32)):
                resid[2 * t1 + odd, k * 64 : (k + 1) * 64, :] = piece
    high, rest = split(jnp.concatenate(left, 1))
    mixed = dot(high, mix_back[...]) + dot(rest, mix_back[...])
    re, im = mixed[:, :128], mixed[:, 128:]
    both = jnp.concatenate([re * tr + im * ti, im * tr - re * ti], 0)
    high, rest = split(both)
    first = dot(back_high[...], jnp.concatenate([high, rest], 1))
    out[...] = first[:, :128] + first[:, 128:] + dot(back_low[...], high)


def call(kernel, shapes, *operands, scratch=(), flops=0):
    single = not isinstance(shapes, list)
    shapes = [shapes] if single else shapes
    spec = pl.BlockSpec(memory_space=pltpu.VMEM)
    bytes_moved = sum(math.prod(s) * 4 for s in shapes) + sum(
        o.size * o.dtype.itemsize for o in operands
    )
    out = pl.pallas_call(
        kernel,
        out_shape=[jax.ShapeDtypeStruct(s, f32) for s in shapes],
        in_specs=[spec] * len(operands),
        out_specs=[spec] * len(shapes),
        scratch_shapes=list(scratch),
        compiler_params=params,
        cost_estimate=pl.CostEstimate(
            flops=flops, bytes_accessed=bytes_moved, transcendentals=0
        ),
    )(*operands)
    return out[0] if single else out


def exchange(value, axes):
    return lax.all_to_all(value, axes, split_axis=0, concat_axis=0, tiled=True)


def wave_numbers(indices, total):
    signed = jnp.where(indices < total // 2, indices, indices - total)
    return 2.0 * jnp.pi / total * signed.astype(f32)


def turns(wavenumber, tx, z, y):
    low = jnp.arange(8, dtype=jnp.int32) % 4
    sent = wave_numbers(tx * 256 + z * 16 + y * 4 + low, 2048)
    heard = wave_numbers(jnp.arange(2048, dtype=jnp.int32).reshape(16, 1, 1, 128), 2048)
    waves = jnp.repeat(wavenumber.reshape(4, 2), 4, axis=1)
    squared = waves * waves
    first = jnp.sqrt(jnp.maximum(squared - (sent * sent)[None, :], 0.0) + root_floor)
    second = jnp.sqrt(
        jnp.maximum(squared[None, :, :, None] - heard * heard, 0.0) + root_floor
    )
    phase = depth_step * (first[None, :, :, None] + second)
    return jnp.stack([jnp.cos(phase), jnp.sin(phase)])


def per_device(spectrum, measured, wavenumber, send_weight, hear_weight, aperture):
    table = tables()
    tx, z, y = lax.axis_index("tx"), lax.axis_index("rx"), lax.axis_index("freq")

    sent = call(send_kernel, (32, 2, 2, 8, 128), spectrum)
    arrived = exchange(sent.reshape(64, 16, 128), ("rx", "freq"))

    turn = turns(wavenumber, tx, z, y)
    gate = aperture.astype(f32)
    weights = (
        send_weight.reshape(16, 16, 1, 1)
        * gate.reshape(16, 1, 8, 1)
        * hear_weight.reshape(1, 1, 8, 16)
    ).reshape(256, 128)
    echoes = exchange(call(pack_kernel, (8, 192, 128), measured, weights), "tx")

    pairs = call(
        pair_kernel,
        (1024, 128),
        arrived.reshape(16, 4, 2, 8, 128),
        turn,
        table["twist_heard"],
        *table["lanes"],
        flops=10**9,
    )
    columns = exchange(pairs.reshape(512, 2, 128), ("rx", "tx", "freq")).reshape(1024, 128)
    back, resid = call(
        middle_kernel,
        [(1024, 128), (8, 128, 128)],
        columns,
        echoes,
        table["twist_sent"],
        table["mix"],
        table["mix_back"],
        *table["long"],
        *table["long_back"],
        flops=3 * 10**9,
    )
    rows = exchange(back.reshape(512, 2, 128), ("rx", "tx", "freq")).reshape(1024, 128)
    residual = call(unpack_kernel, (2, 2, 256, 128), exchange(resid, "tx"))
    gradient = call(
        gradient_kernel,
        (16, 4, 2, 8, 128),
        rows,
        turn,
        table["twist_heard"],
        *table["lanes"],
        scratch=[pltpu.VMEM((4, 16, 2, 8, 128), f32)],
        flops=10**9,
    )
    gathered = exchange(gradient.reshape(64, 16, 128), ("rx", "freq"))
    updated = call(
        update_kernel, (2, 2, 256, 128), gathered.reshape(32, 2, 2, 8, 128), spectrum
    )
    return updated, residual


def solution(mesh):
    placed = (
        P(None, "freq", "tx", "rx"),
        P(None, "freq", "tx", "rx"),
        P(),
        P("tx"),
        P("rx"),
        P("tx", "rx"),
    )
    return jax.shard_map(
        per_device,
        mesh=mesh,
        in_specs=placed,
        out_specs=(P(None, "freq", "tx", "rx"), P(None, "freq", "tx", "rx")),
        check_vma=False,
    )
```

time: 446 us -> 226 us (0.51); the launches traced: 438 us -> 223 us
  local copies, waits for them, and re-layouts: 109 us -> 1.84 us
  waiting for transfers between devices: 139 us -> 64.9 us
  blocking collectives: 26.6 us -> 92.9 us
  starting transfers between devices: 95.3 us -> 35.8 us
  other arithmetic: 33.8 us -> 2.73 us
  Pallas kernels: 0 us -> 23.6 us
  matrix products: 18 us -> 0 us
  between operations: 15.5 us -> 0.8 us
    all_to_all x1 -> x2, blocking collectives: 26.6 us -> 92.9 us  [exchange(): return lax.all_to_all(value, axes, split_axis=0, concat_axis=0, tiled=True)]
    all_to_all x12 -> x4, starting transfers between devices: 95.3 us -> 35.8 us  [exchange(): return lax.all_to_all(value, axes, split_axis=0, concat_axis=0, tiled=True)]
    unnamed x44 -> x16, local copies, waits for them, and re-layouts: 52.2 us -> 0.82 us
    all_to_all x12 -> x4, waiting for transfers between devices: 104 us -> 64.9 us  [exchange(): return lax.all_to_all(value, axes, split_axis=0, concat_axis=0, tiled=True)]
    all_gather x1 -> x0, waiting for transfers between devices: 34.7 us -> none  [in_one_piece(): lax.all_gather(both, axis, axis=dim, tiled=True)]
    pallas_call x0 -> x7, Pallas kernels: none -> 23.6 us  [call(): pl.pallas_call(kernel, out_shape=[jax.ShapeDtypeStruct(s, f32) for s in s...]
    reshape x12 -> x0, local copies, waits for them, and re-layouts: 19 us -> none  [the longest x4 8.46 us: transform_last(): (final_imag * scale).reshape(leading + (total,))]
    dot_general x32 -> x0, matrix products: 18 us -> none  [einsum_of(): return jnp.einsum(form, operand, table, precision=highest)]
  transfers between devices with their start and end apart: 13 -> 4, of which waited for: 13 -> 4; matrix products, arithmetic and copies ran while one was open for 16% -> 2% of each run, Pallas kernels for 0% -> 5%
where the time goes in v1:
time: 226 us; the launch traced here: 223 us
  blocking collectives  92.9 us (41%)
  waiting for transfers between devices  64.9 us (29%)
  starting transfers between devices  35.8 us (16%)
  Pallas kernels  23.6 us (10%)
  other arithmetic  2.73 us (1%)
    all_to_all x2, blocking collectives, exchange(): return lax.all_to_all(value, axes, split_axis=0, concat_axis=0, tiled=True)  92.9 us
    all_to_all x4, waiting for transfers between devices, exchange(): return lax.all_to_all(value, axes, split_axis=0, concat_axis=0, tiled=True)  64.9 us
    all_to_all x4, starting transfers between devices, exchange(): return lax.all_to_all(value, axes, split_axis=0, concat_axis=0, tiled=True)  35.8 us
    pallas_call x7, Pallas kernels, call(): pl.pallas_call(kernel, out_shape=[jax.ShapeDtypeStruct(s, f32) for s in s...  23.6 us
  transfers between devices with their start and end apart: 4, of which 4 were waited for; matrix products, arithmetic and copies ran while one was open for 2% of the time, Pallas kernels for 5%

profile of v1, /device:TPU:1, one launch (start us, length us, event | category | flops | bytes accessed | tf_op | source)
XLA Modules:
  0.0 222.6 jit_solution(6212794584994434948)
XLA Ops:
  0.7 1.9 shard_map.167
  2.6 19.3 %all-to-all-start = ((f32[64,16,128]{2,1,0:T(8,128)}), f32[64,16,128]{2,1,0:T(8,128)S(1)}, u32[]{:S(2)}, u32[]{:S(2)}) async-start(f32[64,16,128]{2,1,0:T(8,128)} %bitcast.11), calls=%async_computation | async-start | bytes 1048576 | tf_op jit(solution)/shard_map/all_to_all | solution.py:312
  22.1 0.1 broadcast_multiply_fusion.1
  22.2 0.3 mul.129
  22.5 0.3 mul.130
  22.9 0.7 broadcast_multiply_fusion.weights
  23.5 2.8 %shard_map.169 = f32[8,192,128]{2,1,0:T(8,128)} custom-call(f32[2,2,256,128]{3,2,1,0:T(8,128)} %measured.1, f32[256,128]{1,0:T(8,128)} %broadcast_multiply_fusion.weights), custom_call_target="tpu_custom_call" | custom-call | bytes 1441792 | tf_op jit(solution)/shard_map/pallas_call | solution.py:297
  26.3 25.6 %all-to-all-done = f32[64,16,128]{2,1,0:T(8,128)S(1)} async-done(((f32[64,16,128]{2,1,0:T(8,128)}), f32[64,16,128]{2,1,0:T(8,128)S(1)}, u32[]{:S(2)}, u32[]{:S(2)}) %all-to-all-start) | async-done | bytes 524320 | tf_op jit(solution)/shard_map/all_to_all | solution.py:312
  51.9 8.1 %all-to-all-start.2 = ((f32[8,192,128]{2,1,0:T(8,128)}), f32[8,192,128]{2,1,0:T(8,128)S(1)}, u32[]{:S(2)}, u32[]{:S(2)}) async-start(f32[8,192,128]{2,1,0:T(8,128)} %shard_map.169), calls=%async_computation.2 | async-start | bytes 1572864 | tf_op jit(solution)/shard_map/all_to_all | solution.py:312
  60.2 1.1 fusion.1
  61.3 0.8 pad_maximum_fusion.turn
  62.2 3.4 %shard_map.168 = f32[1024,128]{1,0:T(8,128)} custom-call(f32[16,4,2,8,128]{4,3,2,1,0:T(8,128)} %bitcast.12, f32[2,16,4,8,128]{4,3,2,1,0:T(8,128)} %pad_maximum_fusion.turn, f32[2,16,8,128]{3,2,1,0:T(8,128)} %constant.80.clone.twist, bf16[256,256]{1,0:T(8,128)(2,1)} %constant.81.clone.table_high, bf16[256,256]{1,0:T(8,128)(2,1)} %constant.82.clone.table_low), custom_call_target="tpu_custom_call" | custom-call | flops 1000000000 | bytes 1966080 | tf_op jit(solution)/shard_map/pallas_call | solution.py:297
  65.5 6.7 %all-to-all-done.2.echoes = f32[8,192,128]{2,1,0:T(8,128)S(1)} async-done(((f32[8,192,128]{2,1,0:T(8,128)}), f32[8,192,128]{2,1,0:T(8,128)S(1)}, u32[]{:S(2)}, u32[]{:S(2)}) %all-to-all-start.2) | async-done | bytes 786464 | tf_op jit(solution)/shard_map/all_to_all | solution.py:312
  72.2 47.3 %all_to_all.30 = f32[512,2,128]{2,1,0:T(2,128)} all-to-all(f32[512,2,128]{2,1,0:T(2,128)} %bitcast.17), channel_id=1, replica_groups=mesh['tx'=8,'rx'=16,'freq'=4] {'rx','tx','freq'}, dimensions={0} | all-to-all | bytes 1048576 | tf_op jit(solution)/shard_map/all_to_all | solution.py:312
  119.5 7.9 %shard_map.170 = (f32[1024,128]{1,0:T(8,128)}, f32[8,128,128]{2,1,0:T(8,128)}) custom-call(f32[1024,128]{1,0:T(8,128)} %bitcast.14, f32[8,192,128]{2,1,0:T(8,128)} %copy-done.2, f32[2,512,128]{2,1,0:T(8,128)} %constant.83.clone.twist, bf16[256,256]{1,0:T(8,128)(2,1)} %constant.84.clone.mix, bf16[256,256]{1,0:T(8,128)(2,1)} %constant.85.clone.mix_back, ...), custom_call_target="tpu_custom_call" | custom-call | flops 3000000000 | bytes 11534336 | tf_op jit(solution)/shard_map/pallas_call | solution.py:297
  127.4 45.6 %all_to_all.31 = f32[512,2,128]{2,1,0:T(2,128)} all-to-all(f32[512,2,128]{2,1,0:T(2,128)} %bitcast.15), channel_id=1, replica_groups=mesh['tx'=8,'rx'=16,'freq'=4] {'rx','tx','freq'}, dimensions={0} | all-to-all | bytes 1048576 | tf_op jit(solution)/shard_map/all_to_all | solution.py:312
  173.0 3.4 %all-to-all-start.5 = ((f32[8,128,128]{2,1,0:T(8,128)}), f32[8,128,128]{2,1,0:T(8,128)S(1)}, u32[]{:S(2)}, u32[]{:S(2)}) async-start(f32[8,128,128]{2,1,0:T(8,128)} %get-tuple-element.5), calls=%async_computation.5 | async-start | bytes 1048576 | tf_op jit(solution)/shard_map/all_to_all | solution.py:312
  176.4 3.2 %shard_map.171 = f32[16,4,2,8,128]{4,3,2,1,0:T(8,128)} custom-call(f32[1024,128]{1,0:T(8,128)} %bitcast.16, f32[2,16,4,8,128]{4,3,2,1,0:T(8,128)} %pad_maximum_fusion.turn, f32[2,16,8,128]{3,2,1,0:T(8,128)} %constant.80.clone.twist, bf16[256,256]{1,0:T(8,128)(2,1)} %constant.81.clone.table_high, bf16[256,256]{1,0:T(8,128)(2,1)} %constant.82.clone.table_low), custom_call_target="tpu_custom_call" | custom-call | flops 1000000000 | bytes 1966080 | tf_op jit(solution)/shard_map/pallas_call | solution.py:297
  179.6 5.8 %all-to-all-done.5.arrived = f32[8,128,128]{2,1,0:T(8,128)S(1)} async-done(((f32[8,128,128]{2,1,0:T(8,128)}), f32[8,128,128]{2,1,0:T(8,128)S(1)}, u32[]{:S(2)}, u32[]{:S(2)}) %all-to-all-start.5) | async-done | bytes 524320 | tf_op jit(solution)/shard_map/all_to_all | solution.py:312
  185.4 5.0 %all-to-all-start.4 = ((f32[64,16,128]{2,1,0:T(8,128)}), f32[64,16,128]{2,1,0:T(8,128)S(1)}, u32[]{:S(2)}, u32[]{:S(2)}) async-start(f32[64,16,128]{2,1,0:T(8,128)} %bitcast.13), calls=%async_computation.4 | async-start | bytes 1048576 | tf_op jit(solution)/shard_map/all_to_all | solution.py:312
  190.5 2.4 %shard_map.173 = f32[2,2,256,128]{3,2,1,0:T(8,128)} custom-call(f32[8,128,128]{2,1,0:T(8,128)} %copy-done.1), custom_call_target="tpu_custom_call" | custom-call | bytes 1048576 | tf_op jit(solution)/shard_map/pallas_call | solution.py:297
  192.9 26.8 %all-to-all-done.4 = f32[64,16,128]{2,1,0:T(8,128)S(1)} async-done(((f32[64,16,128]{2,1,0:T(8,128)}), f32[64,16,128]{2,1,0:T(8,128)S(1)}, u32[]{:S(2)}, u32[]{:S(2)}) %all-to-all-start.4) | async-done | bytes 524320 | tf_op jit(solution)/shard_map/all_to_all | solution.py:312
  219.7 0.8 copy-done
  220.5 2.1 shard_map.172
  (25 shorter events, 0.5 us)
Async XLA Ops:
  0.6 21.3 %copy-start.4 = (s32[16,8]{0,1:T(8,128)S(1)}, s32[16,8]{0,1:T(8,128)}, u32[]{:S(2)}) copy-start(s32[16,8]{0,1:T(8,128)} %param.21) | copy-start | bytes 1540
  0.6 21.3 %copy-start.5 = (f32[256]{0:T(256)S(1)}, f32[256]{0:T(256)}, u32[]{:S(2)}) copy-start(f32[256]{0:T(256)} %param.19) | copy-start | bytes 3076
  0.7 22.2 %copy-start.6 = (f32[128]{0:T(128)S(1)}, f32[128]{0:T(128)}, u32[]{:S(2)}) copy-start(f32[128]{0:T(128)} %param.20) | copy-start | bytes 1540
  2.6 49.3 %all-to-all-start = ((f32[64,16,128]{2,1,0:T(8,128)}), f32[64,16,128]{2,1,0:T(8,128)S(1)}, u32[]{:S(2)}, u32[]{:S(2)}) async-start(f32[64,16,128]{2,1,0:T(8,128)} %bitcast.11), calls=%async_computation | async-start | bytes 1048576 | tf_op jit(solution)/shard_map/all_to_all | solution.py:312
  22.5 37.5 %copy-start.7 = (f32[8]{0:T(128)S(1)}, f32[8]{0:T(128)}, u32[]{:S(2)}) copy-start(f32[8]{0:T(128)} %param.18) | copy-start | bytes 100
  51.9 10.3 %copy-start.3 = (f32[64,16,128]{2,1,0:T(8,128)}, f32[64,16,128]{2,1,0:T(8,128)S(1)}, u32[]{:S(2)}) copy-start(f32[64,16,128]{2,1,0:T(8,128)S(1)} %all-to-all-done) | copy-start | bytes 1572868
  51.9 20.3 %all-to-all-start.2 = ((f32[8,192,128]{2,1,0:T(8,128)}), f32[8,192,128]{2,1,0:T(8,128)S(1)}, u32[]{:S(2)}, u32[]{:S(2)}) async-start(f32[8,192,128]{2,1,0:T(8,128)} %shard_map.169), calls=%async_computation.2 | async-start | bytes 1572864 | tf_op jit(solution)/shard_map/all_to_all | solution.py:312
  72.2 47.3 %copy-start.2 = (f32[8,192,128]{2,1,0:T(8,128)}, f32[8,192,128]{2,1,0:T(8,128)S(1)}, u32[]{:S(2)}) copy-start(f32[8,192,128]{2,1,0:T(8,128)S(1)} %all-to-all-done.2.echoes) | copy-start | bytes 2359300
  173.0 12.4 %all-to-all-start.5 = ((f32[8,128,128]{2,1,0:T(8,128)}), f32[8,128,128]{2,1,0:T(8,128)S(1)}, u32[]{:S(2)}, u32[]{:S(2)}) async-start(f32[8,128,128]{2,1,0:T(8,128)} %get-tuple-element.5), calls=%async_computation.5 | async-start | bytes 1048576 | tf_op jit(solution)/shard_map/all_to_all | solution.py:312
  185.4 5.1 %copy-start.1 = (f32[8,128,128]{2,1,0:T(8,128)}, f32[8,128,128]{2,1,0:T(8,128)S(1)}, u32[]{:S(2)}) copy-start(f32[8,128,128]{2,1,0:T(8,128)S(1)} %all-to-all-done.5.arrived) | copy-start | bytes 1572868
  185.4 34.3 %all-to-all-start.4 = ((f32[64,16,128]{2,1,0:T(8,128)}), f32[64,16,128]{2,1,0:T(8,128)S(1)}, u32[]{:S(2)}, u32[]{:S(2)}) async-start(f32[64,16,128]{2,1,0:T(8,128)} %bitcast.13), calls=%async_computation.4 | async-start | bytes 1048576 | tf_op jit(solution)/shard_map/all_to_all | solution.py:312
  219.7 0.8 copy-start

commit v2 on v1

--- a/solution.py
+++ b/solution.py
@@ -32,21 +32,17 @@
 @functools.cache
 def tables():
     index = np.arange(128)
-    theta = angles(index, index, 128)
+    order = index.reshape(16, 8).T.reshape(-1)
+    theta = angles(order, index, 128)
     scale = 1.0 / math.sqrt(2048.0)
     cosine, sine = np.cos(theta) * scale, np.sin(theta) * scale
     lanes = np.block([[cosine, -sine], [sine, cosine]])
     theta = angles(np.arange(16), index, 2048)
     twist_heard = np.stack([np.cos(theta), np.sin(theta)])
     twist_heard = np.broadcast_to(twist_heard[:, :, None, :], (2, 16, 8, 128)).astype(np.float32)
-    z, tx, y = np.meshgrid(np.arange(16), np.arange(8), np.arange(4), indexing="ij")
-    high = (tx * 64 + z * 4 + y).reshape(-1)
-    theta = angles(np.arange(512), high, 512)
-    cosine, sine = np.cos(theta) * scale, np.sin(theta) * scale
-    long = np.zeros((2, 512, 512, 2))
-    long[0, :, :, 0], long[0, :, :, 1] = cosine, -sine
-    long[1, :, :, 0], long[1, :, :, 1] = sine, cosine
-    long = long.reshape(1024, 1024)
+    index = np.arange(512)
+    theta = angles(index, index, 512)
+    long = halves(np.cos(theta) * scale) + halves(np.sin(theta) * scale)
     low_of_lane = np.arange(128) % 4
     theta = angles(np.arange(512), low_of_lane, 2048)
     twist_sent = np.stack([np.cos(theta), np.sin(theta)]).astype(np.float32)
@@ -65,8 +61,7 @@
     return dict(
         lanes=halves(lanes),
         twist_heard=twist_heard,
-        long=halves(long),
-        long_back=halves(long.T.copy()),
+        long=long,
         twist_sent=twist_sent,
         mix=mix,
         mix_back=mix.T.copy(),
@@ -152,7 +147,8 @@
         out[c, 1] = spectrum[c, 1] + step_size * second
 
 
-def pack_kernel(measured, weights, out):
+def pack_kernel(place, measured, weights, *refs):
+    *outs, held = refs
     for k in range(3):
         pieces = []
         for q in range(4):
@@ -160,12 +156,17 @@
                 rows = pl.ds(q * 64, 64)
                 pieces.append(measured[k, f0, rows, :] if k < 2 else weights[rows, :])
         for d, piece in enumerate(swap_groups(pieces, 16)):
-            out[d, k * 64 : (k + 1) * 64, :] = piece
-
-
-def unpack_kernel(arrived, out):
+            held[d, k * 64 : (k + 1) * 64, :] = piece
+    for step in range(8):
+        outs[step][...] = held[(place[0] + step) & 7]
+
+
+def unpack_kernel(place, *refs):
+    *arrived, out, held = refs
+    for step in range(8):
+        held[(place[0] + 8 - step) & 7] = arrived[step][...]
     for k in range(2):
-        pieces = [arrived[d, k * 64 : (k + 1) * 64, :] for d in range(8)]
+        pieces = [held[d, k * 64 : (k + 1) * 64, :] for d in range(8)]
         for g, piece in enumerate(swap_groups(pieces, 16)):
             out[k, g % 2, pl.ds(g // 2 * 64, 64), :] = piece
 
@@ -242,23 +243,29 @@
                 out[z, y, c] = x + w
 
 
-def middle_kernel(
-    arrived,
-    echoes,
-    twist,
-    mix,
-    mix_back,
-    long_high,
-    long_low,
-    back_high,
-    back_low,
-    out,
-    resid,
-):
-    high, rest = split(arrived[...])
-    first = dot(long_high[...], jnp.concatenate([high, rest], 1))
-    done = first[:, :128] + first[:, 128:] + dot(long_low[...], high)
-    re, im = done[:512], done[512:]
+def long_sums(re, im, tables_of):
+    re_high, re_low = split(re)
+    im_high, im_low = split(im)
+    whole = jnp.concatenate([re_high, re_low, im_high, im_low], 1)
+    high = jnp.concatenate([re_high, im_high], 1)
+    sums = []
+    for k in range(2):
+        first = dot(tables_of[2 * k][...], whole)
+        second = dot(tables_of[2 * k + 1][...], high)
+        sums.append(first[:, :128] + first[:, 128:256] + second[:, :128])
+        sums.append(first[:, 256:384] + first[:, 384:] + second[:, 128:])
+    return sums
+
+
+def middle_kernel(place, arrived, twist, mix, mix_back, *refs):
+    long, echoes, out, sent = refs[:4], refs[4:12], refs[12], refs[13:21]
+    held, resid = refs[21:]
+    for step in range(8):
+        held[(place[0] + 8 - step) & 7] = echoes[step][...]
+    cos_re, cos_im, sin_re, sin_im = long_sums(
+        arrived[pl.ds(0, 512, stride=2), :], arrived[pl.ds(1, 512, stride=2), :], long
+    )
+    re, im = cos_re - sin_im, sin_re + cos_im
     tr, ti = twist[0], twist[1]
     both = jnp.concatenate([re * tr - im * ti, re * ti + im * tr], 1)
     high, rest = split(both)
@@ -267,7 +274,7 @@
     for k in range(3):
         rows = []
         for odd in range(2):
-            pieces = [echoes[2 * t1 + odd, k * 64 : (k + 1) * 64, :] for t1 in range(4)]
+            pieces = [held[2 * t1 + odd, k * 64 : (k + 1) * 64, :] for t1 in range(4)]
             rows += swap_groups(pieces, 32)
         parts.append(jnp.concatenate(rows, 0))
     left = []
@@ -278,28 +285,33 @@
             pieces = [value[odd * 256 + q * 64 : odd * 256 + (q + 1) * 64] for q in range(4)]
             for t1, piece in enumerate(swap_groups(pieces, 32)):
                 resid[2 * t1 + odd, k * 64 : (k + 1) * 64, :] = piece
+    for step in range(8):
+        sent[step][...] = resid[(place[0] + step) & 7]
     high, rest = split(jnp.concatenate(left, 1))
     mixed = dot(high, mix_back[...]) + dot(rest, mix_back[...])
     re, im = mixed[:, :128], mixed[:, 128:]
-    both = jnp.concatenate([re * tr + im * ti, im * tr - re * ti], 0)
-    high, rest = split(both)
-    first = dot(back_high[...], jnp.concatenate([high, rest], 1))
-    out[...] = first[:, :128] + first[:, 128:] + dot(back_low[...], high)
-
-
-def call(kernel, shapes, *operands, scratch=(), flops=0):
+    cos_re, cos_im, sin_re, sin_im = long_sums(re * tr + im * ti, im * tr - re * ti, long)
+    out[pl.ds(0, 512, stride=2), :] = cos_re + sin_im
+    out[pl.ds(1, 512, stride=2), :] = cos_im - sin_re
+
+
+def call(kernel, shapes, *operands, scratch=(), place=None, flops=0):
     single = not isinstance(shapes, list)
     shapes = [shapes] if single else shapes
     spec = pl.BlockSpec(memory_space=pltpu.VMEM)
+    in_specs = [spec] * len(operands)
     bytes_moved = sum(math.prod(s) * 4 for s in shapes) + sum(
         o.size * o.dtype.itemsize for o in operands
     )
+    if place is not None:
+        operands = (place, *operands)
+        in_specs = [pl.BlockSpec(memory_space=pltpu.SMEM), *in_specs]
     out = pl.pallas_call(
         kernel,
         out_shape=[jax.ShapeDtypeStruct(s, f32) for s in shapes],
-        in_specs=[spec] * len(operands),
+        in_specs=in_specs,
         out_specs=[spec] * len(shapes),
-        scratch_shapes=list(scratch),
+        scratch_shapes=[pltpu.VMEM(s, f32) for s in scratch],
         compiler_params=params,
         cost_estimate=pl.CostEstimate(
             flops=flops, bytes_accessed=bytes_moved, transcendentals=0
@@ -310,6 +322,13 @@
 
 def exchange(value, axes):
     return lax.all_to_all(value, axes, split_axis=0, concat_axis=0, tiled=True)
+
+
+def along_tx(pieces):
+    moved = [pieces[0]]
+    for step in range(1, 8):
+        moved.append(lax.ppermute(pieces[step], "tx", [(i, (i + step) % 8) for i in range(8)]))
+    return moved
 
 
 def wave_numbers(indices, total):
@@ -345,7 +364,17 @@
         * gate.reshape(16, 1, 8, 1)
         * hear_weight.reshape(1, 1, 8, 16)
     ).reshape(256, 128)
-    echoes = exchange(call(pack_kernel, (8, 192, 128), measured, weights), "tx")
+    place = tx.astype(jnp.int32).reshape(1)
+    echoes = along_tx(
+        call(
+            pack_kernel,
+            [(192, 128)] * 8,
+            measured,
+            weights,
+            scratch=[(8, 192, 128)],
+            place=place,
+        )
+    )
 
     pairs = call(
         pair_kernel,
@@ -356,21 +385,28 @@
         *table["lanes"],
         flops=10**9,
     )
-    columns = exchange(pairs.reshape(512, 2, 128), ("rx", "tx", "freq")).reshape(1024, 128)
-    back, resid = call(
+    columns = exchange(pairs.reshape(512, 2, 128), ("tx", "rx", "freq")).reshape(1024, 128)
+    back, *resid = call(
         middle_kernel,
-        [(1024, 128), (8, 128, 128)],
+        [(1024, 128)] + [(128, 128)] * 8,
         columns,
-        echoes,
         table["twist_sent"],
         table["mix"],
         table["mix_back"],
         *table["long"],
-        *table["long_back"],
+        *echoes,
+        scratch=[(8, 192, 128), (8, 128, 128)],
+        place=place,
         flops=3 * 10**9,
     )
-    rows = exchange(back.reshape(512, 2, 128), ("rx", "tx", "freq")).reshape(1024, 128)
-    residual = call(unpack_kernel, (2, 2, 256, 128), exchange(resid, "tx"))
+    rows = exchange(back.reshape(512, 2, 128), ("tx", "rx", "freq")).reshape(1024, 128)
+    residual = call(
+        unpack_kernel,
+        (2, 2, 256, 128),
+        *along_tx(resid),
+        scratch=[(8, 128, 128)],
+        place=place,
+    )
     gradient = call(
         gradient_kernel,
         (16, 4, 2, 8, 128),
@@ -378,7 +414,7 @@
         turn,
         table["twist_heard"],
         *table["lanes"],
-        scratch=[pltpu.VMEM((4, 16, 2, 8, 128), f32)],
+        scratch=[(4, 16, 2, 8, 128)],
         flops=10**9,
     )
     gathered = exchange(gradient.reshape(64, 16, 128), ("rx", "freq"))

time: 226 us -> 205 us (0.907)
  blocking collectives: 92.9 us -> 49.1 us
  starting transfers between devices: 35.8 us -> 77.8 us
  waiting for transfers between devices: 64.9 us -> 43.7 us
  local copies, waits for them, and re-layouts: 1.84 us -> 5.62 us
    all_to_all x2 -> x1, blocking collectives: 92.9 us -> 49.1 us  [exchange(): return lax.all_to_all(value, axes, split_axis=0, concat_axis=0, tiled=True)]
    ppermute x0 -> x14, starting transfers between devices: none -> 38 us  [along_tx(): lax.ppermute(pieces[step], 'tx', [(i, (i + step) % 8) for i in range(8)])]
    all_to_all x4 -> x3, waiting for transfers between devices: 64.9 us -> 34.8 us  [exchange(): return lax.all_to_all(value, axes, split_axis=0, concat_axis=0, tiled=True)]
    ppermute x0 -> x14, waiting for transfers between devices: none -> 8.87 us  [along_tx(): lax.ppermute(pieces[step], 'tx', [(i, (i + step) % 8) for i in range(8)])]
    all_to_all x4 -> x3, starting transfers between devices: 35.8 us -> 39.8 us  [exchange(): return lax.all_to_all(value, axes, split_axis=0, concat_axis=0, tiled=True)]
    unnamed x16 -> x56, local copies, waits for them, and re-layouts: 0.82 us -> 4.59 us
  transfers between devices with their start and end apart: 4 -> 17, of which waited for: 4 -> 9; matrix products, arithmetic and copies ran while one was open for 2% -> 2% of each run, Pallas kernels for 5% -> 3%
where the time goes in v2:
time: 205 us; the launch traced here: 201 us
  starting transfers between devices  77.8 us (38%)
  blocking collectives  49.1 us (24%)
  waiting for transfers between devices  43.7 us (21%)
  Pallas kernels  21.4 us (10%)
  local copies, waits for them, and re-layouts  5.62 us (3%)
  other arithmetic  2.72 us (1%)
    all_to_all x1, blocking collectives, exchange(): return lax.all_to_all(value, axes, split_axis=0, concat_axis=0, tiled=True)  49.1 us
    all_to_all x3, starting transfers between devices, exchange(): return lax.all_to_all(value, axes, split_axis=0, concat_axis=0, tiled=True)  39.8 us
    ppermute x14, starting transfers between devices, along_tx(): lax.ppermute(pieces[step], 'tx', [(i, (i + step) % 8) for i in range(8)])  38 us
    all_to_all x3, waiting for transfers between devices, exchange(): return lax.all_to_all(value, axes, split_axis=0, concat_axis=0, tiled=True)  34.8 us
    pallas_call x7, Pallas kernels, call(): pl.pallas_call(kernel, out_shape=[jax.ShapeDtypeStruct(s, f32) for s in s...  21.4 us
    ppermute x14, waiting for transfers between devices, along_tx(): lax.ppermute(pieces[step], 'tx', [(i, (i + step) % 8) for i in range(8)])  8.87 us
    unnamed x56, local copies, waits for them, and re-layouts  4.59 us
  transfers between devices with their start and end apart: 17, of which 9 were waited for; matrix products, arithmetic and copies ran while one was open for 2% of the time, Pallas kernels for 3%

profile of v2, /device:TPU:1, one launch (start us, length us, event | category | flops | bytes accessed | tf_op | source)
XLA Modules:
  0.0 201.4 jit_solution(16206792408513815016)
XLA Ops:
  2.5 19.3 %all-to-all-start = ((f32[64,16,128]{2,1,0:T(8,128)}), f32[64,16,128]{2,1,0:T(8,128)S(1)}, u32[]{:S(2)}, u32[]{:S(2)}) async-start(f32[64,16,128]{2,1,0:T(8,128)} %bitcast.12), calls=%async_computation | async-start | bytes 1048576 | tf_op jit(solution)/shard_map/all_to_all | solution.py:324
  24.7 27.1 %all-to-all-done = f32[64,16,128]{2,1,0:T(8,128)S(1)} async-done(((f32[64,16,128]{2,1,0:T(8,128)}), f32[64,16,128]{2,1,0:T(8,128)S(1)}, u32[]{:S(2)}, u32[]{:S(2)}) %all-to-all-start) | async-done | bytes 524320 | tf_op jit(solution)/shard_map/all_to_all | solution.py:324
  52.6 3.4 %shard_map.168 = f32[1024,128]{1,0:T(8,128)} custom-call(f32[16,4,2,8,128]{4,3,2,1,0:T(8,128)} %bitcast.16, f32[2,16,4,8,128]{4,3,2,1,0:T(8,128)} %pad_maximum_fusion.turn, f32[2,16,8,128]{3,2,1,0:T(8,128)} %constant.80.clone.twist, bf16[256,256]{1,0:T(8,128)(2,1)} %constant.81.clone.table_high, bf16[256,256]{1,0:T(8,128)(2,1)} %constant.82.clone.table_low), custom_call_target="tpu_custom_call" | custom-call | flops 1000000000 | bytes 1966080 | tf_op jit(solution)/shard_map/pallas_call | solution.py:309
  56.0 13.7 %all-to-all-start.1 = ((f32[512,2,128]{2,1,0:T(2,128)}), f32[512,2,128]{2,1,0:T(2,128)S(1)}, u32[]{:S(2)}, u32[]{:S(2)}) async-start(f32[512,2,128]{2,1,0:T(2,128)} %bitcast.14), calls=%async_computation.1 | async-start | bytes 1048576 | tf_op jit(solution)/shard_map/all_to_all | solution.py:324
  72.2 2.9 %shard_map.169 = (f32[192,128]{1,0:T(8,128)}, f32[192,128]{1,0:T(8,128)}, f32[192,128]{1,0:T(8,128)}, f32[192,128]{1,0:T(8,128)}, f32[192,128]{1,0:T(8,128)}, /*...) custom-call(s32[1]{0:T(128)} %bitcast.place, f32[2,2,256,128]{3,2,1,0:T(8,128)} %measured.1, ...), custom_call_target="tpu_custom_call" | custom-call | bytes 1441792 | tf_op jit(solution)/shard_map/pallas_call | solution.py:309
  76.7 3.1 %collective-permute-start.1 = (f32[192,128]{1,0:T(8,128)}, f32[192,128]{1,0:T(8,128)S(1)}, u32[]{:S(2)}, u32[]{:S(2)}) collective-permute-start(f32[192,128]{1,0:T(8,128)} %get-tuple-element.21), channel_id=1, source_target_pairs={{0,128},{64,192},{128,256},{192,320},{256,384},{320,448},{384,0},{... | collective-permute-start | bytes 294920 | tf_op jit(solution)/shard_map/ppermute | solution.py:330
  79.8 3.5 %collective-permute-start.2 = (f32[192,128]{1,0:T(8,128)}, f32[192,128]{1,0:T(8,128)S(1)}, u32[]{:S(2)}, u32[]{:S(2)}) collective-permute-start(f32[192,128]{1,0:T(8,128)} %get-tuple-element.22), channel_id=1, source_target_pairs={{0,192},{64,256},{128,320},{192,384},{256,448},{320,0},{384,64},{4... | collective-permute-start | bytes 294920 | tf_op jit(solution)/shard_map/ppermute | solution.py:330
  83.4 5.5 %collective-permute-start.3 = (f32[192,128]{1,0:T(8,128)}, f32[192,128]{1,0:T(8,128)S(1)}, u32[]{:S(2)}, u32[]{:S(2)}) collective-permute-start(f32[192,128]{1,0:T(8,128)} %get-tuple-element.23), channel_id=1, source_target_pairs={{0,256},{64,320},{128,384},{192,448},{256,0},{320,64},{384,128},{4... | collective-permute-start | bytes 294920 | tf_op jit(solution)/shard_map/ppermute | solution.py:330
  88.9 4.5 %collective-permute-start.4 = (f32[192,128]{1,0:T(8,128)}, f32[192,128]{1,0:T(8,128)S(1)}, u32[]{:S(2)}, u32[]{:S(2)}) collective-permute-start(f32[192,128]{1,0:T(8,128)} %get-tuple-element.24), channel_id=1, source_target_pairs={{0,320},{64,384},{128,448},{192,0},{256,64},{320,128},{384,192},{4... | collective-permute-start | bytes 294920 | tf_op jit(solution)/shard_map/ppermute | solution.py:330
  97.1 3.3 %collective-permute-done.5.refs_10_ = f32[192,128]{1,0:T(8,128)S(1)} collective-permute-done((f32[192,128]{1,0:T(8,128)}, f32[192,128]{1,0:T(8,128)S(1)}, u32[]{:S(2)}, u32[]{:S(2)}) %collective-permute-start.5) | collective-permute-done | bytes 98336 | tf_op jit(solution)/shard_map/ppermute | solution.py:330
  100.7 2.4 %all-to-all-done.1 = f32[512,2,128]{2,1,0:T(2,128)S(1)} async-done(((f32[512,2,128]{2,1,0:T(2,128)}), f32[512,2,128]{2,1,0:T(2,128)S(1)}, u32[]{:S(2)}, u32[]{:S(2)}) %all-to-all-start.1) | async-done | bytes 524320 | tf_op jit(solution)/shard_map/all_to_all | solution.py:324
  103.9 5.5 %shard_map.170 = (f32[1024,128]{1,0:T(8,128)}, f32[128,128]{1,0:T(8,128)}, f32[128,128]{1,0:T(8,128)}, f32[128,128]{1,0:T(8,128)}, f32[128,128]{1,0:T(8,128)}, /...) custom-call(s32[1]{0:T(128)} %bitcast.place, f32[1024,128]{1,0:T(8,128)} %bitcast.13, ...), custom_call_target="tpu_custom_call" | custom-call | flops 3000000000 | bytes 5242880 | tf_op jit(solution)/shard_map/pallas_call | solution.py:309
  109.5 49.1 %all_to_all.20 = f32[512,2,128]{2,1,0:T(2,128)} all-to-all(f32[512,2,128]{2,1,0:T(2,128)} %bitcast.17), channel_id=1, replica_groups=mesh['tx'=8,'rx'=16,'freq'=4] {'tx','rx','freq'}, dimensions={0} | all-to-all | bytes 1048576 | tf_op jit(solution)/shard_map/all_to_all | solution.py:324
  158.5 3.2 %shard_map.171 = f32[16,4,2,8,128]{4,3,2,1,0:T(8,128)} custom-call(f32[1024,128]{1,0:T(8,128)} %bitcast.18, f32[2,16,4,8,128]{4,3,2,1,0:T(8,128)} %pad_maximum_fusion.turn, f32[2,16,8,128]{3,2,1,0:T(8,128)} %constant.80.clone.twist, bf16[256,256]{1,0:T(8,128)(2,1)} %constant.81.clone.table_high, bf16[256,256]{1,0:T(8,128)(2,1)} %constant.82.clone.table_low), custom_call_target="tpu_custom_call" | custom-call | flops 1000000000 | bytes 1966080 | tf_op jit(solution)/shard_map/pallas_call | solution.py:309
  161.8 6.8 %all-to-all-start.3 = ((f32[64,16,128]{2,1,0:T(8,128)}), f32[64,16,128]{2,1,0:T(8,128)S(1)}, u32[]{:S(2)}, u32[]{:S(2)}) async-start(f32[64,16,128]{2,1,0:T(8,128)} %bitcast.15), calls=%async_computation.3 | async-start | bytes 1048576 | tf_op jit(solution)/shard_map/all_to_all | solution.py:324
  169.8 2.2 %collective-permute-start.8 = (f32[128,128]{1,0:T(8,128)S(1)}, f32[128,128]{1,0:T(8,128)S(1)}, u32[]{:S(2)}, u32[]{:S(2)}) collective-permute-start(f32[128,128]{1,0:T(8,128)S(1)} %copy-done.25), channel_id=1, source_target_pairs={{0,128},{64,192},{128,256},{192,320},{256,384},{320,448},{384,0},{... | collective-permute-start | bytes 196616 | tf_op jit(solution)/shard_map/ppermute | solution.py:330
  172.0 3.7 %collective-permute-start.9 = (f32[128,128]{1,0:T(8,128)S(1)}, f32[128,128]{1,0:T(8,128)S(1)}, u32[]{:S(2)}, u32[]{:S(2)}) collective-permute-start(f32[128,128]{1,0:T(8,128)S(1)} %copy-done.24), channel_id=1, source_target_pairs={{0,192},{64,256},{128,320},{192,384},{256,448},{320,0},{384,64},{4... | collective-permute-start | bytes 196616 | tf_op jit(solution)/shard_map/ppermute | solution.py:330
  175.7 3.4 %collective-permute-start.10 = (f32[128,128]{1,0:T(8,128)S(1)}, f32[128,128]{1,0:T(8,128)S(1)}, u32[]{:S(2)}, u32[]{:S(2)}) collective-permute-start(f32[128,128]{1,0:T(8,128)S(1)} %copy-done.23), channel_id=1, source_target_pairs={{0,256},{64,320},{128,384},{192,448},{256,0},{320,64},{384,128},{4... | collective-permute-start | bytes 196616 | tf_op jit(solution)/shard_map/ppermute | solution.py:330
  179.1 4.5 %collective-permute-start.11 = (f32[128,128]{1,0:T(8,128)S(1)}, f32[128,128]{1,0:T(8,128)S(1)}, u32[]{:S(2)}, u32[]{:S(2)}) collective-permute-start(f32[128,128]{1,0:T(8,128)S(1)} %copy-done.22), channel_id=1, source_target_pairs={{0,320},{64,384},{128,448},{192,0},{256,64},{320,128},{384,192},{4... | collective-permute-start | bytes 196616 | tf_op jit(solution)/shard_map/ppermute | solution.py:330
  183.7 1.9 collective-permute-start.12
  186.5 3.2 %collective-permute-done.12.refs_6_ = f32[128,128]{1,0:T(8,128)S(1)} collective-permute-done((f32[128,128]{1,0:T(8,128)S(1)}, f32[128,128]{1,0:T(8,128)S(1)}, u32[]{:S(2)}, u32[]{:S(2)}) %collective-permute-start.12) | collective-permute-done | bytes 65568 | tf_op jit(solution)/shard_map/ppermute | solution.py:330
  190.7 2.5 %shard_map.173 = f32[2,2,256,128]{3,2,1,0:T(8,128)} custom-call(s32[1]{0:T(128)} %bitcast.place, f32[128,128]{1,0:T(8,128)} %get-tuple-element.28.refs_0_, f32[128,128]{1,0:T(8,128)} %copy-done.3, f32[128,128]{1,0:T(8,128)} %copy-done.4, f32[128,128]{1,0:T(8,128)} %copy-done.5, f32[128,128]{1,0:T(8,128)} %copy-done.6, f32[128,128]{1,0:T(8,128)} %copy-done.7, ...), custom_call_target="tpu_custom_call" | custom-call | bytes 1048576 | tf_op jit(solution)/shard_map/pallas_call | solution.py:309
  193.2 5.3 %all-to-all-done.3 = f32[64,16,128]{2,1,0:T(8,128)S(1)} async-done(((f32[64,16,128]{2,1,0:T(8,128)}), f32[64,16,128]{2,1,0:T(8,128)S(1)}, u32[]{:S(2)}, u32[]{:S(2)}) %all-to-all-start.3) | async-done | bytes 524320 | tf_op jit(solution)/shard_map/all_to_all | solution.py:324
  199.3 2.1 %shard_map.172 = f32[2,2,256,128]{3,2,1,0:T(8,128)} custom-call(f32[32,2,2,8,128]{4,3,2,1,0:T(8,128)} %bitcast.11, f32[2,2,256,128]{3,2,1,0:T(8,128)} %spectrum.3), custom_call_target="tpu_custom_call" | custom-call | bytes 1572864 | tf_op jit(solution)/shard_map/pallas_call | solution.py:309
  (90 shorter events, 18.2 us)
Async XLA Ops:
  2.5 49.3 %all-to-all-start = ((f32[64,16,128]{2,1,0:T(8,128)}), f32[64,16,128]{2,1,0:T(8,128)S(1)}, u32[]{:S(2)}, u32[]{:S(2)}) async-start(f32[64,16,128]{2,1,0:T(8,128)} %bitcast.12), calls=%async_computation | async-start | bytes 1048576 | tf_op jit(solution)/shard_map/all_to_all | solution.py:324
  56.0 13.7 %copy-start.10 = (s32[16,8]{0,1:T(8,128)S(1)}, s32[16,8]{0,1:T(8,128)}, u32[]{:S(2)}) copy-start(s32[16,8]{0,1:T(8,128)} %param.21) | copy-start | bytes 1540
  56.0 47.1 %all-to-all-start.1 = ((f32[512,2,128]{2,1,0:T(2,128)}), f32[512,2,128]{2,1,0:T(2,128)S(1)}, u32[]{:S(2)}, u32[]{:S(2)}) async-start(f32[512,2,128]{2,1,0:T(2,128)} %bitcast.14), calls=%async_computation.1 | async-start | bytes 1048576 | tf_op jit(solution)/shard_map/all_to_all | solution.py:324
  75.1 18.3 %collective-permute-start = (f32[192,128]{1,0:T(8,128)}, f32[192,128]{1,0:T(8,128)S(1)}, u32[]{:S(2)}, u32[]{:S(2)}) collective-permute-start(f32[192,128]{1,0:T(8,128)} %get-tuple-element.20), channel_id=1, source_target_pairs={{0,64},{64,128},{128,192},{192,256},{256,320},{320,384},{384,448},... | collective-permute-start | bytes 294920 | tf_op jit(solution)/shard_map/ppermute | solution.py:330
  76.7 18.6 %collective-permute-start.1 = (f32[192,128]{1,0:T(8,128)}, f32[192,128]{1,0:T(8,128)S(1)}, u32[]{:S(2)}, u32[]{:S(2)}) collective-permute-start(f32[192,128]{1,0:T(8,128)} %get-tuple-element.21), channel_id=1, source_target_pairs={{0,128},{64,192},{128,256},{192,320},{256,384},{320,448},{384,0},{... | collective-permute-start | bytes 294920 | tf_op jit(solution)/shard_map/ppermute | solution.py:330
  79.8 16.0 %collective-permute-start.2 = (f32[192,128]{1,0:T(8,128)}, f32[192,128]{1,0:T(8,128)S(1)}, u32[]{:S(2)}, u32[]{:S(2)}) collective-permute-start(f32[192,128]{1,0:T(8,128)} %get-tuple-element.22), channel_id=1, source_target_pairs={{0,192},{64,256},{128,320},{192,384},{256,448},{320,0},{384,64},{4... | collective-permute-start | bytes 294920 | tf_op jit(solution)/shard_map/ppermute | solution.py:330
  83.4 12.4 %collective-permute-start.3 = (f32[192,128]{1,0:T(8,128)}, f32[192,128]{1,0:T(8,128)S(1)}, u32[]{:S(2)}, u32[]{:S(2)}) collective-permute-start(f32[192,128]{1,0:T(8,128)} %get-tuple-element.23), channel_id=1, source_target_pairs={{0,256},{64,320},{128,384},{192,448},{256,0},{320,64},{384,128},{4... | collective-permute-start | bytes 294920 | tf_op jit(solution)/shard_map/ppermute | solution.py:330
  88.9 8.2 %collective-permute-start.4 = (f32[192,128]{1,0:T(8,128)}, f32[192,128]{1,0:T(8,128)S(1)}, u32[]{:S(2)}, u32[]{:S(2)}) collective-permute-start(f32[192,128]{1,0:T(8,128)} %get-tuple-element.24), channel_id=1, source_target_pairs={{0,320},{64,384},{128,448},{192,0},{256,64},{320,128},{384,192},{4... | collective-permute-start | bytes 294920 | tf_op jit(solution)/shard_map/ppermute | solution.py:330
  93.4 9.7 %copy-start.13 = (f32[192,128]{1,0:T(8,128)}, f32[192,128]{1,0:T(8,128)S(1)}, u32[]{:S(2)}) copy-start(f32[192,128]{1,0:T(8,128)S(1)} %collective-permute-done.refs_5_) | copy-start | bytes 294916
  93.5 7.0 %collective-permute-start.5 = (f32[192,128]{1,0:T(8,128)}, f32[192,128]{1,0:T(8,128)S(1)}, u32[]{:S(2)}, u32[]{:S(2)}) collective-permute-start(f32[192,128]{1,0:T(8,128)} %get-tuple-element.25), channel_id=1, source_target_pairs={{0,384},{64,448},{128,0},{192,64},{256,128},{320,192},{384,256},{4... | collective-permute-start | bytes 294920 | tf_op jit(solution)/shard_map/ppermute | solution.py:330
  95.4 5.3 %collective-permute-start.6 = (f32[192,128]{1,0:T(8,128)}, f32[192,128]{1,0:T(8,128)S(1)}, u32[]{:S(2)}, u32[]{:S(2)}) collective-permute-start(f32[192,128]{1,0:T(8,128)} %get-tuple-element.26), channel_id=1, source_target_pairs={{0,448},{64,0},{128,64},{192,128},{256,192},{320,256},{384,320},{4... | collective-permute-start | bytes 294920 | tf_op jit(solution)/shard_map/ppermute | solution.py:330
  161.7 10.3 %copy-start.24 = (f32[128,128]{1,0:T(8,128)S(1)}, f32[128,128]{1,0:T(8,128)}, u32[]{:S(2)}) copy-start(f32[128,128]{1,0:T(8,128)} %get-tuple-element.31) | copy-start | bytes 196612
  161.7 14.0 %copy-start.23 = (f32[128,128]{1,0:T(8,128)S(1)}, f32[128,128]{1,0:T(8,128)}, u32[]{:S(2)}) copy-start(f32[128,128]{1,0:T(8,128)} %get-tuple-element.32) | copy-start | bytes 196612
  161.7 17.4 %copy-start.22 = (f32[128,128]{1,0:T(8,128)S(1)}, f32[128,128]{1,0:T(8,128)}, u32[]{:S(2)}) copy-start(f32[128,128]{1,0:T(8,128)} %get-tuple-element.33) | copy-start | bytes 196612
  161.7 22.0 %copy-start.21 = (f32[128,128]{1,0:T(8,128)S(1)}, f32[128,128]{1,0:T(8,128)}, u32[]{:S(2)}) copy-start(f32[128,128]{1,0:T(8,128)} %get-tuple-element.34) | copy-start | bytes 196612
  161.8 23.9 %copy-start.20 = (f32[128,128]{1,0:T(8,128)S(1)}, f32[128,128]{1,0:T(8,128)}, u32[]{:S(2)}) copy-start(f32[128,128]{1,0:T(8,128)} %get-tuple-element.35) | copy-start | bytes 196612
  161.8 36.7 %all-to-all-start.3 = ((f32[64,16,128]{2,1,0:T(8,128)}), f32[64,16,128]{2,1,0:T(8,128)S(1)}, u32[]{:S(2)}, u32[]{:S(2)}) async-start(f32[64,16,128]{2,1,0:T(8,128)} %bitcast.15), calls=%async_computation.3 | async-start | bytes 1048576 | tf_op jit(solution)/shard_map/all_to_all | solution.py:324
  168.6 15.1 %collective-permute-start.7 = (f32[128,128]{1,0:T(8,128)S(1)}, f32[128,128]{1,0:T(8,128)S(1)}, u32[]{:S(2)}, u32[]{:S(2)}) collective-permute-start(f32[128,128]{1,0:T(8,128)S(1)} %copy-done.26), channel_id=1, source_target_pairs={{0,64},{64,128},{128,192},{192,256},{256,320},{320,384},{384,448},... | collective-permute-start | bytes 196616 | tf_op jit(solution)/shard_map/ppermute | solution.py:330
  169.8 15.8 %collective-permute-start.8 = (f32[128,128]{1,0:T(8,128)S(1)}, f32[128,128]{1,0:T(8,128)S(1)}, u32[]{:S(2)}, u32[]{:S(2)}) collective-permute-start(f32[128,128]{1,0:T(8,128)S(1)} %copy-done.25), channel_id=1, source_target_pairs={{0,128},{64,192},{128,256},{192,320},{256,384},{320,448},{384,0},{... | collective-permute-start | bytes 196616 | tf_op jit(solution)/shard_map/ppermute | solution.py:330
  172.0 14.1 %collective-permute-start.9 = (f32[128,128]{1,0:T(8,128)S(1)}, f32[128,128]{1,0:T(8,128)S(1)}, u32[]{:S(2)}, u32[]{:S(2)}) collective-permute-start(f32[128,128]{1,0:T(8,128)S(1)} %copy-done.24), channel_id=1, source_target_pairs={{0,192},{64,256},{128,320},{192,384},{256,448},{320,0},{384,64},{4... | collective-permute-start | bytes 196616 | tf_op jit(solution)/shard_map/ppermute | solution.py:330
  175.7 10.4 %collective-permute-start.10 = (f32[128,128]{1,0:T(8,128)S(1)}, f32[128,128]{1,0:T(8,128)S(1)}, u32[]{:S(2)}, u32[]{:S(2)}) collective-permute-start(f32[128,128]{1,0:T(8,128)S(1)} %copy-done.23), channel_id=1, source_target_pairs={{0,256},{64,320},{128,384},{192,448},{256,0},{320,64},{384,128},{4... | collective-permute-start | bytes 196616 | tf_op jit(solution)/shard_map/ppermute | solution.py:330
  179.1 7.4 %collective-permute-start.11 = (f32[128,128]{1,0:T(8,128)S(1)}, f32[128,128]{1,0:T(8,128)S(1)}, u32[]{:S(2)}, u32[]{:S(2)}) collective-permute-start(f32[128,128]{1,0:T(8,128)S(1)} %copy-done.22), channel_id=1, source_target_pairs={{0,320},{64,384},{128,448},{192,0},{256,64},{320,128},{384,192},{4... | collective-permute-start | bytes 196616 | tf_op jit(solution)/shard_map/ppermute | solution.py:330
  183.7 6.0 %collective-permute-start.12 = (f32[128,128]{1,0:T(8,128)S(1)}, f32[128,128]{1,0:T(8,128)S(1)}, u32[]{:S(2)}, u32[]{:S(2)}) collective-permute-start(f32[128,128]{1,0:T(8,128)S(1)} %copy-done.21), channel_id=1, source_target_pairs={{0,384},{64,448},{128,0},{192,64},{256,128},{320,192},{384,256},{4... | collective-permute-start | bytes 196616 | tf_op jit(solution)/shard_map/ppermute | solution.py:330
  185.7 4.5 %collective-permute-start.13 = (f32[128,128]{1,0:T(8,128)S(1)}, f32[128,128]{1,0:T(8,128)S(1)}, u32[]{:S(2)}, u32[]{:S(2)}) collective-permute-start(f32[128,128]{1,0:T(8,128)S(1)} %copy-done.20), channel_id=1, source_target_pairs={{0,448},{64,0},{128,64},{192,128},{256,192},{320,256},{384,320},{4... | collective-permute-start | bytes 196616 | tf_op jit(solution)/shard_map/ppermute | solution.py:330
  (21 other events, 76.7 us)

commit v3 on v2

--- a/solution.py
+++ b/solution.py
@@ -13,10 +13,12 @@
 depth_step = 2.0
 step_size = 0.125
 root_floor = 0.25
+early_echoes = 3
+early_pieces = 5
 bf16 = jnp.bfloat16
 f32 = jnp.float32
 nt_form = (((1,), (1,)), ((), ()))
-params = pltpu.CompilerParams(vmem_limit_bytes=56 * 1024 * 1024)
+params = pltpu.CompilerParams(vmem_limit_bytes=24 * 1024 * 1024)
 
 
 def halves(table):
@@ -147,14 +149,21 @@
         out[c, 1] = spectrum[c, 1] + step_size * second
 
 
-def pack_kernel(place, measured, weights, *refs):
+def pack_kernel(place, measured, send, hear, gate, *refs):
     *outs, held = refs
+    tile = lax.broadcasted_iota(jnp.int32, (256, 16), 0) // 16
+    down = (tile == lax.broadcasted_iota(jnp.int32, (256, 16), 1)).astype(bf16)
+    tile = lax.broadcasted_iota(jnp.int32, (8, 128), 1) // 16
+    along = (tile == lax.broadcasted_iota(jnp.int32, (8, 128), 0)).astype(bf16)
+    live = dot(dot(down, gate[...].astype(f32).astype(bf16)).astype(bf16), along)
+    columns = [jnp.broadcast_to(send[k : k + 1, :], (128, 128)).T for k in range(2)]
+    weights = jnp.concatenate(columns, 0) * hear[...] * live
     for k in range(3):
         pieces = []
         for q in range(4):
             for f0 in range(2):
-                rows = pl.ds(q * 64, 64)
-                pieces.append(measured[k, f0, rows, :] if k < 2 else weights[rows, :])
+                rows = slice(q * 64, (q + 1) * 64)
+                pieces.append(measured[k, f0, rows, :] if k < 2 else weights[rows])
         for d, piece in enumerate(swap_groups(pieces, 16)):
             held[d, k * 64 : (k + 1) * 64, :] = piece
     for step in range(8):
@@ -171,7 +180,8 @@
             out[k, g % 2, pl.ds(g // 2 * 64, 64), :] = piece
 
 
-def pair_kernel(arrived, turn, twist, table_high, table_low, out):
+def pair_kernel(arrived, turn, twist, table_high, table_low, *refs):
+    out = refs[-1]
     low = lax.broadcasted_iota(jnp.int32, (8, 128), 0) < 4
     for y in range(4):
         points = []
@@ -206,7 +216,8 @@
             out[pl.ds(y * 2 + c, 128, stride=8), :] = done[c * 128 : (c + 1) * 128]
 
 
-def gradient_kernel(arrived, turn, twist, table_high, table_low, out, points):
+def gradient_kernel(arrived, turn, twist, table_high, table_low, *refs):
+    out, points = refs[-2:]
     for y in range(4):
         re = arrived[pl.ds(y * 2, 128, stride=8), :]
         im = arrived[pl.ds(y * 2 + 1, 128, stride=8), :]
@@ -257,19 +268,18 @@
     return sums
 
 
-def middle_kernel(place, arrived, twist, mix, mix_back, *refs):
-    long, echoes, out, sent = refs[:4], refs[4:12], refs[12], refs[13:21]
-    held, resid = refs[21:]
+def middle_kernel(place, arrived, *refs):
+    echoes, given, out, sent = refs[:8], refs[8:15], refs[15], refs[16:24]
+    held, resid, arrival = refs[24], refs[25], refs[33]
+    copies = [
+        pltpu.make_async_copy(source, target, arrival.at[k])
+        for k, (source, target) in enumerate(zip(given, refs[26:33]))
+    ]
+    for copy in copies:
+        copy.start()
+    long, twist, mix, mix_back = refs[26:30], refs[30], refs[31], refs[32]
     for step in range(8):
         held[(place[0] + 8 - step) & 7] = echoes[step][...]
-    cos_re, cos_im, sin_re, sin_im = long_sums(
-        arrived[pl.ds(0, 512, stride=2), :], arrived[pl.ds(1, 512, stride=2), :], long
-    )
-    re, im = cos_re - sin_im, sin_re + cos_im
-    tr, ti = twist[0], twist[1]
-    both = jnp.concatenate([re * tr - im * ti, re * ti + im * tr], 1)
-    high, rest = split(both)
-    field = dot(high, mix[...]) + dot(rest, mix[...])
     parts = []
     for k in range(3):
         rows = []
@@ -277,6 +287,16 @@
             pieces = [held[2 * t1 + odd, k * 64 : (k + 1) * 64, :] for t1 in range(4)]
             rows += swap_groups(pieces, 32)
         parts.append(jnp.concatenate(rows, 0))
+    for copy in copies:
+        copy.wait()
+    cos_re, cos_im, sin_re, sin_im = long_sums(
+        arrived[pl.ds(0, 512, stride=2), :], arrived[pl.ds(1, 512, stride=2), :], long
+    )
+    re, im = cos_re - sin_im, sin_re + cos_im
+    tr, ti = twist[0], twist[1]
+    both = jnp.concatenate([re * tr - im * ti, re * ti + im * tr], 1)
+    high, rest = split(both)
+    field = dot(high, mix[...]) + dot(rest, mix[...])
     left = []
     for k in range(2):
         value = parts[2] * (parts[k] - field[:, k * 128 : (k + 1) * 128])
@@ -295,27 +315,28 @@
     out[pl.ds(1, 512, stride=2), :] = cos_im - sin_re
 
 
-def call(kernel, shapes, *operands, scratch=(), place=None, flops=0):
-    single = not isinstance(shapes, list)
-    shapes = [shapes] if single else shapes
+def call(kernel, outs, *operands, near=0, apart=0, far=False, scratch=(), place=None, flops=0):
+    single = not isinstance(outs, list)
+    outs = [outs] if single else outs
+    outs = [jax.ShapeDtypeStruct(o, f32) for o in outs]
+    moved = sum(math.prod(o.shape) * o.dtype.itemsize for o in [*outs, *operands])
     spec = pl.BlockSpec(memory_space=pltpu.VMEM)
-    in_specs = [spec] * len(operands)
-    bytes_moved = sum(math.prod(s) * 4 for s in shapes) + sum(
-        o.size * o.dtype.itemsize for o in operands
-    )
+    in_specs = [spec] * (len(operands) - apart) + [pl.BlockSpec(memory_space=pl.ANY)] * apart
+    operands = [
+        pltpu.with_memory_space_constraint(o, pltpu.VMEM) if k < near else o
+        for k, o in enumerate(operands)
+    ]
     if place is not None:
-        operands = (place, *operands)
+        operands = [place, *operands]
         in_specs = [pl.BlockSpec(memory_space=pltpu.SMEM), *in_specs]
     out = pl.pallas_call(
         kernel,
-        out_shape=[jax.ShapeDtypeStruct(s, f32) for s in shapes],
+        out_shape=outs if far else [pltpu.VMEM(o.shape, o.dtype) for o in outs],
         in_specs=in_specs,
-        out_specs=[spec] * len(shapes),
-        scratch_shapes=[pltpu.VMEM(s, f32) for s in scratch],
+        out_specs=[spec] * len(outs),
+        scratch_shapes=[pltpu.VMEM(s, f32) if isinstance(s, tuple) else s for s in scratch],
         compiler_params=params,
-        cost_estimate=pl.CostEstimate(
-            flops=flops, bytes_accessed=bytes_moved, transcendentals=0
-        ),
+        cost_estimate=pl.CostEstimate(flops=flops, bytes_accessed=moved, transcendentals=0),
     )(*operands)
     return out[0] if single else out
 
@@ -358,24 +379,19 @@
     arrived = exchange(sent.reshape(64, 16, 128), ("rx", "freq"))
 
     turn = turns(wavenumber, tx, z, y)
-    gate = aperture.astype(f32)
-    weights = (
-        send_weight.reshape(16, 16, 1, 1)
-        * gate.reshape(16, 1, 8, 1)
-        * hear_weight.reshape(1, 1, 8, 16)
-    ).reshape(256, 128)
     place = tx.astype(jnp.int32).reshape(1)
-    echoes = along_tx(
-        call(
-            pack_kernel,
-            [(192, 128)] * 8,
-            measured,
-            weights,
-            scratch=[(8, 192, 128)],
-            place=place,
-        )
-    )
-
+    packed = call(
+        pack_kernel,
+        [(192, 128)] * 8,
+        measured,
+        send_weight.reshape(2, 128),
+        hear_weight.reshape(1, 128),
+        aperture,
+        scratch=[(8, 192, 128)],
+        place=place,
+    )
+    echoes = along_tx(packed)
+    early = echoes[:early_echoes]
     pairs = call(
         pair_kernel,
         (1024, 128),
@@ -383,30 +399,40 @@
         turn,
         table["twist_heard"],
         *table["lanes"],
+        *early,
+        near=5,
+        apart=len(early),
         flops=10**9,
     )
     columns = exchange(pairs.reshape(512, 2, 128), ("tx", "rx", "freq")).reshape(1024, 128)
+    given = [*table["long"], table["twist_sent"], table["mix"], table["mix_back"]]
+    given = [pltpu.with_memory_space_constraint(jnp.asarray(t), pltpu.HBM) for t in given]
     back, *resid = call(
         middle_kernel,
         [(1024, 128)] + [(128, 128)] * 8,
         columns,
-        table["twist_sent"],
-        table["mix"],
-        table["mix_back"],
-        *table["long"],
         *echoes,
-        scratch=[(8, 192, 128), (8, 128, 128)],
+        *given,
+        near=9,
+        apart=7,
+        scratch=[(8, 192, 128), (8, 128, 128)]
+        + [pltpu.VMEM(t.shape, t.dtype) for t in given]
+        + [pltpu.SemaphoreType.DMA((7,))],
         place=place,
         flops=3 * 10**9,
     )
     rows = exchange(back.reshape(512, 2, 128), ("tx", "rx", "freq")).reshape(1024, 128)
+    pieces = along_tx(resid)
     residual = call(
         unpack_kernel,
         (2, 2, 256, 128),
-        *along_tx(resid),
+        *pieces,
+        near=8,
+        far=True,
         scratch=[(8, 128, 128)],
         place=place,
     )
+    early = pieces[:early_pieces]
     gradient = call(
         gradient_kernel,
         (16, 4, 2, 8, 128),
@@ -414,12 +440,20 @@
         turn,
         table["twist_heard"],
         *table["lanes"],
+        *early,
+        near=5,
+        apart=len(early),
         scratch=[(4, 16, 2, 8, 128)],
         flops=10**9,
     )
     gathered = exchange(gradient.reshape(64, 16, 128), ("rx", "freq"))
     updated = call(
-        update_kernel, (2, 2, 256, 128), gathered.reshape(32, 2, 2, 8, 128), spectrum
+        update_kernel,
+        (2, 2, 256, 128),
+        gathered.reshape(32, 2, 2, 8, 128),
+        spectrum,
+        near=2,
+        far=True,
     )
     return updated, residual
 

time: 205 us -> 194 us (0.946)
  blocking collectives: 49.1 us -> 0 us
  waiting for transfers between devices: 43.7 us -> 79.8 us
  starting transfers between devices: 77.8 us -> 92.5 us
  Pallas kernels: 21.4 us -> 13.6 us
  local copies, waits for them, and re-layouts: 5.62 us -> 3.39 us
    all_to_all x1 -> x0, blocking collectives: 49.1 us -> none  [exchange(): return lax.all_to_all(value, axes, split_axis=0, concat_axis=0, tiled=True)]
    all_to_all x3 -> x4, waiting for transfers between devices: 34.8 us -> 66 us  [exchange(): return lax.all_to_all(value, axes, split_axis=0, concat_axis=0, tiled=True)]
    all_to_all x3 -> x4, starting transfers between devices: 39.8 us -> 50.9 us  [exchange(): return lax.all_to_all(value, axes, split_axis=0, concat_axis=0, tiled=True)]
    pallas_call x7, Pallas kernels: 21.4 us -> 13.6 us  [call(): pl.pallas_call(kernel, out_shape=outs if far else [pltpu.VMEM(o.shape, o....]
    ppermute x14, waiting for transfers between devices: 8.87 us -> 13.8 us  [along_tx(): lax.ppermute(pieces[step], 'tx', [(i, (i + step) % 8) for i in range(8)])]
    ppermute x14, starting transfers between devices: 38 us -> 41.7 us  [along_tx(): lax.ppermute(pieces[step], 'tx', [(i, (i + step) % 8) for i in range(8)])]
    unnamed x56 -> x21, local copies, waits for them, and re-layouts: 4.59 us -> 3.14 us
  transfers between devices with their start and end apart: 17 -> 18, of which waited for: 9 -> 12; matrix products, arithmetic and copies ran while one was open for 2% -> 1% of each run, Pallas kernels for 3% -> 1%
where the time goes in v3:
time: 194 us; the launch traced here: 191 us
  starting transfers between devices  92.5 us (48%)
  waiting for transfers between devices  79.8 us (41%)
  Pallas kernels  13.6 us (7%)
  local copies, waits for them, and re-layouts  3.39 us (2%)
    all_to_all x4, waiting for transfers between devices, exchange(): return lax.all_to_all(value, axes, split_axis=0, concat_axis=0, tiled=True)  66 us
    all_to_all x4, starting transfers between devices, exchange(): return lax.all_to_all(value, axes, split_axis=0, concat_axis=0, tiled=True)  50.9 us
    ppermute x14, starting transfers between devices, along_tx(): lax.ppermute(pieces[step], 'tx', [(i, (i + step) % 8) for i in range(8)])  41.7 us
    ppermute x14, waiting for transfers between devices, along_tx(): lax.ppermute(pieces[step], 'tx', [(i, (i + step) % 8) for i in range(8)])  13.8 us
    pallas_call x7, Pallas kernels, call(): pl.pallas_call(kernel, out_shape=outs if far else [pltpu.VMEM(o.shape, o....  13.6 us
  transfers between devices with their start and end apart: 18, of which 12 were waited for; matrix products, arithmetic and copies ran while one was open for 1% of the time, Pallas kernels for 1%

profile of v3, /device:TPU:1, one launch (start us, length us, event | category | flops | bytes accessed | tf_op | source)
XLA Modules:
  0.0 191.4 jit_solution(4618606835210122698)
XLA Ops:
  2.5 19.4 %all-to-all-start = ((f32[64,16,128]{2,1,0:T(8,128)}), f32[64,16,128]{2,1,0:T(8,128)S(1)}, u32[]{:S(2)}, u32[]{:S(2)}) async-start(f32[64,16,128]{2,1,0:T(8,128)} %bitcast.1), calls=%async_computation | async-start | bytes 1048576 | tf_op jit(solution)/shard_map/all_to_all | solution.py:345
  24.3 2.1 %collective-permute-start = (f32[192,128]{1,0:T(8,128)S(1)}, f32[192,128]{1,0:T(8,128)S(1)}, u32[]{:S(2)}, u32[]{:S(2)}) collective-permute-start(f32[192,128]{1,0:T(8,128)S(1)} %get-tuple-element.20), channel_id=1, source_target_pairs={{0,64},{64,128},{128,192},{192,256},{256,320},{320,384},{384,448},... | collective-permute-start | bytes 294920 | tf_op jit(solution)/shard_map/ppermute | solution.py:351
  26.4 3.1 %collective-permute-start.1 = (f32[192,128]{1,0:T(8,128)S(1)}, f32[192,128]{1,0:T(8,128)S(1)}, u32[]{:S(2)}, u32[]{:S(2)}) collective-permute-start(f32[192,128]{1,0:T(8,128)S(1)} %get-tuple-element.21), channel_id=1, source_target_pairs={{0,128},{64,192},{128,256},{192,320},{256,384},{320,448},{384,0},{... | collective-permute-start | bytes 294920 | tf_op jit(solution)/shard_map/ppermute | solution.py:351
  31.7 2.1 %collective-permute-done.1.refs_2_ = f32[192,128]{1,0:T(8,128)S(1)} collective-permute-done((f32[192,128]{1,0:T(8,128)S(1)}, f32[192,128]{1,0:T(8,128)S(1)}, u32[]{:S(2)}, u32[]{:S(2)}) %collective-permute-start.1) | collective-permute-done | bytes 98336 | tf_op jit(solution)/shard_map/ppermute | solution.py:351
  33.7 18.3 %all-to-all-done = f32[64,16,128]{2,1,0:T(8,128)S(1)} async-done(((f32[64,16,128]{2,1,0:T(8,128)}), f32[64,16,128]{2,1,0:T(8,128)S(1)}, u32[]{:S(2)}, u32[]{:S(2)}) %all-to-all-start) | async-done | bytes 524320 | tf_op jit(solution)/shard_map/all_to_all | solution.py:345
  52.0 2.1 %shard_map.169 = f32[1024,128]{1,0:T(8,128)} custom-call(f32[16,4,2,8,128]{4,3,2,1,0:T(8,128)S(1)} %bitcast.12, f32[2,16,4,8,128]{4,3,2,1,0:T(8,128)S(1)} %pad_maximum_fusion.turn, f32[2,16,8,128]{3,2,1,0:T(8,128)S(1)} %copy-done.7, bf16[256,256]{1,0:T(8,128)(2,1)S(1)} %copy-done.6, bf16[256,256]{1,0:T(8,128)(2,1)S(1)} %copy-done.5, ...), custom_call_target="tpu_custom_call" | custom-call | flops 1000000000 | bytes 2260992 | tf_op jit(solution)/shard_map/pallas_call | solution.py:332
  54.1 13.7 %all-to-all-start.1 = ((f32[512,2,128]{2,1,0:T(2,128)}), f32[512,2,128]{2,1,0:T(2,128)S(1)}, u32[]{:S(2)}, u32[]{:S(2)}) async-start(f32[512,2,128]{2,1,0:T(2,128)} %bitcast.5), calls=%async_computation.1 | async-start | bytes 1048576 | tf_op jit(solution)/shard_map/all_to_all | solution.py:345
  67.7 5.0 %collective-permute-start.2 = (f32[192,128]{1,0:T(8,128)S(1)}, f32[192,128]{1,0:T(8,128)S(1)}, u32[]{:S(2)}, u32[]{:S(2)}) collective-permute-start(f32[192,128]{1,0:T(8,128)S(1)} %get-tuple-element.22), channel_id=1, source_target_pairs={{0,192},{64,256},{128,320},{192,384},{256,448},{320,0},{384,64},{4... | collective-permute-start | bytes 294920 | tf_op jit(solution)/shard_map/ppermute | solution.py:351
  72.8 5.9 %collective-permute-start.3 = (f32[192,128]{1,0:T(8,128)S(1)}, f32[192,128]{1,0:T(8,128)S(1)}, u32[]{:S(2)}, u32[]{:S(2)}) collective-permute-start(f32[192,128]{1,0:T(8,128)S(1)} %get-tuple-element.23), channel_id=1, source_target_pairs={{0,256},{64,320},{128,384},{192,448},{256,0},{320,64},{384,128},{4... | collective-permute-start | bytes 294920 | tf_op jit(solution)/shard_map/ppermute | solution.py:351
  80.6 2.5 %collective-permute-start.5 = (f32[192,128]{1,0:T(8,128)S(1)}, f32[192,128]{1,0:T(8,128)S(1)}, u32[]{:S(2)}, u32[]{:S(2)}) collective-permute-start(f32[192,128]{1,0:T(8,128)S(1)} %get-tuple-element.25), channel_id=1, source_target_pairs={{0,384},{64,448},{128,0},{192,64},{256,128},{320,192},{384,256},{4... | collective-permute-start | bytes 294920 | tf_op jit(solution)/shard_map/ppermute | solution.py:351
  83.2 3.6 %collective-permute-done.4.refs_5_ = f32[192,128]{1,0:T(8,128)S(1)} collective-permute-done((f32[192,128]{1,0:T(8,128)S(1)}, f32[192,128]{1,0:T(8,128)S(1)}, u32[]{:S(2)}, u32[]{:S(2)}) %collective-permute-start.4) | collective-permute-done | bytes 98336 | tf_op jit(solution)/shard_map/ppermute | solution.py:351
  87.1 2.2 %collective-permute-done.6.refs_7_ = f32[192,128]{1,0:T(8,128)S(1)} collective-permute-done((f32[192,128]{1,0:T(8,128)S(1)}, f32[192,128]{1,0:T(8,128)S(1)}, u32[]{:S(2)}, u32[]{:S(2)}) %collective-permute-start.6) | collective-permute-done | bytes 98336 | tf_op jit(solution)/shard_map/ppermute | solution.py:351
  89.3 11.8 %all-to-all-done.1 = f32[512,2,128]{2,1,0:T(2,128)S(1)} async-done(((f32[512,2,128]{2,1,0:T(2,128)}), f32[512,2,128]{2,1,0:T(2,128)S(1)}, u32[]{:S(2)}, u32[]{:S(2)}) %all-to-all-start.1) | async-done | bytes 524320 | tf_op jit(solution)/shard_map/all_to_all | solution.py:345
  101.2 5.5 %shard_map.170 = (f32[1024,128]{1,0:T(8,128)}, f32[128,128]{1,0:T(8,128)S(1)}, f32[128,128]{1,0:T(8,128)S(1)}, f32[128,128]{1,0:T(8,128)S(1)}, f32[128,128]{1,0:...) custom-call(s32[1]{0:T(128)} %bitcast.place, ...), custom_call_target="tpu_custom_call" | custom-call | flops 3000000000 | bytes 5242880 | tf_op jit(solution)/shard_map/pallas_call | solution.py:332
  106.7 11.0 %all-to-all-start.2 = ((f32[512,2,128]{2,1,0:T(2,128)}), f32[512,2,128]{2,1,0:T(2,128)S(1)}, u32[]{:S(2)}, u32[]{:S(2)}) async-start(f32[512,2,128]{2,1,0:T(2,128)} %bitcast.7), calls=%async_computation.2 | async-start | bytes 1048576 | tf_op jit(solution)/shard_map/all_to_all | solution.py:345
  119.4 3.1 %collective-permute-start.8 = (f32[128,128]{1,0:T(8,128)S(1)}, f32[128,128]{1,0:T(8,128)S(1)}, u32[]{:S(2)}, u32[]{:S(2)}) collective-permute-start(f32[128,128]{1,0:T(8,128)S(1)} %get-tuple-element.30), channel_id=1, source_target_pairs={{0,128},{64,192},{128,256},{192,320},{256,384},{320,448},{384,0},{... | collective-permute-start | bytes 196616 | tf_op jit(solution)/shard_map/ppermute | solution.py:351
  122.5 3.6 %collective-permute-start.9 = (f32[128,128]{1,0:T(8,128)S(1)}, f32[128,128]{1,0:T(8,128)S(1)}, u32[]{:S(2)}, u32[]{:S(2)}) collective-permute-start(f32[128,128]{1,0:T(8,128)S(1)} %get-tuple-element.31), channel_id=1, source_target_pairs={{0,192},{64,256},{128,320},{192,384},{256,448},{320,0},{384,64},{4... | collective-permute-start | bytes 196616 | tf_op jit(solution)/shard_map/ppermute | solution.py:351
  126.1 5.6 %collective-permute-start.10 = (f32[128,128]{1,0:T(8,128)S(1)}, f32[128,128]{1,0:T(8,128)S(1)}, u32[]{:S(2)}, u32[]{:S(2)}) collective-permute-start(f32[128,128]{1,0:T(8,128)S(1)} %get-tuple-element.32), channel_id=1, source_target_pairs={{0,256},{64,320},{128,384},{192,448},{256,0},{320,64},{384,128},{4... | collective-permute-start | bytes 196616 | tf_op jit(solution)/shard_map/ppermute | solution.py:351
  132.3 2.1 %collective-permute-done.10.refs_4_ = f32[128,128]{1,0:T(8,128)S(1)} collective-permute-done((f32[128,128]{1,0:T(8,128)S(1)}, f32[128,128]{1,0:T(8,128)S(1)}, u32[]{:S(2)}, u32[]{:S(2)}) %collective-permute-start.10) | collective-permute-done | bytes 65568 | tf_op jit(solution)/shard_map/ppermute | solution.py:351
  134.3 17.1 %all-to-all-done.2 = f32[512,2,128]{2,1,0:T(2,128)S(1)} async-done(((f32[512,2,128]{2,1,0:T(2,128)}), f32[512,2,128]{2,1,0:T(2,128)S(1)}, u32[]{:S(2)}, u32[]{:S(2)}) %all-to-all-start.2) | async-done | bytes 524320 | tf_op jit(solution)/shard_map/all_to_all | solution.py:345
  153.2 6.8 %all-to-all-start.3 = ((f32[64,16,128]{2,1,0:T(8,128)}), f32[64,16,128]{2,1,0:T(8,128)S(1)}, u32[]{:S(2)}, u32[]{:S(2)}) async-start(f32[64,16,128]{2,1,0:T(8,128)} %bitcast.9), calls=%async_computation.3 | async-start | bytes 1048576 | tf_op jit(solution)/shard_map/all_to_all | solution.py:345
  160.0 3.5 %collective-permute-start.11 = (f32[128,128]{1,0:T(8,128)S(1)}, f32[128,128]{1,0:T(8,128)S(1)}, u32[]{:S(2)}, u32[]{:S(2)}) collective-permute-start(f32[128,128]{1,0:T(8,128)S(1)} %get-tuple-element.33), channel_id=1, source_target_pairs={{0,320},{64,384},{128,448},{192,0},{256,64},{320,128},{384,192},{4... | collective-permute-start | bytes 196616 | tf_op jit(solution)/shard_map/ppermute | solution.py:351
  163.5 2.4 %collective-permute-start.12 = (f32[128,128]{1,0:T(8,128)S(1)}, f32[128,128]{1,0:T(8,128)S(1)}, u32[]{:S(2)}, u32[]{:S(2)}) collective-permute-start(f32[128,128]{1,0:T(8,128)S(1)} %get-tuple-element.34), channel_id=1, source_target_pairs={{0,384},{64,448},{128,0},{192,64},{256,128},{320,192},{384,256},{4... | collective-permute-start | bytes 196616 | tf_op jit(solution)/shard_map/ppermute | solution.py:351
  171.6 18.9 %all-to-all-done.3 = f32[64,16,128]{2,1,0:T(8,128)S(1)} async-done(((f32[64,16,128]{2,1,0:T(8,128)}), f32[64,16,128]{2,1,0:T(8,128)S(1)}, u32[]{:S(2)}, u32[]{:S(2)}) %all-to-all-start.3) | async-done | bytes 524320 | tf_op jit(solution)/shard_map/all_to_all | solution.py:345
  (49 shorter events, 19.3 us)
Async XLA Ops:
  0.6 1.0 copy-start
  2.5 20.2 %copy-start.2 = (f32[2,2,256,128]{3,2,1,0:T(8,128)S(1)}, f32[2,2,256,128]{3,2,1,0:T(8,128)}, u32[]{:S(2)}) copy-start(f32[2,2,256,128]{3,2,1,0:T(8,128)} %measured.1) | copy-start | bytes 1572868
  2.5 49.4 %all-to-all-start = ((f32[64,16,128]{2,1,0:T(8,128)}), f32[64,16,128]{2,1,0:T(8,128)S(1)}, u32[]{:S(2)}, u32[]{:S(2)}) async-start(f32[64,16,128]{2,1,0:T(8,128)} %bitcast.1), calls=%async_computation | async-start | bytes 1048576 | tf_op jit(solution)/shard_map/all_to_all | solution.py:345
  24.3 7.3 %collective-permute-start = (f32[192,128]{1,0:T(8,128)S(1)}, f32[192,128]{1,0:T(8,128)S(1)}, u32[]{:S(2)}, u32[]{:S(2)}) collective-permute-start(f32[192,128]{1,0:T(8,128)S(1)} %get-tuple-element.20), channel_id=1, source_target_pairs={{0,64},{64,128},{128,192},{192,256},{256,320},{320,384},{384,448},... | collective-permute-start | bytes 294920 | tf_op jit(solution)/shard_map/ppermute | solution.py:351
  26.4 7.3 %collective-permute-start.1 = (f32[192,128]{1,0:T(8,128)S(1)}, f32[192,128]{1,0:T(8,128)S(1)}, u32[]{:S(2)}, u32[]{:S(2)}) collective-permute-start(f32[192,128]{1,0:T(8,128)S(1)} %get-tuple-element.21), channel_id=1, source_target_pairs={{0,128},{64,192},{128,256},{192,320},{256,384},{320,448},{384,0},{... | collective-permute-start | bytes 294920 | tf_op jit(solution)/shard_map/ppermute | solution.py:351
  31.6 20.4 %copy-start.5 = (bf16[256,256]{1,0:T(8,128)(2,1)S(1)}, bf16[256,256]{1,0:T(8,128)(2,1)}, u32[]{:S(2)}) copy-start(bf16[256,256]{1,0:T(8,128)(2,1)} %constant.82.clone.table_low) | copy-start | bytes 393220
  31.6 20.4 %copy-start.6 = (bf16[256,256]{1,0:T(8,128)(2,1)S(1)}, bf16[256,256]{1,0:T(8,128)(2,1)}, u32[]{:S(2)}) copy-start(bf16[256,256]{1,0:T(8,128)(2,1)} %constant.81.clone.table_high) | copy-start | bytes 393220
  31.6 20.4 %copy-start.7 = (f32[2,16,8,128]{3,2,1,0:T(8,128)S(1)}, f32[2,16,8,128]{3,2,1,0:T(8,128)}, u32[]{:S(2)}) copy-start(f32[2,16,8,128]{3,2,1,0:T(8,128)} %constant.80.clone.twist) | copy-start | bytes 393220
  54.1 47.1 %all-to-all-start.1 = ((f32[512,2,128]{2,1,0:T(2,128)}), f32[512,2,128]{2,1,0:T(2,128)S(1)}, u32[]{:S(2)}, u32[]{:S(2)}) async-start(f32[512,2,128]{2,1,0:T(2,128)} %bitcast.5), calls=%async_computation.1 | async-start | bytes 1048576 | tf_op jit(solution)/shard_map/all_to_all | solution.py:345
  67.7 15.4 %collective-permute-start.2 = (f32[192,128]{1,0:T(8,128)S(1)}, f32[192,128]{1,0:T(8,128)S(1)}, u32[]{:S(2)}, u32[]{:S(2)}) collective-permute-start(f32[192,128]{1,0:T(8,128)S(1)} %get-tuple-element.22), channel_id=1, source_target_pairs={{0,192},{64,256},{128,320},{192,384},{256,448},{320,0},{384,64},{4... | collective-permute-start | bytes 294920 | tf_op jit(solution)/shard_map/ppermute | solution.py:351
  72.8 10.4 %collective-permute-start.3 = (f32[192,128]{1,0:T(8,128)S(1)}, f32[192,128]{1,0:T(8,128)S(1)}, u32[]{:S(2)}, u32[]{:S(2)}) collective-permute-start(f32[192,128]{1,0:T(8,128)S(1)} %get-tuple-element.23), channel_id=1, source_target_pairs={{0,256},{64,320},{128,384},{192,448},{256,0},{320,64},{384,128},{4... | collective-permute-start | bytes 294920 | tf_op jit(solution)/shard_map/ppermute | solution.py:351
  78.7 8.1 %collective-permute-start.4 = (f32[192,128]{1,0:T(8,128)S(1)}, f32[192,128]{1,0:T(8,128)S(1)}, u32[]{:S(2)}, u32[]{:S(2)}) collective-permute-start(f32[192,128]{1,0:T(8,128)S(1)} %get-tuple-element.24), channel_id=1, source_target_pairs={{0,320},{64,384},{128,448},{192,0},{256,64},{320,128},{384,192},{4... | collective-permute-start | bytes 294920 | tf_op jit(solution)/shard_map/ppermute | solution.py:351
  80.6 6.5 %collective-permute-start.5 = (f32[192,128]{1,0:T(8,128)S(1)}, f32[192,128]{1,0:T(8,128)S(1)}, u32[]{:S(2)}, u32[]{:S(2)}) collective-permute-start(f32[192,128]{1,0:T(8,128)S(1)} %get-tuple-element.25), channel_id=1, source_target_pairs={{0,384},{64,448},{128,0},{192,64},{256,128},{320,192},{384,256},{4... | collective-permute-start | bytes 294920 | tf_op jit(solution)/shard_map/ppermute | solution.py:351
  83.1 6.2 %collective-permute-start.6 = (f32[192,128]{1,0:T(8,128)S(1)}, f32[192,128]{1,0:T(8,128)S(1)}, u32[]{:S(2)}, u32[]{:S(2)}) collective-permute-start(f32[192,128]{1,0:T(8,128)S(1)} %get-tuple-element.26), channel_id=1, source_target_pairs={{0,448},{64,0},{128,64},{192,128},{256,192},{320,256},{384,320},{4... | collective-permute-start | bytes 294920 | tf_op jit(solution)/shard_map/ppermute | solution.py:351
  106.7 44.6 %all-to-all-start.2 = ((f32[512,2,128]{2,1,0:T(2,128)}), f32[512,2,128]{2,1,0:T(2,128)S(1)}, u32[]{:S(2)}, u32[]{:S(2)}) async-start(f32[512,2,128]{2,1,0:T(2,128)} %bitcast.7), calls=%async_computation.2 | async-start | bytes 1048576 | tf_op jit(solution)/shard_map/all_to_all | solution.py:345
  117.7 13.9 %collective-permute-start.7 = (f32[128,128]{1,0:T(8,128)S(1)}, f32[128,128]{1,0:T(8,128)S(1)}, u32[]{:S(2)}, u32[]{:S(2)}) collective-permute-start(f32[128,128]{1,0:T(8,128)S(1)} %get-tuple-element.29), channel_id=1, source_target_pairs={{0,64},{64,128},{128,192},{192,256},{256,320},{320,384},{384,448},... | collective-permute-start | bytes 196616 | tf_op jit(solution)/shard_map/ppermute | solution.py:351
  119.4 12.3 %collective-permute-start.8 = (f32[128,128]{1,0:T(8,128)S(1)}, f32[128,128]{1,0:T(8,128)S(1)}, u32[]{:S(2)}, u32[]{:S(2)}) collective-permute-start(f32[128,128]{1,0:T(8,128)S(1)} %get-tuple-element.30), channel_id=1, source_target_pairs={{0,128},{64,192},{128,256},{192,320},{256,384},{320,448},{384,0},{... | collective-permute-start | bytes 196616 | tf_op jit(solution)/shard_map/ppermute | solution.py:351
  122.5 9.7 %collective-permute-start.9 = (f32[128,128]{1,0:T(8,128)S(1)}, f32[128,128]{1,0:T(8,128)S(1)}, u32[]{:S(2)}, u32[]{:S(2)}) collective-permute-start(f32[128,128]{1,0:T(8,128)S(1)} %get-tuple-element.31), channel_id=1, source_target_pairs={{0,192},{64,256},{128,320},{192,384},{256,448},{320,0},{384,64},{4... | collective-permute-start | bytes 196616 | tf_op jit(solution)/shard_map/ppermute | solution.py:351
  126.1 8.2 %collective-permute-start.10 = (f32[128,128]{1,0:T(8,128)S(1)}, f32[128,128]{1,0:T(8,128)S(1)}, u32[]{:S(2)}, u32[]{:S(2)}) collective-permute-start(f32[128,128]{1,0:T(8,128)S(1)} %get-tuple-element.32), channel_id=1, source_target_pairs={{0,256},{64,320},{128,384},{192,448},{256,0},{320,64},{384,128},{4... | collective-permute-start | bytes 196616 | tf_op jit(solution)/shard_map/ppermute | solution.py:351
  153.2 37.3 %all-to-all-start.3 = ((f32[64,16,128]{2,1,0:T(8,128)}), f32[64,16,128]{2,1,0:T(8,128)S(1)}, u32[]{:S(2)}, u32[]{:S(2)}) async-start(f32[64,16,128]{2,1,0:T(8,128)} %bitcast.9), calls=%async_computation.3 | async-start | bytes 1048576 | tf_op jit(solution)/shard_map/all_to_all | solution.py:345
  160.0 7.2 %collective-permute-start.11 = (f32[128,128]{1,0:T(8,128)S(1)}, f32[128,128]{1,0:T(8,128)S(1)}, u32[]{:S(2)}, u32[]{:S(2)}) collective-permute-start(f32[128,128]{1,0:T(8,128)S(1)} %get-tuple-element.33), channel_id=1, source_target_pairs={{0,320},{64,384},{128,448},{192,0},{256,64},{320,128},{384,192},{4... | collective-permute-start | bytes 196616 | tf_op jit(solution)/shard_map/ppermute | solution.py:351
  163.5 5.7 %collective-permute-start.12 = (f32[128,128]{1,0:T(8,128)S(1)}, f32[128,128]{1,0:T(8,128)S(1)}, u32[]{:S(2)}, u32[]{:S(2)}) collective-permute-start(f32[128,128]{1,0:T(8,128)S(1)} %get-tuple-element.34), channel_id=1, source_target_pairs={{0,384},{64,448},{128,0},{192,64},{256,128},{320,192},{384,256},{4... | collective-permute-start | bytes 196616 | tf_op jit(solution)/shard_map/ppermute | solution.py:351
  165.9 24.6 %copy-start.1 = (f32[2,2,256,128]{3,2,1,0:T(8,128)S(1)}, f32[2,2,256,128]{3,2,1,0:T(8,128)}, u32[]{:S(2)}) copy-start(f32[2,2,256,128]{3,2,1,0:T(8,128)} %spectrum.3) | copy-start | bytes 1572868
  165.9 4.3 %collective-permute-start.13 = (f32[128,128]{1,0:T(8,128)S(1)}, f32[128,128]{1,0:T(8,128)S(1)}, u32[]{:S(2)}, u32[]{:S(2)}) collective-permute-start(f32[128,128]{1,0:T(8,128)S(1)} %get-tuple-element.35), channel_id=1, source_target_pairs={{0,448},{64,0},{128,64},{192,128},{256,192},{320,256},{384,320},{4... | collective-permute-start | bytes 196616 | tf_op jit(solution)/shard_map/ppermute | solution.py:351
  (4 other events, 2.7 us)

commit v4 on v3

--- a/solution.py
+++ b/solution.py
@@ -13,7 +13,7 @@
 depth_step = 2.0
 step_size = 0.125
 root_floor = 0.25
-early_echoes = 3
+early_echoes = 4
 early_pieces = 5
 bf16 = jnp.bfloat16
 f32 = jnp.float32
@@ -42,11 +42,11 @@
     theta = angles(np.arange(16), index, 2048)
     twist_heard = np.stack([np.cos(theta), np.sin(theta)])
     twist_heard = np.broadcast_to(twist_heard[:, :, None, :], (2, 16, 8, 128)).astype(np.float32)
-    index = np.arange(512)
-    theta = angles(index, index, 512)
+    index = np.arange(256)
+    theta = angles(index, index, 256)
     long = halves(np.cos(theta) * scale) + halves(np.sin(theta) * scale)
     low_of_lane = np.arange(128) % 4
-    theta = angles(np.arange(512), low_of_lane, 2048)
+    theta = angles(index, low_of_lane, 2048)
     twist_sent = np.stack([np.cos(theta), np.sin(theta)]).astype(np.float32)
     mix = np.zeros((2, 16, 2, 4, 2, 4, 2, 16))
     quarter = ((1, 0), (0, 1), (-1, 0), (0, -1))
@@ -66,7 +66,6 @@
         long=long,
         twist_sent=twist_sent,
         mix=mix,
-        mix_back=mix.T.copy(),
     )
 
 
@@ -254,30 +253,55 @@
                 out[z, y, c] = x + w
 
 
-def long_sums(re, im, tables_of):
-    re_high, re_low = split(re)
-    im_high, im_low = split(im)
-    whole = jnp.concatenate([re_high, re_low, im_high, im_low], 1)
-    high = jnp.concatenate([re_high, im_high], 1)
+def half_sums(pairs, tables_of):
+    columns, highs = [], []
+    for pair in pairs:
+        for value in pair:
+            high, rest = split(value)
+            columns += [high, rest]
+            highs.append(high)
+    columns, highs = jnp.concatenate(columns, 1), jnp.concatenate(highs, 1)
     sums = []
     for k in range(2):
-        first = dot(tables_of[2 * k][...], whole)
-        second = dot(tables_of[2 * k + 1][...], high)
-        sums.append(first[:, :128] + first[:, 128:256] + second[:, :128])
-        sums.append(first[:, 256:384] + first[:, 384:] + second[:, 128:])
-    return sums
+        first = dot(tables_of[2 * k][...], columns)
+        second = dot(tables_of[2 * k + 1][...], highs)
+        sums.append(
+            [
+                first[:, 256 * j : 256 * j + 128]
+                + first[:, 256 * j + 128 : 256 * j + 256]
+                + second[:, 128 * j : 128 * j + 128]
+                for j in range(4)
+            ]
+        )
+    cosine, sine = sums
+    return [(*cosine[2 * p : 2 * p + 2], *sine[2 * p : 2 * p + 2]) for p in range(2)]
+
+
+def turned(value, by):
+    return value[0] * by[0] - value[1] * by[1], value[0] * by[1] + value[1] * by[0]
+
+
+def turned_back(value, by):
+    return value[0] * by[0] + value[1] * by[1], value[1] * by[0] - value[0] * by[1]
+
+
+def sent_twists(twist):
+    first = twist[0], twist[1]
+    quarter = [jnp.broadcast_to(part[:, 2:3], part.shape) for part in first]
+    low = lax.broadcasted_iota(jnp.int32, first[0].shape, 1) & 3
+    half = math.sqrt(0.5)
+    eighth = (
+        jnp.where(low == 0, 1.0, jnp.where(low == 1, half, jnp.where(low == 2, 0.0, -half))),
+        jnp.where(low == 0, 0.0, jnp.where(low == 2, 1.0, half)),
+    )
+    second = turned(first, eighth)
+    whole = [jnp.concatenate([a, b], 0) for a, b in zip(first, second)]
+    return whole, turned(quarter, quarter)
 
 
 def middle_kernel(place, arrived, *refs):
-    echoes, given, out, sent = refs[:8], refs[8:15], refs[15], refs[16:24]
-    held, resid, arrival = refs[24], refs[25], refs[33]
-    copies = [
-        pltpu.make_async_copy(source, target, arrival.at[k])
-        for k, (source, target) in enumerate(zip(given, refs[26:33]))
-    ]
-    for copy in copies:
-        copy.start()
-    long, twist, mix, mix_back = refs[26:30], refs[30], refs[31], refs[32]
+    echoes, given, out, sent = refs[:8], refs[8:14], refs[14], refs[15:23]
+    held, resid = refs[23:]
     for step in range(8):
         held[(place[0] + 8 - step) & 7] = echoes[step][...]
     parts = []
@@ -287,16 +311,20 @@
             pieces = [held[2 * t1 + odd, k * 64 : (k + 1) * 64, :] for t1 in range(4)]
             rows += swap_groups(pieces, 32)
         parts.append(jnp.concatenate(rows, 0))
-    for copy in copies:
-        copy.wait()
-    cos_re, cos_im, sin_re, sin_im = long_sums(
-        arrived[pl.ds(0, 512, stride=2), :], arrived[pl.ds(1, 512, stride=2), :], long
-    )
-    re, im = cos_re - sin_im, sin_re + cos_im
-    tr, ti = twist[0], twist[1]
-    both = jnp.concatenate([re * tr - im * ti, re * ti + im * tr], 1)
+    long, twist, mix = given[:4], given[4], given[5][...]
+    both_twists, odd_twist = sent_twists(twist)
+    pairs = [
+        tuple(arrived[pl.ds(2 * p + c, 256, stride=4), :] for c in range(2)) for p in range(2)
+    ]
+    even, odd = [
+        (cos_re - sin_im, sin_re + cos_im)
+        for cos_re, cos_im, sin_re, sin_im in half_sums(pairs, long)
+    ]
+    odd = turned(odd, odd_twist)
+    value = [jnp.concatenate([a + b, a - b], 0) for a, b in zip(even, odd)]
+    both = jnp.concatenate(turned(value, both_twists), 1)
     high, rest = split(both)
-    field = dot(high, mix[...]) + dot(rest, mix[...])
+    field = dot(high, mix) + dot(rest, mix)
     left = []
     for k in range(2):
         value = parts[2] * (parts[k] - field[:, k * 128 : (k + 1) * 128])
@@ -307,12 +335,17 @@
                 resid[2 * t1 + odd, k * 64 : (k + 1) * 64, :] = piece
     for step in range(8):
         sent[step][...] = resid[(place[0] + step) & 7]
-    high, rest = split(jnp.concatenate(left, 1))
-    mixed = dot(high, mix_back[...]) + dot(rest, mix_back[...])
-    re, im = mixed[:, :128], mixed[:, 128:]
-    cos_re, cos_im, sin_re, sin_im = long_sums(re * tr + im * ti, im * tr - re * ti, long)
-    out[pl.ds(0, 512, stride=2), :] = cos_re + sin_im
-    out[pl.ds(1, 512, stride=2), :] = cos_im - sin_re
+    mixed = sum(
+        lax.dot_general(half, mix, nt_form, preferred_element_type=f32)
+        for half in split(jnp.concatenate(left, 1))
+    )
+    value = turned_back((mixed[:, :128], mixed[:, 128:]), both_twists)
+    even = [part[:256] + part[256:] for part in value]
+    odd = turned_back([part[:256] - part[256:] for part in value], odd_twist)
+    for p, sums in enumerate(half_sums([even, odd], long)):
+        cos_re, cos_im, sin_re, sin_im = sums
+        out[pl.ds(2 * p, 256, stride=4), :] = cos_re + sin_im
+        out[pl.ds(2 * p + 1, 256, stride=4), :] = cos_im - sin_re
 
 
 def call(kernel, outs, *operands, near=0, apart=0, far=False, scratch=(), place=None, flops=0):
@@ -405,19 +438,15 @@
         flops=10**9,
     )
     columns = exchange(pairs.reshape(512, 2, 128), ("tx", "rx", "freq")).reshape(1024, 128)
-    given = [*table["long"], table["twist_sent"], table["mix"], table["mix_back"]]
-    given = [pltpu.with_memory_space_constraint(jnp.asarray(t), pltpu.HBM) for t in given]
+    given = [*table["long"], table["twist_sent"], table["mix"]]
     back, *resid = call(
         middle_kernel,
         [(1024, 128)] + [(128, 128)] * 8,
         columns,
         *echoes,
         *given,
-        near=9,
-        apart=7,
-        scratch=[(8, 192, 128), (8, 128, 128)]
-        + [pltpu.VMEM(t.shape, t.dtype) for t in given]
-        + [pltpu.SemaphoreType.DMA((7,))],
+        near=15,
+        scratch=[(8, 192, 128), (8, 128, 128)],
         place=place,
         flops=3 * 10**9,
     )

time: 194 us -> 192 us (0.990)
  Pallas kernels: 13.6 us -> 10.8 us
    pallas_call x7, Pallas kernels: 13.6 us -> 10.8 us  [call(): pl.pallas_call(kernel, out_shape=outs if far else [pltpu.VMEM(o.shape, o....]
    unnamed x21 -> x33, local copies, waits for them, and re-layouts: 3.14 us -> 4.06 us
where the time goes in v4:
time: 192 us; the launch traced here: 189 us
  starting transfers between devices  93.9 us (49%)
  waiting for transfers between devices  78.3 us (41%)
  Pallas kernels  10.8 us (6%)
  local copies, waits for them, and re-layouts  4.31 us (2%)
    all_to_all x4, waiting for transfers between devices, exchange(): return lax.all_to_all(value, axes, split_axis=0, concat_axis=0, tiled=True)  66.1 us
    all_to_all x4, starting transfers between devices, exchange(): return lax.all_to_all(value, axes, split_axis=0, concat_axis=0, tiled=True)  50.7 us
    ppermute x14, starting transfers between devices, along_tx(): lax.ppermute(pieces[step], 'tx', [(i, (i + step) % 8) for i in range(8)])  43.2 us
    ppermute x14, waiting for transfers between devices, along_tx(): lax.ppermute(pieces[step], 'tx', [(i, (i + step) % 8) for i in range(8)])  12.2 us
    pallas_call x7, Pallas kernels, call(): pl.pallas_call(kernel, out_shape=outs if far else [pltpu.VMEM(o.shape, o....  10.8 us
    unnamed x33, local copies, waits for them, and re-layouts  4.06 us
  transfers between devices with their start and end apart: 18, of which 12 were waited for; matrix products, arithmetic and copies ran while one was open for 1% of the time, Pallas kernels for 1%

profile of v4, /device:TPU:1, one launch (start us, length us, event | category | flops | bytes accessed | tf_op | source)
XLA Modules:
  0.0 189.4 jit_solution(3003307385054791725)
XLA Ops:
  2.5 19.4 %all-to-all-start = ((f32[64,16,128]{2,1,0:T(8,128)}), f32[64,16,128]{2,1,0:T(8,128)S(1)}, u32[]{:S(2)}, u32[]{:S(2)}) async-start(f32[64,16,128]{2,1,0:T(8,128)} %bitcast.1), calls=%async_computation | async-start | bytes 1048576 | tf_op jit(solution)/shard_map/all_to_all | solution.py:378
  24.3 2.1 %collective-permute-start = (f32[192,128]{1,0:T(8,128)S(1)}, f32[192,128]{1,0:T(8,128)S(1)}, u32[]{:S(2)}, u32[]{:S(2)}) collective-permute-start(f32[192,128]{1,0:T(8,128)S(1)} %get-tuple-element.20), channel_id=1, source_target_pairs={{0,64},{64,128},{128,192},{192,256},{256,320},{320,384},{384,448},... | collective-permute-start | bytes 294920 | tf_op jit(solution)/shard_map/ppermute | solution.py:384
  26.4 3.1 %collective-permute-start.1 = (f32[192,128]{1,0:T(8,128)S(1)}, f32[192,128]{1,0:T(8,128)S(1)}, u32[]{:S(2)}, u32[]{:S(2)}) collective-permute-start(f32[192,128]{1,0:T(8,128)S(1)} %get-tuple-element.21), channel_id=1, source_target_pairs={{0,128},{64,192},{128,256},{192,320},{256,384},{320,448},{384,0},{... | collective-permute-start | bytes 294920 | tf_op jit(solution)/shard_map/ppermute | solution.py:384
  29.5 3.5 %collective-permute-start.2 = (f32[192,128]{1,0:T(8,128)S(1)}, f32[192,128]{1,0:T(8,128)S(1)}, u32[]{:S(2)}, u32[]{:S(2)}) collective-permute-start(f32[192,128]{1,0:T(8,128)S(1)} %get-tuple-element.22), channel_id=1, source_target_pairs={{0,192},{64,256},{128,320},{192,384},{256,448},{320,0},{384,64},{4... | collective-permute-start | bytes 294920 | tf_op jit(solution)/shard_map/ppermute | solution.py:384
  37.0 15.0 %all-to-all-done = f32[64,16,128]{2,1,0:T(8,128)S(1)} async-done(((f32[64,16,128]{2,1,0:T(8,128)}), f32[64,16,128]{2,1,0:T(8,128)S(1)}, u32[]{:S(2)}, u32[]{:S(2)}) %all-to-all-start) | async-done | bytes 524320 | tf_op jit(solution)/shard_map/all_to_all | solution.py:378
  52.0 2.1 %shard_map.160 = f32[1024,128]{1,0:T(8,128)} custom-call(f32[16,4,2,8,128]{4,3,2,1,0:T(8,128)S(1)} %bitcast.12, f32[2,16,4,8,128]{4,3,2,1,0:T(8,128)S(1)} %pad_maximum_fusion.turn, f32[2,16,8,128]{3,2,1,0:T(8,128)S(1)} %copy-done.8, bf16[256,256]{1,0:T(8,128)(2,1)S(1)} %copy-done.7, bf16[256,256]{1,0:T(8,128)(2,1)S(1)} %copy-done.6, ...), custom_call_target="tpu_custom_call" | custom-call | flops 1000000000 | bytes 2359296 | tf_op jit(solution)/shard_map/pallas_call | solution.py:365
  54.1 13.7 %all-to-all-start.1 = ((f32[512,2,128]{2,1,0:T(2,128)}), f32[512,2,128]{2,1,0:T(2,128)S(1)}, u32[]{:S(2)}, u32[]{:S(2)}) async-start(f32[512,2,128]{2,1,0:T(2,128)} %bitcast.5), calls=%async_computation.1 | async-start | bytes 1048576 | tf_op jit(solution)/shard_map/all_to_all | solution.py:378
  67.8 4.8 %collective-permute-start.3 = (f32[192,128]{1,0:T(8,128)S(1)}, f32[192,128]{1,0:T(8,128)S(1)}, u32[]{:S(2)}, u32[]{:S(2)}) collective-permute-start(f32[192,128]{1,0:T(8,128)S(1)} %get-tuple-element.23), channel_id=1, source_target_pairs={{0,256},{64,320},{128,384},{192,448},{256,0},{320,64},{384,128},{4... | collective-permute-start | bytes 294920 | tf_op jit(solution)/shard_map/ppermute | solution.py:384
  72.6 3.3 %collective-permute-start.4 = (f32[192,128]{1,0:T(8,128)S(1)}, f32[192,128]{1,0:T(8,128)S(1)}, u32[]{:S(2)}, u32[]{:S(2)}) collective-permute-start(f32[192,128]{1,0:T(8,128)S(1)} %get-tuple-element.24), channel_id=1, source_target_pairs={{0,320},{64,384},{128,448},{192,0},{256,64},{320,128},{384,192},{4... | collective-permute-start | bytes 294920 | tf_op jit(solution)/shard_map/ppermute | solution.py:384
  75.9 5.3 %collective-permute-start.5 = (f32[192,128]{1,0:T(8,128)S(1)}, f32[192,128]{1,0:T(8,128)S(1)}, u32[]{:S(2)}, u32[]{:S(2)}) collective-permute-start(f32[192,128]{1,0:T(8,128)S(1)} %get-tuple-element.25), channel_id=1, source_target_pairs={{0,384},{64,448},{128,0},{192,64},{256,128},{320,192},{384,256},{4... | collective-permute-start | bytes 294920 | tf_op jit(solution)/shard_map/ppermute | solution.py:384
  83.9 2.1 %collective-permute-done.6.refs_7_ = f32[192,128]{1,0:T(8,128)S(1)} collective-permute-done((f32[192,128]{1,0:T(8,128)S(1)}, f32[192,128]{1,0:T(8,128)S(1)}, u32[]{:S(2)}, u32[]{:S(2)}) %collective-permute-start.6) | collective-permute-done | bytes 98336 | tf_op jit(solution)/shard_map/ppermute | solution.py:384
  85.9 15.3 %all-to-all-done.1 = f32[512,2,128]{2,1,0:T(2,128)S(1)} async-done(((f32[512,2,128]{2,1,0:T(2,128)}), f32[512,2,128]{2,1,0:T(2,128)S(1)}, u32[]{:S(2)}, u32[]{:S(2)}) %all-to-all-start.1) | async-done | bytes 524320 | tf_op jit(solution)/shard_map/all_to_all | solution.py:378
  102.1 2.8 %shard_map.161 = (f32[1024,128]{1,0:T(8,128)}, f32[128,128]{1,0:T(8,128)S(1)}, f32[128,128]{1,0:T(8,128)S(1)}, f32[128,128]{1,0:T(8,128)S(1)}, f32[128,128]{1,0:...) custom-call(s32[1]{0:T(128)} %bitcast.place, ...), custom_call_target="tpu_custom_call" | custom-call | flops 3000000000 | bytes 3276800 | tf_op jit(solution)/shard_map/pallas_call | solution.py:365
  104.9 10.8 %all-to-all-start.2 = ((f32[512,2,128]{2,1,0:T(2,128)}), f32[512,2,128]{2,1,0:T(2,128)S(1)}, u32[]{:S(2)}, u32[]{:S(2)}) async-start(f32[512,2,128]{2,1,0:T(2,128)} %bitcast.7), calls=%async_computation.2 | async-start | bytes 1048576 | tf_op jit(solution)/shard_map/all_to_all | solution.py:378
  117.4 3.1 %collective-permute-start.8 = (f32[128,128]{1,0:T(8,128)S(1)}, f32[128,128]{1,0:T(8,128)S(1)}, u32[]{:S(2)}, u32[]{:S(2)}) collective-permute-start(f32[128,128]{1,0:T(8,128)S(1)} %get-tuple-element.30), channel_id=1, source_target_pairs={{0,128},{64,192},{128,256},{192,320},{256,384},{320,448},{384,0},{... | collective-permute-start | bytes 196616 | tf_op jit(solution)/shard_map/ppermute | solution.py:384
  120.5 3.6 %collective-permute-start.9 = (f32[128,128]{1,0:T(8,128)S(1)}, f32[128,128]{1,0:T(8,128)S(1)}, u32[]{:S(2)}, u32[]{:S(2)}) collective-permute-start(f32[128,128]{1,0:T(8,128)S(1)} %get-tuple-element.31), channel_id=1, source_target_pairs={{0,192},{64,256},{128,320},{192,384},{256,448},{320,0},{384,64},{4... | collective-permute-start | bytes 196616 | tf_op jit(solution)/shard_map/ppermute | solution.py:384
  124.1 5.6 %collective-permute-start.10 = (f32[128,128]{1,0:T(8,128)S(1)}, f32[128,128]{1,0:T(8,128)S(1)}, u32[]{:S(2)}, u32[]{:S(2)}) collective-permute-start(f32[128,128]{1,0:T(8,128)S(1)} %get-tuple-element.32), channel_id=1, source_target_pairs={{0,256},{64,320},{128,384},{192,448},{256,0},{320,64},{384,128},{4... | collective-permute-start | bytes 196616 | tf_op jit(solution)/shard_map/ppermute | solution.py:384
  130.3 2.1 %collective-permute-done.10.refs_4_ = f32[128,128]{1,0:T(8,128)S(1)} collective-permute-done((f32[128,128]{1,0:T(8,128)S(1)}, f32[128,128]{1,0:T(8,128)S(1)}, u32[]{:S(2)}, u32[]{:S(2)}) %collective-permute-start.10) | collective-permute-done | bytes 65568 | tf_op jit(solution)/shard_map/ppermute | solution.py:384
  132.4 17.0 %all-to-all-done.2 = f32[512,2,128]{2,1,0:T(2,128)S(1)} async-done(((f32[512,2,128]{2,1,0:T(2,128)}), f32[512,2,128]{2,1,0:T(2,128)S(1)}, u32[]{:S(2)}, u32[]{:S(2)}) %all-to-all-start.2) | async-done | bytes 524320 | tf_op jit(solution)/shard_map/all_to_all | solution.py:378
  151.3 6.8 %all-to-all-start.3 = ((f32[64,16,128]{2,1,0:T(8,128)}), f32[64,16,128]{2,1,0:T(8,128)S(1)}, u32[]{:S(2)}, u32[]{:S(2)}) async-start(f32[64,16,128]{2,1,0:T(8,128)} %bitcast.9), calls=%async_computation.3 | async-start | bytes 1048576 | tf_op jit(solution)/shard_map/all_to_all | solution.py:378
  158.0 3.5 %collective-permute-start.11 = (f32[128,128]{1,0:T(8,128)S(1)}, f32[128,128]{1,0:T(8,128)S(1)}, u32[]{:S(2)}, u32[]{:S(2)}) collective-permute-start(f32[128,128]{1,0:T(8,128)S(1)} %get-tuple-element.33), channel_id=1, source_target_pairs={{0,320},{64,384},{128,448},{192,0},{256,64},{320,128},{384,192},{4... | collective-permute-start | bytes 196616 | tf_op jit(solution)/shard_map/ppermute | solution.py:384
  161.5 2.4 %collective-permute-start.12 = (f32[128,128]{1,0:T(8,128)S(1)}, f32[128,128]{1,0:T(8,128)S(1)}, u32[]{:S(2)}, u32[]{:S(2)}) collective-permute-start(f32[128,128]{1,0:T(8,128)S(1)} %get-tuple-element.34), channel_id=1, source_target_pairs={{0,384},{64,448},{128,0},{192,64},{256,128},{320,192},{384,256},{4... | collective-permute-start | bytes 196616 | tf_op jit(solution)/shard_map/ppermute | solution.py:384
  165.3 2.0 %collective-permute-done.12.refs_6_ = f32[128,128]{1,0:T(8,128)S(1)} collective-permute-done((f32[128,128]{1,0:T(8,128)S(1)}, f32[128,128]{1,0:T(8,128)S(1)}, u32[]{:S(2)}, u32[]{:S(2)}) %collective-permute-start.12) | collective-permute-done | bytes 65568 | tf_op jit(solution)/shard_map/ppermute | solution.py:384
  169.6 18.9 %all-to-all-done.3 = f32[64,16,128]{2,1,0:T(8,128)S(1)} async-done(((f32[64,16,128]{2,1,0:T(8,128)}), f32[64,16,128]{2,1,0:T(8,128)S(1)}, u32[]{:S(2)}, u32[]{:S(2)}) %all-to-all-start.3) | async-done | bytes 524320 | tf_op jit(solution)/shard_map/all_to_all | solution.py:378
  (61 shorter events, 20.4 us)
Async XLA Ops:
  2.5 49.4 %all-to-all-start = ((f32[64,16,128]{2,1,0:T(8,128)}), f32[64,16,128]{2,1,0:T(8,128)S(1)}, u32[]{:S(2)}, u32[]{:S(2)}) async-start(f32[64,16,128]{2,1,0:T(8,128)} %bitcast.1), calls=%async_computation | async-start | bytes 1048576 | tf_op jit(solution)/shard_map/all_to_all | solution.py:378
  24.3 10.8 %collective-permute-start = (f32[192,128]{1,0:T(8,128)S(1)}, f32[192,128]{1,0:T(8,128)S(1)}, u32[]{:S(2)}, u32[]{:S(2)}) collective-permute-start(f32[192,128]{1,0:T(8,128)S(1)} %get-tuple-element.20), channel_id=1, source_target_pairs={{0,64},{64,128},{128,192},{192,256},{256,320},{320,384},{384,448},... | collective-permute-start | bytes 294920 | tf_op jit(solution)/shard_map/ppermute | solution.py:384
  26.4 8.7 %collective-permute-start.1 = (f32[192,128]{1,0:T(8,128)S(1)}, f32[192,128]{1,0:T(8,128)S(1)}, u32[]{:S(2)}, u32[]{:S(2)}) collective-permute-start(f32[192,128]{1,0:T(8,128)S(1)} %get-tuple-element.21), channel_id=1, source_target_pairs={{0,128},{64,192},{128,256},{192,320},{256,384},{320,448},{384,0},{... | collective-permute-start | bytes 294920 | tf_op jit(solution)/shard_map/ppermute | solution.py:384
  29.5 7.4 %collective-permute-start.2 = (f32[192,128]{1,0:T(8,128)S(1)}, f32[192,128]{1,0:T(8,128)S(1)}, u32[]{:S(2)}, u32[]{:S(2)}) collective-permute-start(f32[192,128]{1,0:T(8,128)S(1)} %get-tuple-element.22), channel_id=1, source_target_pairs={{0,192},{64,256},{128,320},{192,384},{256,448},{320,0},{384,64},{4... | collective-permute-start | bytes 294920 | tf_op jit(solution)/shard_map/ppermute | solution.py:384
  54.1 47.1 %copy-start.5 = (f32[2,256,128]{2,1,0:T(8,128)S(1)}, f32[2,256,128]{2,1,0:T(8,128)}, u32[]{:S(2)}) copy-start(f32[2,256,128]{2,1,0:T(8,128)} %constant.85.clone.refs_12_) | copy-start | bytes 786436
  54.1 47.1 %copy-start.9 = (bf16[256,256]{1,0:T(8,128)(2,1)S(1)}, bf16[256,256]{1,0:T(8,128)(2,1)}, u32[]{:S(2)}) copy-start(bf16[256,256]{1,0:T(8,128)(2,1)} %constant.86.clone.refs_13_) | copy-start | bytes 393220
  54.1 47.1 %copy-start.10 = (bf16[256,256]{1,0:T(8,128)(2,1)S(1)}, bf16[256,256]{1,0:T(8,128)(2,1)}, u32[]{:S(2)}) copy-start(bf16[256,256]{1,0:T(8,128)(2,1)} %constant.84.clone.refs_11_) | copy-start | bytes 393220
  54.1 47.1 %copy-start.11 = (bf16[256,256]{1,0:T(8,128)(2,1)S(1)}, bf16[256,256]{1,0:T(8,128)(2,1)}, u32[]{:S(2)}) copy-start(bf16[256,256]{1,0:T(8,128)(2,1)} %constant.83.clone.refs_10_) | copy-start | bytes 393220
  54.1 47.2 %copy-start.12 = (bf16[256,256]{1,0:T(8,128)(2,1)S(1)}, bf16[256,256]{1,0:T(8,128)(2,1)}, u32[]{:S(2)}) copy-start(bf16[256,256]{1,0:T(8,128)(2,1)} %constant.82.clone.refs_9_) | copy-start | bytes 393220
  54.1 47.1 %all-to-all-start.1 = ((f32[512,2,128]{2,1,0:T(2,128)}), f32[512,2,128]{2,1,0:T(2,128)S(1)}, u32[]{:S(2)}, u32[]{:S(2)}) async-start(f32[512,2,128]{2,1,0:T(2,128)} %bitcast.5), calls=%async_computation.1 | async-start | bytes 1048576 | tf_op jit(solution)/shard_map/all_to_all | solution.py:378
  67.8 13.5 %collective-permute-start.3 = (f32[192,128]{1,0:T(8,128)S(1)}, f32[192,128]{1,0:T(8,128)S(1)}, u32[]{:S(2)}, u32[]{:S(2)}) collective-permute-start(f32[192,128]{1,0:T(8,128)S(1)} %get-tuple-element.23), channel_id=1, source_target_pairs={{0,256},{64,320},{128,384},{192,448},{256,0},{320,64},{384,128},{4... | collective-permute-start | bytes 294920 | tf_op jit(solution)/shard_map/ppermute | solution.py:384
  72.6 9.4 %collective-permute-start.4 = (f32[192,128]{1,0:T(8,128)S(1)}, f32[192,128]{1,0:T(8,128)S(1)}, u32[]{:S(2)}, u32[]{:S(2)}) collective-permute-start(f32[192,128]{1,0:T(8,128)S(1)} %get-tuple-element.24), channel_id=1, source_target_pairs={{0,320},{64,384},{128,448},{192,0},{256,64},{320,128},{384,192},{4... | collective-permute-start | bytes 294920 | tf_op jit(solution)/shard_map/ppermute | solution.py:384
  75.9 8.0 %collective-permute-start.5 = (f32[192,128]{1,0:T(8,128)S(1)}, f32[192,128]{1,0:T(8,128)S(1)}, u32[]{:S(2)}, u32[]{:S(2)}) collective-permute-start(f32[192,128]{1,0:T(8,128)S(1)} %get-tuple-element.25), channel_id=1, source_target_pairs={{0,384},{64,448},{128,0},{192,64},{256,128},{320,192},{384,256},{4... | collective-permute-start | bytes 294920 | tf_op jit(solution)/shard_map/ppermute | solution.py:384
  81.2 4.7 %collective-permute-start.6 = (f32[192,128]{1,0:T(8,128)S(1)}, f32[192,128]{1,0:T(8,128)S(1)}, u32[]{:S(2)}, u32[]{:S(2)}) collective-permute-start(f32[192,128]{1,0:T(8,128)S(1)} %get-tuple-element.26), channel_id=1, source_target_pairs={{0,448},{64,0},{128,64},{192,128},{256,192},{320,256},{384,320},{4... | collective-permute-start | bytes 294920 | tf_op jit(solution)/shard_map/ppermute | solution.py:384
  104.9 44.4 %all-to-all-start.2 = ((f32[512,2,128]{2,1,0:T(2,128)}), f32[512,2,128]{2,1,0:T(2,128)S(1)}, u32[]{:S(2)}, u32[]{:S(2)}) async-start(f32[512,2,128]{2,1,0:T(2,128)} %bitcast.7), calls=%async_computation.2 | async-start | bytes 1048576 | tf_op jit(solution)/shard_map/all_to_all | solution.py:378
  115.8 13.9 %collective-permute-start.7 = (f32[128,128]{1,0:T(8,128)S(1)}, f32[128,128]{1,0:T(8,128)S(1)}, u32[]{:S(2)}, u32[]{:S(2)}) collective-permute-start(f32[128,128]{1,0:T(8,128)S(1)} %get-tuple-element.29), channel_id=1, source_target_pairs={{0,64},{64,128},{128,192},{192,256},{256,320},{320,384},{384,448},... | collective-permute-start | bytes 196616 | tf_op jit(solution)/shard_map/ppermute | solution.py:384
  117.4 12.3 %collective-permute-start.8 = (f32[128,128]{1,0:T(8,128)S(1)}, f32[128,128]{1,0:T(8,128)S(1)}, u32[]{:S(2)}, u32[]{:S(2)}) collective-permute-start(f32[128,128]{1,0:T(8,128)S(1)} %get-tuple-element.30), channel_id=1, source_target_pairs={{0,128},{64,192},{128,256},{192,320},{256,384},{320,448},{384,0},{... | collective-permute-start | bytes 196616 | tf_op jit(solution)/shard_map/ppermute | solution.py:384
  120.5 9.7 %collective-permute-start.9 = (f32[128,128]{1,0:T(8,128)S(1)}, f32[128,128]{1,0:T(8,128)S(1)}, u32[]{:S(2)}, u32[]{:S(2)}) collective-permute-start(f32[128,128]{1,0:T(8,128)S(1)} %get-tuple-element.31), channel_id=1, source_target_pairs={{0,192},{64,256},{128,320},{192,384},{256,448},{320,0},{384,64},{4... | collective-permute-start | bytes 196616 | tf_op jit(solution)/shard_map/ppermute | solution.py:384
  124.1 8.3 %collective-permute-start.10 = (f32[128,128]{1,0:T(8,128)S(1)}, f32[128,128]{1,0:T(8,128)S(1)}, u32[]{:S(2)}, u32[]{:S(2)}) collective-permute-start(f32[128,128]{1,0:T(8,128)S(1)} %get-tuple-element.32), channel_id=1, source_target_pairs={{0,256},{64,320},{128,384},{192,448},{256,0},{320,64},{384,128},{4... | collective-permute-start | bytes 196616 | tf_op jit(solution)/shard_map/ppermute | solution.py:384
  151.3 37.2 %all-to-all-start.3 = ((f32[64,16,128]{2,1,0:T(8,128)}), f32[64,16,128]{2,1,0:T(8,128)S(1)}, u32[]{:S(2)}, u32[]{:S(2)}) async-start(f32[64,16,128]{2,1,0:T(8,128)} %bitcast.9), calls=%async_computation.3 | async-start | bytes 1048576 | tf_op jit(solution)/shard_map/all_to_all | solution.py:378
  158.0 7.2 %collective-permute-start.11 = (f32[128,128]{1,0:T(8,128)S(1)}, f32[128,128]{1,0:T(8,128)S(1)}, u32[]{:S(2)}, u32[]{:S(2)}) collective-permute-start(f32[128,128]{1,0:T(8,128)S(1)} %get-tuple-element.33), channel_id=1, source_target_pairs={{0,320},{64,384},{128,448},{192,0},{256,64},{320,128},{384,192},{4... | collective-permute-start | bytes 196616 | tf_op jit(solution)/shard_map/ppermute | solution.py:384
  161.5 5.7 %collective-permute-start.12 = (f32[128,128]{1,0:T(8,128)S(1)}, f32[128,128]{1,0:T(8,128)S(1)}, u32[]{:S(2)}, u32[]{:S(2)}) collective-permute-start(f32[128,128]{1,0:T(8,128)S(1)} %get-tuple-element.34), channel_id=1, source_target_pairs={{0,384},{64,448},{128,0},{192,64},{256,128},{320,192},{384,256},{4... | collective-permute-start | bytes 196616 | tf_op jit(solution)/shard_map/ppermute | solution.py:384
  163.9 24.6 %copy-start.1 = (f32[2,2,256,128]{3,2,1,0:T(8,128)S(1)}, f32[2,2,256,128]{3,2,1,0:T(8,128)}, u32[]{:S(2)}) copy-start(f32[2,2,256,128]{3,2,1,0:T(8,128)} %spectrum.3) | copy-start | bytes 1572868
  163.9 4.3 %collective-permute-start.13 = (f32[128,128]{1,0:T(8,128)S(1)}, f32[128,128]{1,0:T(8,128)S(1)}, u32[]{:S(2)}, u32[]{:S(2)}) collective-permute-start(f32[128,128]{1,0:T(8,128)S(1)} %get-tuple-element.35), channel_id=1, source_target_pairs={{0,448},{64,0},{128,64},{192,128},{256,192},{320,256},{384,320},{4... | collective-permute-start | bytes 196616 | tf_op jit(solution)/shard_map/ppermute | solution.py:384
  (10 other events, 75.7 us)

commit v5 on v4

--- a/solution.py
+++ b/solution.py
@@ -128,13 +128,23 @@
     return first + second
 
 
-def send_kernel(spectrum, out):
-    for c in range(2):
-        a = spectrum[c, 0].reshape(32, 8, 128)
-        b = spectrum[c, 1].reshape(32, 8, 128)
+def send_kernel(spectrum, out, held, arrival):
+    parts = [(c, h) for c in range(2) for h in range(2)]
+    copies = []
+    for k, (c, h) in enumerate(parts):
+        rows = pl.ds(h * 128, 128)
+        copies.append(
+            pltpu.make_async_copy(spectrum.at[c, :, rows], held.at[c, :, rows], arrival.at[k])
+        )
+    for copy in copies:
+        copy.start()
+    for copy, (c, h) in zip(copies, parts):
+        copy.wait()
+        a = held[c, 0, h * 128 : (h + 1) * 128].reshape(16, 8, 128)
+        b = held[c, 1, h * 128 : (h + 1) * 128].reshape(16, 8, 128)
         low = lax.broadcasted_iota(jnp.int32, a.shape, 1) < 4
-        out[:, 0, c] = jnp.where(low, a, pltpu.roll(b, 4, 1))
-        out[:, 1, c] = jnp.where(low, pltpu.roll(a, 4, 1), b)
+        out[16 * h : 16 * h + 16, 0, c] = jnp.where(low, a, pltpu.roll(b, 4, 1))
+        out[16 * h : 16 * h + 16, 1, c] = jnp.where(low, pltpu.roll(a, 4, 1), b)
 
 
 def update_kernel(arrived, spectrum, out):
@@ -301,7 +311,9 @@
 
 def middle_kernel(place, arrived, *refs):
     echoes, given, out, sent = refs[:8], refs[8:14], refs[14], refs[15:23]
-    held, resid = refs[23:]
+    held, resid, first, arrival = refs[23:]
+    copy = pltpu.make_async_copy(given[5], first, arrival)
+    copy.start()
     for step in range(8):
         held[(place[0] + 8 - step) & 7] = echoes[step][...]
     parts = []
@@ -311,7 +323,8 @@
             pieces = [held[2 * t1 + odd, k * 64 : (k + 1) * 64, :] for t1 in range(4)]
             rows += swap_groups(pieces, 32)
         parts.append(jnp.concatenate(rows, 0))
-    long, twist, mix = given[:4], given[4], given[5][...]
+    copy.wait()
+    long, twist, mix = [first, *given[:3]], given[3], given[4][...]
     both_twists, odd_twist = sent_twists(twist)
     pairs = [
         tuple(arrived[pl.ds(2 * p + c, 256, stride=4), :] for c in range(2)) for p in range(2)
@@ -408,7 +421,13 @@
     table = tables()
     tx, z, y = lax.axis_index("tx"), lax.axis_index("rx"), lax.axis_index("freq")
 
-    sent = call(send_kernel, (32, 2, 2, 8, 128), spectrum)
+    sent = call(
+        send_kernel,
+        (32, 2, 2, 8, 128),
+        pltpu.with_memory_space_constraint(spectrum, pltpu.HBM),
+        apart=1,
+        scratch=[(2, 2, 256, 128), pltpu.SemaphoreType.DMA((4,))],
+    )
     arrived = exchange(sent.reshape(64, 16, 128), ("rx", "freq"))
 
     turn = turns(wavenumber, tx, z, y)
@@ -438,15 +457,22 @@
         flops=10**9,
     )
     columns = exchange(pairs.reshape(512, 2, 128), ("tx", "rx", "freq")).reshape(1024, 128)
-    given = [*table["long"], table["twist_sent"], table["mix"]]
+    given = [*table["long"][1:], table["twist_sent"], table["mix"]]
+    given.append(pltpu.with_memory_space_constraint(jnp.asarray(table["long"][0]), pltpu.HBM))
     back, *resid = call(
         middle_kernel,
         [(1024, 128)] + [(128, 128)] * 8,
         columns,
         *echoes,
         *given,
-        near=15,
-        scratch=[(8, 192, 128), (8, 128, 128)],
+        near=14,
+        apart=1,
+        scratch=[
+            (8, 192, 128),
+            (8, 128, 128),
+            pltpu.VMEM((256, 256), bf16),
+            pltpu.SemaphoreType.DMA,
+        ],
         place=place,
         flops=3 * 10**9,
     )

time: 192 us -> 192 us (level)
  Pallas kernels: 10.8 us -> 13.2 us
  local copies, waits for them, and re-layouts: 4.31 us -> 2.37 us
    pallas_call x7, Pallas kernels: 10.8 us -> 13.2 us  [call(): pl.pallas_call(kernel, out_shape=outs if far else [pltpu.VMEM(o.shape, o....]
    unnamed x33 -> x29, local copies, waits for them, and re-layouts: 4.06 us -> 2.13 us
where the time goes in v5:
time: 192 us; the launch traced here: 190 us
  starting transfers between devices  94.1 us (49%)
  waiting for transfers between devices  78.3 us (41%)
  Pallas kernels  13.2 us (7%)
  local copies, waits for them, and re-layouts  2.37 us (1%)
    all_to_all x4, waiting for transfers between devices, exchange(): return lax.all_to_all(value, axes, split_axis=0, concat_axis=0, tiled=True)  66.2 us
    all_to_all x4, starting transfers between devices, exchange(): return lax.all_to_all(value, axes, split_axis=0, concat_axis=0, tiled=True)  50.9 us
    ppermute x14, starting transfers between devices, along_tx(): lax.ppermute(pieces[step], 'tx', [(i, (i + step) % 8) for i in range(8)])  43.2 us
    pallas_call x7, Pallas kernels, call(): pl.pallas_call(kernel, out_shape=outs if far else [pltpu.VMEM(o.shape, o....  13.2 us
    ppermute x14, waiting for transfers between devices, along_tx(): lax.ppermute(pieces[step], 'tx', [(i, (i + step) % 8) for i in range(8)])  12.1 us
  transfers between devices with their start and end apart: 18, of which 12 were waited for; matrix products, arithmetic and copies ran while one was open for 1% of the time, Pallas kernels for 1%

profile of v5, /device:TPU:1, one launch (start us, length us, event | category | flops | bytes accessed | tf_op | source)
XLA Modules:
  0.0 190.0 jit_solution(9989518115604248835)
XLA Ops:
  2.6 19.4 %all-to-all-start = ((f32[64,16,128]{2,1,0:T(8,128)}), f32[64,16,128]{2,1,0:T(8,128)S(1)}, u32[]{:S(2)}, u32[]{:S(2)}) async-start(f32[64,16,128]{2,1,0:T(8,128)} %bitcast.1), calls=%async_computation | async-start | bytes 1048576 | tf_op jit(solution)/shard_map/all_to_all | solution.py:391
  24.4 2.1 %collective-permute-start = (f32[192,128]{1,0:T(8,128)S(1)}, f32[192,128]{1,0:T(8,128)S(1)}, u32[]{:S(2)}, u32[]{:S(2)}) collective-permute-start(f32[192,128]{1,0:T(8,128)S(1)} %get-tuple-element.20), channel_id=1, source_target_pairs={{0,64},{64,128},{128,192},{192,256},{256,320},{320,384},{384,448},... | collective-permute-start | bytes 294920 | tf_op jit(solution)/shard_map/ppermute | solution.py:397
  26.5 3.1 %collective-permute-start.1 = (f32[192,128]{1,0:T(8,128)S(1)}, f32[192,128]{1,0:T(8,128)S(1)}, u32[]{:S(2)}, u32[]{:S(2)}) collective-permute-start(f32[192,128]{1,0:T(8,128)S(1)} %get-tuple-element.21), channel_id=1, source_target_pairs={{0,128},{64,192},{128,256},{192,320},{256,384},{320,448},{384,0},{... | collective-permute-start | bytes 294920 | tf_op jit(solution)/shard_map/ppermute | solution.py:397
  29.6 3.5 %collective-permute-start.2 = (f32[192,128]{1,0:T(8,128)S(1)}, f32[192,128]{1,0:T(8,128)S(1)}, u32[]{:S(2)}, u32[]{:S(2)}) collective-permute-start(f32[192,128]{1,0:T(8,128)S(1)} %get-tuple-element.22), channel_id=1, source_target_pairs={{0,192},{64,256},{128,320},{192,384},{256,448},{320,0},{384,64},{4... | collective-permute-start | bytes 294920 | tf_op jit(solution)/shard_map/ppermute | solution.py:397
  37.0 15.0 %all-to-all-done = f32[64,16,128]{2,1,0:T(8,128)S(1)} async-done(((f32[64,16,128]{2,1,0:T(8,128)}), f32[64,16,128]{2,1,0:T(8,128)S(1)}, u32[]{:S(2)}, u32[]{:S(2)}) %all-to-all-start) | async-done | bytes 524320 | tf_op jit(solution)/shard_map/all_to_all | solution.py:391
  52.0 2.1 %shard_map.160 = f32[1024,128]{1,0:T(8,128)} custom-call(f32[16,4,2,8,128]{4,3,2,1,0:T(8,128)S(1)} %bitcast.12, f32[2,16,4,8,128]{4,3,2,1,0:T(8,128)S(1)} %pad_maximum_fusion.turn, f32[2,16,8,128]{3,2,1,0:T(8,128)S(1)} %copy-done.7, bf16[256,256]{1,0:T(8,128)(2,1)S(1)} %copy-done.6, bf16[256,256]{1,0:T(8,128)(2,1)S(1)} %copy-done.5, ...), custom_call_target="tpu_custom_call" | custom-call | flops 1000000000 | bytes 2359296 | tf_op jit(solution)/shard_map/pallas_call | solution.py:378
  54.1 13.7 %all-to-all-start.1 = ((f32[512,2,128]{2,1,0:T(2,128)}), f32[512,2,128]{2,1,0:T(2,128)S(1)}, u32[]{:S(2)}, u32[]{:S(2)}) async-start(f32[512,2,128]{2,1,0:T(2,128)} %bitcast.5), calls=%async_computation.1 | async-start | bytes 1048576 | tf_op jit(solution)/shard_map/all_to_all | solution.py:391
  67.8 4.8 %collective-permute-start.3 = (f32[192,128]{1,0:T(8,128)S(1)}, f32[192,128]{1,0:T(8,128)S(1)}, u32[]{:S(2)}, u32[]{:S(2)}) collective-permute-start(f32[192,128]{1,0:T(8,128)S(1)} %get-tuple-element.23), channel_id=1, source_target_pairs={{0,256},{64,320},{128,384},{192,448},{256,0},{320,64},{384,128},{4... | collective-permute-start | bytes 294920 | tf_op jit(solution)/shard_map/ppermute | solution.py:397
  72.6 3.3 %collective-permute-start.4 = (f32[192,128]{1,0:T(8,128)S(1)}, f32[192,128]{1,0:T(8,128)S(1)}, u32[]{:S(2)}, u32[]{:S(2)}) collective-permute-start(f32[192,128]{1,0:T(8,128)S(1)} %get-tuple-element.24), channel_id=1, source_target_pairs={{0,320},{64,384},{128,448},{192,0},{256,64},{320,128},{384,192},{4... | collective-permute-start | bytes 294920 | tf_op jit(solution)/shard_map/ppermute | solution.py:397
  76.0 5.3 %collective-permute-start.5 = (f32[192,128]{1,0:T(8,128)S(1)}, f32[192,128]{1,0:T(8,128)S(1)}, u32[]{:S(2)}, u32[]{:S(2)}) collective-permute-start(f32[192,128]{1,0:T(8,128)S(1)} %get-tuple-element.25), channel_id=1, source_target_pairs={{0,384},{64,448},{128,0},{192,64},{256,128},{320,192},{384,256},{4... | collective-permute-start | bytes 294920 | tf_op jit(solution)/shard_map/ppermute | solution.py:397
  83.9 2.1 %collective-permute-done.6.refs_7_ = f32[192,128]{1,0:T(8,128)S(1)} collective-permute-done((f32[192,128]{1,0:T(8,128)S(1)}, f32[192,128]{1,0:T(8,128)S(1)}, u32[]{:S(2)}, u32[]{:S(2)}) %collective-permute-start.6) | collective-permute-done | bytes 98336 | tf_op jit(solution)/shard_map/ppermute | solution.py:397
  86.0 15.3 %all-to-all-done.1 = f32[512,2,128]{2,1,0:T(2,128)S(1)} async-done(((f32[512,2,128]{2,1,0:T(2,128)}), f32[512,2,128]{2,1,0:T(2,128)S(1)}, u32[]{:S(2)}, u32[]{:S(2)}) %all-to-all-start.1) | async-done | bytes 524320 | tf_op jit(solution)/shard_map/all_to_all | solution.py:391
  101.3 4.1 %shard_map.161 = (f32[1024,128]{1,0:T(8,128)}, f32[128,128]{1,0:T(8,128)S(1)}, f32[128,128]{1,0:T(8,128)S(1)}, f32[128,128]{1,0:T(8,128)S(1)}, f32[128,128]{1,0:...) custom-call(s32[1]{0:T(128)} %bitcast.place, ...), custom_call_target="tpu_custom_call" | custom-call | flops 3000000000 | bytes 3276800 | tf_op jit(solution)/shard_map/pallas_call | solution.py:378
  105.4 11.0 %all-to-all-start.2 = ((f32[512,2,128]{2,1,0:T(2,128)}), f32[512,2,128]{2,1,0:T(2,128)S(1)}, u32[]{:S(2)}, u32[]{:S(2)}) async-start(f32[512,2,128]{2,1,0:T(2,128)} %bitcast.7), calls=%async_computation.2 | async-start | bytes 1048576 | tf_op jit(solution)/shard_map/all_to_all | solution.py:391
  118.1 3.1 %collective-permute-start.8 = (f32[128,128]{1,0:T(8,128)S(1)}, f32[128,128]{1,0:T(8,128)S(1)}, u32[]{:S(2)}, u32[]{:S(2)}) collective-permute-start(f32[128,128]{1,0:T(8,128)S(1)} %get-tuple-element.30), channel_id=1, source_target_pairs={{0,128},{64,192},{128,256},{192,320},{256,384},{320,448},{384,0},{... | collective-permute-start | bytes 196616 | tf_op jit(solution)/shard_map/ppermute | solution.py:397
  121.2 3.6 %collective-permute-start.9 = (f32[128,128]{1,0:T(8,128)S(1)}, f32[128,128]{1,0:T(8,128)S(1)}, u32[]{:S(2)}, u32[]{:S(2)}) collective-permute-start(f32[128,128]{1,0:T(8,128)S(1)} %get-tuple-element.31), channel_id=1, source_target_pairs={{0,192},{64,256},{128,320},{192,384},{256,448},{320,0},{384,64},{4... | collective-permute-start | bytes 196616 | tf_op jit(solution)/shard_map/ppermute | solution.py:397
  124.7 5.6 %collective-permute-start.10 = (f32[128,128]{1,0:T(8,128)S(1)}, f32[128,128]{1,0:T(8,128)S(1)}, u32[]{:S(2)}, u32[]{:S(2)}) collective-permute-start(f32[128,128]{1,0:T(8,128)S(1)} %get-tuple-element.32), channel_id=1, source_target_pairs={{0,256},{64,320},{128,384},{192,448},{256,0},{320,64},{384,128},{4... | collective-permute-start | bytes 196616 | tf_op jit(solution)/shard_map/ppermute | solution.py:397
  130.9 2.1 %collective-permute-done.10.refs_4_ = f32[128,128]{1,0:T(8,128)S(1)} collective-permute-done((f32[128,128]{1,0:T(8,128)S(1)}, f32[128,128]{1,0:T(8,128)S(1)}, u32[]{:S(2)}, u32[]{:S(2)}) %collective-permute-start.10) | collective-permute-done | bytes 65568 | tf_op jit(solution)/shard_map/ppermute | solution.py:397
  133.0 17.1 %all-to-all-done.2 = f32[512,2,128]{2,1,0:T(2,128)S(1)} async-done(((f32[512,2,128]{2,1,0:T(2,128)}), f32[512,2,128]{2,1,0:T(2,128)S(1)}, u32[]{:S(2)}, u32[]{:S(2)}) %all-to-all-start.2) | async-done | bytes 524320 | tf_op jit(solution)/shard_map/all_to_all | solution.py:391
  151.9 6.8 %all-to-all-start.3 = ((f32[64,16,128]{2,1,0:T(8,128)}), f32[64,16,128]{2,1,0:T(8,128)S(1)}, u32[]{:S(2)}, u32[]{:S(2)}) async-start(f32[64,16,128]{2,1,0:T(8,128)} %bitcast.9), calls=%async_computation.3 | async-start | bytes 1048576 | tf_op jit(solution)/shard_map/all_to_all | solution.py:391
  158.7 3.5 %collective-permute-start.11 = (f32[128,128]{1,0:T(8,128)S(1)}, f32[128,128]{1,0:T(8,128)S(1)}, u32[]{:S(2)}, u32[]{:S(2)}) collective-permute-start(f32[128,128]{1,0:T(8,128)S(1)} %get-tuple-element.33), channel_id=1, source_target_pairs={{0,320},{64,384},{128,448},{192,0},{256,64},{320,128},{384,192},{4... | collective-permute-start | bytes 196616 | tf_op jit(solution)/shard_map/ppermute | solution.py:397
  162.2 2.4 %collective-permute-start.12 = (f32[128,128]{1,0:T(8,128)S(1)}, f32[128,128]{1,0:T(8,128)S(1)}, u32[]{:S(2)}, u32[]{:S(2)}) collective-permute-start(f32[128,128]{1,0:T(8,128)S(1)} %get-tuple-element.34), channel_id=1, source_target_pairs={{0,384},{64,448},{128,0},{192,64},{256,128},{320,192},{384,256},{4... | collective-permute-start | bytes 196616 | tf_op jit(solution)/shard_map/ppermute | solution.py:397
  165.9 2.0 %collective-permute-done.12.refs_6_ = f32[128,128]{1,0:T(8,128)S(1)} collective-permute-done((f32[128,128]{1,0:T(8,128)S(1)}, f32[128,128]{1,0:T(8,128)S(1)}, u32[]{:S(2)}, u32[]{:S(2)}) %collective-permute-start.12) | collective-permute-done | bytes 65568 | tf_op jit(solution)/shard_map/ppermute | solution.py:397
  170.3 18.9 %all-to-all-done.3 = f32[64,16,128]{2,1,0:T(8,128)S(1)} async-done(((f32[64,16,128]{2,1,0:T(8,128)}), f32[64,16,128]{2,1,0:T(8,128)S(1)}, u32[]{:S(2)}, u32[]{:S(2)}) %all-to-all-start.3) | async-done | bytes 524320 | tf_op jit(solution)/shard_map/all_to_all | solution.py:391
  (57 shorter events, 19.5 us)
Async XLA Ops:
  2.6 49.5 %all-to-all-start = ((f32[64,16,128]{2,1,0:T(8,128)}), f32[64,16,128]{2,1,0:T(8,128)S(1)}, u32[]{:S(2)}, u32[]{:S(2)}) async-start(f32[64,16,128]{2,1,0:T(8,128)} %bitcast.1), calls=%async_computation | async-start | bytes 1048576 | tf_op jit(solution)/shard_map/all_to_all | solution.py:391
  24.4 10.8 %collective-permute-start = (f32[192,128]{1,0:T(8,128)S(1)}, f32[192,128]{1,0:T(8,128)S(1)}, u32[]{:S(2)}, u32[]{:S(2)}) collective-permute-start(f32[192,128]{1,0:T(8,128)S(1)} %get-tuple-element.20), channel_id=1, source_target_pairs={{0,64},{64,128},{128,192},{192,256},{256,320},{320,384},{384,448},... | collective-permute-start | bytes 294920 | tf_op jit(solution)/shard_map/ppermute | solution.py:397
  26.5 8.7 %collective-permute-start.1 = (f32[192,128]{1,0:T(8,128)S(1)}, f32[192,128]{1,0:T(8,128)S(1)}, u32[]{:S(2)}, u32[]{:S(2)}) collective-permute-start(f32[192,128]{1,0:T(8,128)S(1)} %get-tuple-element.21), channel_id=1, source_target_pairs={{0,128},{64,192},{128,256},{192,320},{256,384},{320,448},{384,0},{... | collective-permute-start | bytes 294920 | tf_op jit(solution)/shard_map/ppermute | solution.py:397
  29.6 7.4 %collective-permute-start.2 = (f32[192,128]{1,0:T(8,128)S(1)}, f32[192,128]{1,0:T(8,128)S(1)}, u32[]{:S(2)}, u32[]{:S(2)}) collective-permute-start(f32[192,128]{1,0:T(8,128)S(1)} %get-tuple-element.22), channel_id=1, source_target_pairs={{0,192},{64,256},{128,320},{192,384},{256,448},{320,0},{384,64},{4... | collective-permute-start | bytes 294920 | tf_op jit(solution)/shard_map/ppermute | solution.py:397
  54.1 47.1 %copy-start.4 = (f32[2,256,128]{2,1,0:T(8,128)S(1)}, f32[2,256,128]{2,1,0:T(8,128)}, u32[]{:S(2)}) copy-start(f32[2,256,128]{2,1,0:T(8,128)} %constant.85.clone.refs_11_) | copy-start | bytes 786436
  54.1 47.1 %copy-start.8 = (bf16[256,256]{1,0:T(8,128)(2,1)S(1)}, bf16[256,256]{1,0:T(8,128)(2,1)}, u32[]{:S(2)}) copy-start(bf16[256,256]{1,0:T(8,128)(2,1)} %constant.86.clone.refs_12_) | copy-start | bytes 393220
  54.1 47.1 %copy-start.9 = (bf16[256,256]{1,0:T(8,128)(2,1)S(1)}, bf16[256,256]{1,0:T(8,128)(2,1)}, u32[]{:S(2)}) copy-start(bf16[256,256]{1,0:T(8,128)(2,1)} %constant.84.clone.refs_10_) | copy-start | bytes 393220
  54.1 47.1 %copy-start.10 = (bf16[256,256]{1,0:T(8,128)(2,1)S(1)}, bf16[256,256]{1,0:T(8,128)(2,1)}, u32[]{:S(2)}) copy-start(bf16[256,256]{1,0:T(8,128)(2,1)} %constant.83.clone.refs_9_) | copy-start | bytes 393220
  54.1 47.2 %copy-start.11 = (bf16[256,256]{1,0:T(8,128)(2,1)S(1)}, bf16[256,256]{1,0:T(8,128)(2,1)}, u32[]{:S(2)}) copy-start(bf16[256,256]{1,0:T(8,128)(2,1)} %constant.82.clone.refs_8_) | copy-start | bytes 393220
  54.1 47.1 %all-to-all-start.1 = ((f32[512,2,128]{2,1,0:T(2,128)}), f32[512,2,128]{2,1,0:T(2,128)S(1)}, u32[]{:S(2)}, u32[]{:S(2)}) async-start(f32[512,2,128]{2,1,0:T(2,128)} %bitcast.5), calls=%async_computation.1 | async-start | bytes 1048576 | tf_op jit(solution)/shard_map/all_to_all | solution.py:391
  67.8 13.5 %collective-permute-start.3 = (f32[192,128]{1,0:T(8,128)S(1)}, f32[192,128]{1,0:T(8,128)S(1)}, u32[]{:S(2)}, u32[]{:S(2)}) collective-permute-start(f32[192,128]{1,0:T(8,128)S(1)} %get-tuple-element.23), channel_id=1, source_target_pairs={{0,256},{64,320},{128,384},{192,448},{256,0},{320,64},{384,128},{4... | collective-permute-start | bytes 294920 | tf_op jit(solution)/shard_map/ppermute | solution.py:397
  72.6 9.4 %collective-permute-start.4 = (f32[192,128]{1,0:T(8,128)S(1)}, f32[192,128]{1,0:T(8,128)S(1)}, u32[]{:S(2)}, u32[]{:S(2)}) collective-permute-start(f32[192,128]{1,0:T(8,128)S(1)} %get-tuple-element.24), channel_id=1, source_target_pairs={{0,320},{64,384},{128,448},{192,0},{256,64},{320,128},{384,192},{4... | collective-permute-start | bytes 294920 | tf_op jit(solution)/shard_map/ppermute | solution.py:397
  76.0 8.0 %collective-permute-start.5 = (f32[192,128]{1,0:T(8,128)S(1)}, f32[192,128]{1,0:T(8,128)S(1)}, u32[]{:S(2)}, u32[]{:S(2)}) collective-permute-start(f32[192,128]{1,0:T(8,128)S(1)} %get-tuple-element.25), channel_id=1, source_target_pairs={{0,384},{64,448},{128,0},{192,64},{256,128},{320,192},{384,256},{4... | collective-permute-start | bytes 294920 | tf_op jit(solution)/shard_map/ppermute | solution.py:397
  81.3 4.7 %collective-permute-start.6 = (f32[192,128]{1,0:T(8,128)S(1)}, f32[192,128]{1,0:T(8,128)S(1)}, u32[]{:S(2)}, u32[]{:S(2)}) collective-permute-start(f32[192,128]{1,0:T(8,128)S(1)} %get-tuple-element.26), channel_id=1, source_target_pairs={{0,448},{64,0},{128,64},{192,128},{256,192},{320,256},{384,320},{4... | collective-permute-start | bytes 294920 | tf_op jit(solution)/shard_map/ppermute | solution.py:397
  105.4 44.6 %all-to-all-start.2 = ((f32[512,2,128]{2,1,0:T(2,128)}), f32[512,2,128]{2,1,0:T(2,128)S(1)}, u32[]{:S(2)}, u32[]{:S(2)}) async-start(f32[512,2,128]{2,1,0:T(2,128)} %bitcast.7), calls=%async_computation.2 | async-start | bytes 1048576 | tf_op jit(solution)/shard_map/all_to_all | solution.py:391
  116.4 13.9 %collective-permute-start.7 = (f32[128,128]{1,0:T(8,128)S(1)}, f32[128,128]{1,0:T(8,128)S(1)}, u32[]{:S(2)}, u32[]{:S(2)}) collective-permute-start(f32[128,128]{1,0:T(8,128)S(1)} %get-tuple-element.29), channel_id=1, source_target_pairs={{0,64},{64,128},{128,192},{192,256},{256,320},{320,384},{384,448},... | collective-permute-start | bytes 196616 | tf_op jit(solution)/shard_map/ppermute | solution.py:397
  118.1 12.3 %collective-permute-start.8 = (f32[128,128]{1,0:T(8,128)S(1)}, f32[128,128]{1,0:T(8,128)S(1)}, u32[]{:S(2)}, u32[]{:S(2)}) collective-permute-start(f32[128,128]{1,0:T(8,128)S(1)} %get-tuple-element.30), channel_id=1, source_target_pairs={{0,128},{64,192},{128,256},{192,320},{256,384},{320,448},{384,0},{... | collective-permute-start | bytes 196616 | tf_op jit(solution)/shard_map/ppermute | solution.py:397
  121.2 9.7 %collective-permute-start.9 = (f32[128,128]{1,0:T(8,128)S(1)}, f32[128,128]{1,0:T(8,128)S(1)}, u32[]{:S(2)}, u32[]{:S(2)}) collective-permute-start(f32[128,128]{1,0:T(8,128)S(1)} %get-tuple-element.31), channel_id=1, source_target_pairs={{0,192},{64,256},{128,320},{192,384},{256,448},{320,0},{384,64},{4... | collective-permute-start | bytes 196616 | tf_op jit(solution)/shard_map/ppermute | solution.py:397
  124.7 8.2 %collective-permute-start.10 = (f32[128,128]{1,0:T(8,128)S(1)}, f32[128,128]{1,0:T(8,128)S(1)}, u32[]{:S(2)}, u32[]{:S(2)}) collective-permute-start(f32[128,128]{1,0:T(8,128)S(1)} %get-tuple-element.32), channel_id=1, source_target_pairs={{0,256},{64,320},{128,384},{192,448},{256,0},{320,64},{384,128},{4... | collective-permute-start | bytes 196616 | tf_op jit(solution)/shard_map/ppermute | solution.py:397
  151.9 37.2 %all-to-all-start.3 = ((f32[64,16,128]{2,1,0:T(8,128)}), f32[64,16,128]{2,1,0:T(8,128)S(1)}, u32[]{:S(2)}, u32[]{:S(2)}) async-start(f32[64,16,128]{2,1,0:T(8,128)} %bitcast.9), calls=%async_computation.3 | async-start | bytes 1048576 | tf_op jit(solution)/shard_map/all_to_all | solution.py:391
  158.7 7.2 %collective-permute-start.11 = (f32[128,128]{1,0:T(8,128)S(1)}, f32[128,128]{1,0:T(8,128)S(1)}, u32[]{:S(2)}, u32[]{:S(2)}) collective-permute-start(f32[128,128]{1,0:T(8,128)S(1)} %get-tuple-element.33), channel_id=1, source_target_pairs={{0,320},{64,384},{128,448},{192,0},{256,64},{320,128},{384,192},{4... | collective-permute-start | bytes 196616 | tf_op jit(solution)/shard_map/ppermute | solution.py:397
  162.2 5.7 %collective-permute-start.12 = (f32[128,128]{1,0:T(8,128)S(1)}, f32[128,128]{1,0:T(8,128)S(1)}, u32[]{:S(2)}, u32[]{:S(2)}) collective-permute-start(f32[128,128]{1,0:T(8,128)S(1)} %get-tuple-element.34), channel_id=1, source_target_pairs={{0,384},{64,448},{128,0},{192,64},{256,128},{320,192},{384,256},{4... | collective-permute-start | bytes 196616 | tf_op jit(solution)/shard_map/ppermute | solution.py:397
  164.5 24.6 %copy-start = (f32[2,2,256,128]{3,2,1,0:T(8,128)S(1)}, f32[2,2,256,128]{3,2,1,0:T(8,128)}, u32[]{:S(2)}) copy-start(f32[2,2,256,128]{3,2,1,0:T(8,128)} %spectrum.3) | copy-start | bytes 1572868
  164.6 4.3 %collective-permute-start.13 = (f32[128,128]{1,0:T(8,128)S(1)}, f32[128,128]{1,0:T(8,128)S(1)}, u32[]{:S(2)}, u32[]{:S(2)}) collective-permute-start(f32[128,128]{1,0:T(8,128)S(1)} %get-tuple-element.35), channel_id=1, source_target_pairs={{0,448},{64,0},{128,64},{192,128},{256,192},{320,256},{384,320},{4... | collective-permute-start | bytes 196616 | tf_op jit(solution)/shard_map/ppermute | solution.py:397
  (8 other events, 73.8 us)

commit v6 on v4

--- a/solution.py
+++ b/solution.py
@@ -299,9 +299,18 @@
     return whole, turned(quarter, quarter)
 
 
+def mix_table():
+    row = lax.broadcasted_iota(jnp.int32, (256, 256), 0)
+    column = lax.broadcasted_iota(jnp.int32, (256, 256), 1)
+    same = ((row >> 2) & 1) * 16 + ((row >> 3) & 15) == (column & 31)
+    power = ((row & 3) * ((column >> 5) & 3) + (row >> 7) - (column >> 7)) & 3
+    value = jnp.where(power & 1 == 1, 0.0, jnp.where(power == 0, 1.0, -1.0))
+    return jnp.where(same, value, 0.0).astype(bf16)
+
+
 def middle_kernel(place, arrived, *refs):
-    echoes, given, out, sent = refs[:8], refs[8:14], refs[14], refs[15:23]
-    held, resid = refs[23:]
+    echoes, given, out, sent = refs[:8], refs[8:10], refs[10], refs[11:19]
+    held, resid = refs[19:]
     for step in range(8):
         held[(place[0] + 8 - step) & 7] = echoes[step][...]
     parts = []
@@ -311,7 +320,8 @@
             pieces = [held[2 * t1 + odd, k * 64 : (k + 1) * 64, :] for t1 in range(4)]
             rows += swap_groups(pieces, 32)
         parts.append(jnp.concatenate(rows, 0))
-    long, twist, mix = given[:4], given[4], given[5][...]
+    long = [given[0].at[pl.ds(256 * k, 256)] for k in range(4)]
+    twist, mix = given[1], mix_table()
     both_twists, odd_twist = sent_twists(twist)
     pairs = [
         tuple(arrived[pl.ds(2 * p + c, 256, stride=4), :] for c in range(2)) for p in range(2)
@@ -438,14 +448,14 @@
         flops=10**9,
     )
     columns = exchange(pairs.reshape(512, 2, 128), ("tx", "rx", "freq")).reshape(1024, 128)
-    given = [*table["long"], table["twist_sent"], table["mix"]]
+    given = [np.concatenate(table["long"], 0), table["twist_sent"]]
     back, *resid = call(
         middle_kernel,
         [(1024, 128)] + [(128, 128)] * 8,
         columns,
         *echoes,
         *given,
-        near=15,
+        near=11,
         scratch=[(8, 192, 128), (8, 128, 128)],
         place=place,
         flops=3 * 10**9,

time: 192 us -> 191 us (level)
    unnamed x33 -> x25, local copies, waits for them, and re-layouts: 4.06 us -> 3.15 us
where the time goes in v6:
time: 191 us; the launch traced here: 188 us
  starting transfers between devices  94 us (49%)
  waiting for transfers between devices  78.1 us (41%)
  Pallas kernels  10.9 us (6%)
  local copies, waits for them, and re-layouts  3.39 us (2%)
    all_to_all x4, waiting for transfers between devices, exchange(): return lax.all_to_all(value, axes, split_axis=0, concat_axis=0, tiled=True)  66.1 us
    all_to_all x4, starting transfers between devices, exchange(): return lax.all_to_all(value, axes, split_axis=0, concat_axis=0, tiled=True)  50.6 us
    ppermute x14, starting transfers between devices, along_tx(): lax.ppermute(pieces[step], 'tx', [(i, (i + step) % 8) for i in range(8)])  43.4 us
    ppermute x14, waiting for transfers between devices, along_tx(): lax.ppermute(pieces[step], 'tx', [(i, (i + step) % 8) for i in range(8)])  12 us
    pallas_call x7, Pallas kernels, call(): pl.pallas_call(kernel, out_shape=outs if far else [pltpu.VMEM(o.shape, o....  10.9 us
  transfers between devices with their start and end apart: 18, of which 12 were waited for; matrix products, arithmetic and copies ran while one was open for 1% of the time, Pallas kernels for 1%

profile of v6, /device:TPU:1, one launch (start us, length us, event | category | flops | bytes accessed | tf_op | source)
XLA Modules:
  0.0 188.5 jit_solution(4587820364623759060)
XLA Ops:
  2.5 19.4 %all-to-all-start = ((f32[64,16,128]{2,1,0:T(8,128)}), f32[64,16,128]{2,1,0:T(8,128)S(1)}, u32[]{:S(2)}, u32[]{:S(2)}) async-start(f32[64,16,128]{2,1,0:T(8,128)} %bitcast.1), calls=%async_computation | async-start | bytes 1048576 | tf_op jit(solution)/shard_map/all_to_all | solution.py:388
  24.3 2.1 %collective-permute-start = (f32[192,128]{1,0:T(8,128)S(1)}, f32[192,128]{1,0:T(8,128)S(1)}, u32[]{:S(2)}, u32[]{:S(2)}) collective-permute-start(f32[192,128]{1,0:T(8,128)S(1)} %get-tuple-element.20), channel_id=1, source_target_pairs={{0,64},{64,128},{128,192},{192,256},{256,320},{320,384},{384,448},... | collective-permute-start | bytes 294920 | tf_op jit(solution)/shard_map/ppermute | solution.py:394
  26.4 3.1 %collective-permute-start.1 = (f32[192,128]{1,0:T(8,128)S(1)}, f32[192,128]{1,0:T(8,128)S(1)}, u32[]{:S(2)}, u32[]{:S(2)}) collective-permute-start(f32[192,128]{1,0:T(8,128)S(1)} %get-tuple-element.21), channel_id=1, source_target_pairs={{0,128},{64,192},{128,256},{192,320},{256,384},{320,448},{384,0},{... | collective-permute-start | bytes 294920 | tf_op jit(solution)/shard_map/ppermute | solution.py:394
  29.5 3.5 %collective-permute-start.2 = (f32[192,128]{1,0:T(8,128)S(1)}, f32[192,128]{1,0:T(8,128)S(1)}, u32[]{:S(2)}, u32[]{:S(2)}) collective-permute-start(f32[192,128]{1,0:T(8,128)S(1)} %get-tuple-element.22), channel_id=1, source_target_pairs={{0,192},{64,256},{128,320},{192,384},{256,448},{320,0},{384,64},{4... | collective-permute-start | bytes 294920 | tf_op jit(solution)/shard_map/ppermute | solution.py:394
  37.0 15.0 %all-to-all-done = f32[64,16,128]{2,1,0:T(8,128)S(1)} async-done(((f32[64,16,128]{2,1,0:T(8,128)}), f32[64,16,128]{2,1,0:T(8,128)S(1)}, u32[]{:S(2)}, u32[]{:S(2)}) %all-to-all-start) | async-done | bytes 524320 | tf_op jit(solution)/shard_map/all_to_all | solution.py:388
  52.0 2.1 %shard_map.124 = f32[1024,128]{1,0:T(8,128)} custom-call(f32[16,4,2,8,128]{4,3,2,1,0:T(8,128)S(1)} %bitcast.12, f32[2,16,4,8,128]{4,3,2,1,0:T(8,128)S(1)} %pad_maximum_fusion.turn, f32[2,16,8,128]{3,2,1,0:T(8,128)S(1)} %copy-done.9, bf16[256,256]{1,0:T(8,128)(2,1)S(1)} %copy-done.8, bf16[256,256]{1,0:T(8,128)(2,1)S(1)} %copy-done.7, ...), custom_call_target="tpu_custom_call" | custom-call | flops 1000000000 | bytes 2359296 | tf_op jit(solution)/shard_map/pallas_call | solution.py:375
  54.1 13.7 %all-to-all-start.1 = ((f32[512,2,128]{2,1,0:T(2,128)}), f32[512,2,128]{2,1,0:T(2,128)S(1)}, u32[]{:S(2)}, u32[]{:S(2)}) async-start(f32[512,2,128]{2,1,0:T(2,128)} %bitcast.5), calls=%async_computation.1 | async-start | bytes 1048576 | tf_op jit(solution)/shard_map/all_to_all | solution.py:388
  67.7 4.8 %collective-permute-start.3 = (f32[192,128]{1,0:T(8,128)S(1)}, f32[192,128]{1,0:T(8,128)S(1)}, u32[]{:S(2)}, u32[]{:S(2)}) collective-permute-start(f32[192,128]{1,0:T(8,128)S(1)} %get-tuple-element.23), channel_id=1, source_target_pairs={{0,256},{64,320},{128,384},{192,448},{256,0},{320,64},{384,128},{4... | collective-permute-start | bytes 294920 | tf_op jit(solution)/shard_map/ppermute | solution.py:394
  72.5 3.3 %collective-permute-start.4 = (f32[192,128]{1,0:T(8,128)S(1)}, f32[192,128]{1,0:T(8,128)S(1)}, u32[]{:S(2)}, u32[]{:S(2)}) collective-permute-start(f32[192,128]{1,0:T(8,128)S(1)} %get-tuple-element.24), channel_id=1, source_target_pairs={{0,320},{64,384},{128,448},{192,0},{256,64},{320,128},{384,192},{4... | collective-permute-start | bytes 294920 | tf_op jit(solution)/shard_map/ppermute | solution.py:394
  75.9 5.3 %collective-permute-start.5 = (f32[192,128]{1,0:T(8,128)S(1)}, f32[192,128]{1,0:T(8,128)S(1)}, u32[]{:S(2)}, u32[]{:S(2)}) collective-permute-start(f32[192,128]{1,0:T(8,128)S(1)} %get-tuple-element.25), channel_id=1, source_target_pairs={{0,384},{64,448},{128,0},{192,64},{256,128},{320,192},{384,256},{4... | collective-permute-start | bytes 294920 | tf_op jit(solution)/shard_map/ppermute | solution.py:394
  83.8 2.1 %collective-permute-done.6.refs_7_ = f32[192,128]{1,0:T(8,128)S(1)} collective-permute-done((f32[192,128]{1,0:T(8,128)S(1)}, f32[192,128]{1,0:T(8,128)S(1)}, u32[]{:S(2)}, u32[]{:S(2)}) %collective-permute-start.6) | collective-permute-done | bytes 98336 | tf_op jit(solution)/shard_map/ppermute | solution.py:394
  85.9 15.3 %all-to-all-done.1 = f32[512,2,128]{2,1,0:T(2,128)S(1)} async-done(((f32[512,2,128]{2,1,0:T(2,128)}), f32[512,2,128]{2,1,0:T(2,128)S(1)}, u32[]{:S(2)}, u32[]{:S(2)}) %all-to-all-start.1) | async-done | bytes 524320 | tf_op jit(solution)/shard_map/all_to_all | solution.py:388
  101.2 2.9 %shard_map.125 = (f32[1024,128]{1,0:T(8,128)}, f32[128,128]{1,0:T(8,128)S(1)}, f32[128,128]{1,0:T(8,128)S(1)}, f32[128,128]{1,0:T(8,128)S(1)}, f32[128,128]{1,0:...) custom-call(s32[1]{0:T(128)} %bitcast.place, ...), custom_call_target="tpu_custom_call" | custom-call | flops 3000000000 | bytes 3145728 | tf_op jit(solution)/shard_map/pallas_call | solution.py:375
  104.1 10.8 %all-to-all-start.2 = ((f32[512,2,128]{2,1,0:T(2,128)}), f32[512,2,128]{2,1,0:T(2,128)S(1)}, u32[]{:S(2)}, u32[]{:S(2)}) async-start(f32[512,2,128]{2,1,0:T(2,128)} %bitcast.7), calls=%async_computation.2 | async-start | bytes 1048576 | tf_op jit(solution)/shard_map/all_to_all | solution.py:388
  116.5 3.1 %collective-permute-start.8 = (f32[128,128]{1,0:T(8,128)S(1)}, f32[128,128]{1,0:T(8,128)S(1)}, u32[]{:S(2)}, u32[]{:S(2)}) collective-permute-start(f32[128,128]{1,0:T(8,128)S(1)} %get-tuple-element.30), channel_id=1, source_target_pairs={{0,128},{64,192},{128,256},{192,320},{256,384},{320,448},{384,0},{... | collective-permute-start | bytes 196616 | tf_op jit(solution)/shard_map/ppermute | solution.py:394
  119.6 3.7 %collective-permute-start.9 = (f32[128,128]{1,0:T(8,128)S(1)}, f32[128,128]{1,0:T(8,128)S(1)}, u32[]{:S(2)}, u32[]{:S(2)}) collective-permute-start(f32[128,128]{1,0:T(8,128)S(1)} %get-tuple-element.31), channel_id=1, source_target_pairs={{0,192},{64,256},{128,320},{192,384},{256,448},{320,0},{384,64},{4... | collective-permute-start | bytes 196616 | tf_op jit(solution)/shard_map/ppermute | solution.py:394
  123.4 5.6 %collective-permute-start.10 = (f32[128,128]{1,0:T(8,128)S(1)}, f32[128,128]{1,0:T(8,128)S(1)}, u32[]{:S(2)}, u32[]{:S(2)}) collective-permute-start(f32[128,128]{1,0:T(8,128)S(1)} %get-tuple-element.32), channel_id=1, source_target_pairs={{0,256},{64,320},{128,384},{192,448},{256,0},{320,64},{384,128},{4... | collective-permute-start | bytes 196616 | tf_op jit(solution)/shard_map/ppermute | solution.py:394
  129.4 2.1 %collective-permute-done.10.refs_4_ = f32[128,128]{1,0:T(8,128)S(1)} collective-permute-done((f32[128,128]{1,0:T(8,128)S(1)}, f32[128,128]{1,0:T(8,128)S(1)}, u32[]{:S(2)}, u32[]{:S(2)}) %collective-permute-start.10) | collective-permute-done | bytes 65568 | tf_op jit(solution)/shard_map/ppermute | solution.py:394
  131.5 17.0 %all-to-all-done.2 = f32[512,2,128]{2,1,0:T(2,128)S(1)} async-done(((f32[512,2,128]{2,1,0:T(2,128)}), f32[512,2,128]{2,1,0:T(2,128)S(1)}, u32[]{:S(2)}, u32[]{:S(2)}) %all-to-all-start.2) | async-done | bytes 524320 | tf_op jit(solution)/shard_map/all_to_all | solution.py:388
  150.4 6.8 %all-to-all-start.3 = ((f32[64,16,128]{2,1,0:T(8,128)}), f32[64,16,128]{2,1,0:T(8,128)S(1)}, u32[]{:S(2)}, u32[]{:S(2)}) async-start(f32[64,16,128]{2,1,0:T(8,128)} %bitcast.9), calls=%async_computation.3 | async-start | bytes 1048576 | tf_op jit(solution)/shard_map/all_to_all | solution.py:388
  157.1 3.5 %collective-permute-start.11 = (f32[128,128]{1,0:T(8,128)S(1)}, f32[128,128]{1,0:T(8,128)S(1)}, u32[]{:S(2)}, u32[]{:S(2)}) collective-permute-start(f32[128,128]{1,0:T(8,128)S(1)} %get-tuple-element.33), channel_id=1, source_target_pairs={{0,320},{64,384},{128,448},{192,0},{256,64},{320,128},{384,192},{4... | collective-permute-start | bytes 196616 | tf_op jit(solution)/shard_map/ppermute | solution.py:394
  160.6 2.4 %collective-permute-start.12 = (f32[128,128]{1,0:T(8,128)S(1)}, f32[128,128]{1,0:T(8,128)S(1)}, u32[]{:S(2)}, u32[]{:S(2)}) collective-permute-start(f32[128,128]{1,0:T(8,128)S(1)} %get-tuple-element.34), channel_id=1, source_target_pairs={{0,384},{64,448},{128,0},{192,64},{256,128},{320,192},{384,256},{4... | collective-permute-start | bytes 196616 | tf_op jit(solution)/shard_map/ppermute | solution.py:394
  164.4 2.0 %collective-permute-done.12.refs_6_ = f32[128,128]{1,0:T(8,128)S(1)} collective-permute-done((f32[128,128]{1,0:T(8,128)S(1)}, f32[128,128]{1,0:T(8,128)S(1)}, u32[]{:S(2)}, u32[]{:S(2)}) %collective-permute-start.12) | collective-permute-done | bytes 65568 | tf_op jit(solution)/shard_map/ppermute | solution.py:394
  168.7 18.9 %all-to-all-done.3 = f32[64,16,128]{2,1,0:T(8,128)S(1)} async-done(((f32[64,16,128]{2,1,0:T(8,128)}), f32[64,16,128]{2,1,0:T(8,128)S(1)}, u32[]{:S(2)}, u32[]{:S(2)}) %all-to-all-start.3) | async-done | bytes 524320 | tf_op jit(solution)/shard_map/all_to_all | solution.py:388
  (53 shorter events, 19.3 us)
Async XLA Ops:
  2.5 20.2 %copy-start.2 = (f32[2,2,256,128]{3,2,1,0:T(8,128)S(1)}, f32[2,2,256,128]{3,2,1,0:T(8,128)}, u32[]{:S(2)}) copy-start(f32[2,2,256,128]{3,2,1,0:T(8,128)} %measured.1) | copy-start | bytes 1572868
  2.5 49.4 %all-to-all-start = ((f32[64,16,128]{2,1,0:T(8,128)}), f32[64,16,128]{2,1,0:T(8,128)S(1)}, u32[]{:S(2)}, u32[]{:S(2)}) async-start(f32[64,16,128]{2,1,0:T(8,128)} %bitcast.1), calls=%async_computation | async-start | bytes 1048576 | tf_op jit(solution)/shard_map/all_to_all | solution.py:388
  24.3 10.8 %collective-permute-start = (f32[192,128]{1,0:T(8,128)S(1)}, f32[192,128]{1,0:T(8,128)S(1)}, u32[]{:S(2)}, u32[]{:S(2)}) collective-permute-start(f32[192,128]{1,0:T(8,128)S(1)} %get-tuple-element.20), channel_id=1, source_target_pairs={{0,64},{64,128},{128,192},{192,256},{256,320},{320,384},{384,448},... | collective-permute-start | bytes 294920 | tf_op jit(solution)/shard_map/ppermute | solution.py:394
  26.4 8.7 %collective-permute-start.1 = (f32[192,128]{1,0:T(8,128)S(1)}, f32[192,128]{1,0:T(8,128)S(1)}, u32[]{:S(2)}, u32[]{:S(2)}) collective-permute-start(f32[192,128]{1,0:T(8,128)S(1)} %get-tuple-element.21), channel_id=1, source_target_pairs={{0,128},{64,192},{128,256},{192,320},{256,384},{320,448},{384,0},{... | collective-permute-start | bytes 294920 | tf_op jit(solution)/shard_map/ppermute | solution.py:394
  29.5 7.4 %collective-permute-start.2 = (f32[192,128]{1,0:T(8,128)S(1)}, f32[192,128]{1,0:T(8,128)S(1)}, u32[]{:S(2)}, u32[]{:S(2)}) collective-permute-start(f32[192,128]{1,0:T(8,128)S(1)} %get-tuple-element.22), channel_id=1, source_target_pairs={{0,192},{64,256},{128,320},{192,384},{256,448},{320,0},{384,64},{4... | collective-permute-start | bytes 294920 | tf_op jit(solution)/shard_map/ppermute | solution.py:394
  35.0 17.0 %copy-start.7 = (bf16[256,256]{1,0:T(8,128)(2,1)S(1)}, bf16[256,256]{1,0:T(8,128)(2,1)}, u32[]{:S(2)}) copy-start(bf16[256,256]{1,0:T(8,128)(2,1)} %constant.72.clone.table_low) | copy-start | bytes 393220
  35.0 17.0 %copy-start.8 = (bf16[256,256]{1,0:T(8,128)(2,1)S(1)}, bf16[256,256]{1,0:T(8,128)(2,1)}, u32[]{:S(2)}) copy-start(bf16[256,256]{1,0:T(8,128)(2,1)} %constant.71.clone.table_high) | copy-start | bytes 393220
  54.1 47.1 %copy-start.5 = (bf16[1024,256]{1,0:T(8,128)(2,1)S(1)}, bf16[1024,256]{1,0:T(8,128)(2,1)}, u32[]{:S(2)}) copy-start(bf16[1024,256]{1,0:T(8,128)(2,1)} %constant.73.clone.refs_8_) | copy-start | bytes 1572868
  54.1 47.1 %copy-start.6 = (f32[2,256,128]{2,1,0:T(8,128)S(1)}, f32[2,256,128]{2,1,0:T(8,128)}, u32[]{:S(2)}) copy-start(f32[2,256,128]{2,1,0:T(8,128)} %constant.74.clone.refs_9_) | copy-start | bytes 786436
  54.1 47.1 %all-to-all-start.1 = ((f32[512,2,128]{2,1,0:T(2,128)}), f32[512,2,128]{2,1,0:T(2,128)S(1)}, u32[]{:S(2)}, u32[]{:S(2)}) async-start(f32[512,2,128]{2,1,0:T(2,128)} %bitcast.5), calls=%async_computation.1 | async-start | bytes 1048576 | tf_op jit(solution)/shard_map/all_to_all | solution.py:388
  67.7 13.5 %collective-permute-start.3 = (f32[192,128]{1,0:T(8,128)S(1)}, f32[192,128]{1,0:T(8,128)S(1)}, u32[]{:S(2)}, u32[]{:S(2)}) collective-permute-start(f32[192,128]{1,0:T(8,128)S(1)} %get-tuple-element.23), channel_id=1, source_target_pairs={{0,256},{64,320},{128,384},{192,448},{256,0},{320,64},{384,128},{4... | collective-permute-start | bytes 294920 | tf_op jit(solution)/shard_map/ppermute | solution.py:394
  72.5 9.4 %collective-permute-start.4 = (f32[192,128]{1,0:T(8,128)S(1)}, f32[192,128]{1,0:T(8,128)S(1)}, u32[]{:S(2)}, u32[]{:S(2)}) collective-permute-start(f32[192,128]{1,0:T(8,128)S(1)} %get-tuple-element.24), channel_id=1, source_target_pairs={{0,320},{64,384},{128,448},{192,0},{256,64},{320,128},{384,192},{4... | collective-permute-start | bytes 294920 | tf_op jit(solution)/shard_map/ppermute | solution.py:394
  75.9 8.0 %collective-permute-start.5 = (f32[192,128]{1,0:T(8,128)S(1)}, f32[192,128]{1,0:T(8,128)S(1)}, u32[]{:S(2)}, u32[]{:S(2)}) collective-permute-start(f32[192,128]{1,0:T(8,128)S(1)} %get-tuple-element.25), channel_id=1, source_target_pairs={{0,384},{64,448},{128,0},{192,64},{256,128},{320,192},{384,256},{4... | collective-permute-start | bytes 294920 | tf_op jit(solution)/shard_map/ppermute | solution.py:394
  81.2 4.7 %collective-permute-start.6 = (f32[192,128]{1,0:T(8,128)S(1)}, f32[192,128]{1,0:T(8,128)S(1)}, u32[]{:S(2)}, u32[]{:S(2)}) collective-permute-start(f32[192,128]{1,0:T(8,128)S(1)} %get-tuple-element.26), channel_id=1, source_target_pairs={{0,448},{64,0},{128,64},{192,128},{256,192},{320,256},{384,320},{4... | collective-permute-start | bytes 294920 | tf_op jit(solution)/shard_map/ppermute | solution.py:394
  104.1 44.4 %all-to-all-start.2 = ((f32[512,2,128]{2,1,0:T(2,128)}), f32[512,2,128]{2,1,0:T(2,128)S(1)}, u32[]{:S(2)}, u32[]{:S(2)}) async-start(f32[512,2,128]{2,1,0:T(2,128)} %bitcast.7), calls=%async_computation.2 | async-start | bytes 1048576 | tf_op jit(solution)/shard_map/all_to_all | solution.py:388
  114.9 14.1 %collective-permute-start.7 = (f32[128,128]{1,0:T(8,128)S(1)}, f32[128,128]{1,0:T(8,128)S(1)}, u32[]{:S(2)}, u32[]{:S(2)}) collective-permute-start(f32[128,128]{1,0:T(8,128)S(1)} %get-tuple-element.29), channel_id=1, source_target_pairs={{0,64},{64,128},{128,192},{192,256},{256,320},{320,384},{384,448},... | collective-permute-start | bytes 196616 | tf_op jit(solution)/shard_map/ppermute | solution.py:394
  116.5 12.5 %collective-permute-start.8 = (f32[128,128]{1,0:T(8,128)S(1)}, f32[128,128]{1,0:T(8,128)S(1)}, u32[]{:S(2)}, u32[]{:S(2)}) collective-permute-start(f32[128,128]{1,0:T(8,128)S(1)} %get-tuple-element.30), channel_id=1, source_target_pairs={{0,128},{64,192},{128,256},{192,320},{256,384},{320,448},{384,0},{... | collective-permute-start | bytes 196616 | tf_op jit(solution)/shard_map/ppermute | solution.py:394
  119.6 9.7 %collective-permute-start.9 = (f32[128,128]{1,0:T(8,128)S(1)}, f32[128,128]{1,0:T(8,128)S(1)}, u32[]{:S(2)}, u32[]{:S(2)}) collective-permute-start(f32[128,128]{1,0:T(8,128)S(1)} %get-tuple-element.31), channel_id=1, source_target_pairs={{0,192},{64,256},{128,320},{192,384},{256,448},{320,0},{384,64},{4... | collective-permute-start | bytes 196616 | tf_op jit(solution)/shard_map/ppermute | solution.py:394
  123.4 8.1 %collective-permute-start.10 = (f32[128,128]{1,0:T(8,128)S(1)}, f32[128,128]{1,0:T(8,128)S(1)}, u32[]{:S(2)}, u32[]{:S(2)}) collective-permute-start(f32[128,128]{1,0:T(8,128)S(1)} %get-tuple-element.32), channel_id=1, source_target_pairs={{0,256},{64,320},{128,384},{192,448},{256,0},{320,64},{384,128},{4... | collective-permute-start | bytes 196616 | tf_op jit(solution)/shard_map/ppermute | solution.py:394
  150.4 37.2 %all-to-all-start.3 = ((f32[64,16,128]{2,1,0:T(8,128)}), f32[64,16,128]{2,1,0:T(8,128)S(1)}, u32[]{:S(2)}, u32[]{:S(2)}) async-start(f32[64,16,128]{2,1,0:T(8,128)} %bitcast.9), calls=%async_computation.3 | async-start | bytes 1048576 | tf_op jit(solution)/shard_map/all_to_all | solution.py:388
  157.1 7.2 %collective-permute-start.11 = (f32[128,128]{1,0:T(8,128)S(1)}, f32[128,128]{1,0:T(8,128)S(1)}, u32[]{:S(2)}, u32[]{:S(2)}) collective-permute-start(f32[128,128]{1,0:T(8,128)S(1)} %get-tuple-element.33), channel_id=1, source_target_pairs={{0,320},{64,384},{128,448},{192,0},{256,64},{320,128},{384,192},{4... | collective-permute-start | bytes 196616 | tf_op jit(solution)/shard_map/ppermute | solution.py:394
  160.6 5.7 %collective-permute-start.12 = (f32[128,128]{1,0:T(8,128)S(1)}, f32[128,128]{1,0:T(8,128)S(1)}, u32[]{:S(2)}, u32[]{:S(2)}) collective-permute-start(f32[128,128]{1,0:T(8,128)S(1)} %get-tuple-element.34), channel_id=1, source_target_pairs={{0,384},{64,448},{128,0},{192,64},{256,128},{320,192},{384,256},{4... | collective-permute-start | bytes 196616 | tf_op jit(solution)/shard_map/ppermute | solution.py:394
  163.0 24.6 %copy-start.1 = (f32[2,2,256,128]{3,2,1,0:T(8,128)S(1)}, f32[2,2,256,128]{3,2,1,0:T(8,128)}, u32[]{:S(2)}) copy-start(f32[2,2,256,128]{3,2,1,0:T(8,128)} %spectrum.3) | copy-start | bytes 1572868
  163.0 4.3 %collective-permute-start.13 = (f32[128,128]{1,0:T(8,128)S(1)}, f32[128,128]{1,0:T(8,128)S(1)}, u32[]{:S(2)}, u32[]{:S(2)}) collective-permute-start(f32[128,128]{1,0:T(8,128)S(1)} %get-tuple-element.35), channel_id=1, source_target_pairs={{0,448},{64,0},{128,64},{192,128},{256,192},{320,256},{384,320},{4... | collective-permute-start | bytes 196616 | tf_op jit(solution)/shard_map/ppermute | solution.py:394
  (6 other events, 20.7 us)
